TPU v7x, 32 devices: a whole 2x2x4 slice. The times are simulated.
32 devices in a mesh: dp: 4 (over y, x), expert: 4 (over z), tensor: 2 (over core).
Axes of the slice: x: 2, y: 2, z: 4, core: 2. Of those that a mesh axis runs over, the one named last changes fastest.
Arguments:
- tokens: bfloat16 [2048, 2048], P(('dp', 'expert')), may hold values from -6 to 6
- expert_ids: int32 [2048, 2], P(('dp', 'expert')), may hold values from 0 to 3, all different within a row; in each aligned block of 128 rows (0 to 127, 128 to 255, ...) at most 96 rows name the same one
- gate_values: float32 [2048, 2], P(('dp', 'expert')), may hold values from 0.1 to 1
- tag_labels: int32 [2048], P(('dp', 'expert')), may hold values from 0 to 31
- w_gate: bfloat16 [4, 2048, 7168], P('expert', 'dp', 'tensor'), may hold values from -0.125 to 0.125
- w_up: bfloat16 [4, 2048, 7168], P('expert', 'dp', 'tensor'), may hold values from -0.125 to 0.125
- w_down: bfloat16 [4, 7168, 2048], P('expert', 'tensor', 'dp'), may hold values from -0.0625 to 0.0625
- adapter_in: bfloat16 [4, 16, 2048], P('expert'), may hold values from -0.125 to 0.125
- adapter_out: bfloat16 [4, 16, 7168], P('expert', None, 'tensor'), may hold values from -1.5 to 1.5
- tag_weight: bfloat16 [2048, 32], replicated, may hold values from -0.125 to 0.125
Outputs:
- layer_out: bfloat16 [2048, 2048], P(('dp', 'expert'), 'tensor')
- in_gradient: float32 [4, 16, 2048], P('expert')
- out_gradient: float32 [4, 16, 7168], P('expert', None, 'tensor')
Inputs may be any that keep to these rules, and one draw needn't show every extreme that they name: `expert_ids`: each row names 2 different experts; the rows of one index of dp and expert name each expert at most 96 times, a bound that some block reaches.
All inputs are finite; a program needn't handle non-finite values.
Results may differ from a plain program's by a relative error of at most 0.017.
Values may be sent and summed in bfloat16 or wider, within the bound.
No kernel may reach another device: no remote copies, remote signals or barrier semaphores. Data moves between devices by JAX's collectives and lax.ppermute only.
A program may use at most 128 MiB of HBM per device.

v0:
```python
import jax
import jax.numpy as jnp
from jax import lax
from jax.sharding import PartitionSpec as P

adapter_scale = 2.0


def contract_last(left, right):
    return lax.dot_general(
        left, right, (((1,), (1,)), ((), ())), preferred_element_type=jnp.float32
    )


def contract_first(left, right):
    return lax.dot_general(
        left, right, (((0,), (0,)), ((), ())), preferred_element_type=jnp.float32
    )


def tag_gradient(logits, tag_labels):
    exp_logits = jnp.exp(logits)
    probability = exp_logits / jnp.sum(exp_logits, axis=1, keepdims=True)
    labels_hot = (
        tag_labels[:, None] == jnp.arange(logits.shape[1], dtype=jnp.int32)[None, :]
    ).astype(jnp.float32)
    return probability - labels_hot


def local(
    tokens,
    expert_ids,
    gate_values,
    tag_labels,
    w_gate,
    w_up,
    w_down,
    adapter_in,
    adapter_out,
    tag_weight,
):
    experts = lax.axis_size("expert")
    shards = lax.axis_size("tensor")
    tok_count = tokens.shape[0]
    model_width = tokens.shape[1]
    share_width = model_width // shards
    capacity = 3 * tok_count // experts
    slot_count = experts * capacity
    flat_ids = expert_ids.reshape(-1)
    onehot = (flat_ids[:, None] == jnp.arange(experts, dtype=jnp.int32)[None, :]).astype(jnp.int32)
    before = jnp.cumsum(onehot, axis=0) - onehot
    position = jnp.sum(before * onehot, axis=1)
    slot_index = (flat_ids * capacity + position).reshape(tok_count, expert_ids.shape[1])
    matches = jnp.arange(slot_count, dtype=jnp.int32)[:, None, None] == slot_index[None, :, :]
    dispatch = jnp.sum(matches.astype(jnp.float32), axis=2).astype(jnp.bfloat16)
    combine = jnp.sum(jnp.where(matches, gate_values[None, :, :], jnp.float32(0.0)), axis=2).T
    outgoing = jnp.dot(dispatch, tokens, preferred_element_type=jnp.float32).astype(jnp.bfloat16)
    arrived = lax.all_to_all(
        outgoing.reshape(experts, capacity, model_width),
        "expert",
        split_axis=0,
        concat_axis=0,
        tiled=True,
    ).reshape(slot_count, model_width)
    gate_acc = jnp.dot(
        arrived,
        lax.all_gather(w_gate, "dp", axis=1, tiled=True)[0],
        preferred_element_type=jnp.float32,
    )
    up_acc = jnp.dot(
        arrived,
        lax.all_gather(w_up, "dp", axis=1, tiled=True)[0],
        preferred_element_type=jnp.float32,
    )
    low_rank = contract_last(arrived, adapter_in[0]).astype(jnp.bfloat16)
    up_full = up_acc + adapter_scale * jnp.dot(
        low_rank, adapter_out[0], preferred_element_type=jnp.float32
    )
    activated = jax.nn.silu(gate_acc)
    hidden = (activated * up_full).astype(jnp.bfloat16)
    down_full = lax.all_gather(w_down, "dp", axis=2, tiled=True)[0]
    partial_value = jnp.dot(hidden, down_full, preferred_element_type=jnp.float32)
    column_start = lax.axis_index("tensor") * share_width
    summed = lax.psum(partial_value, "tensor").astype(jnp.bfloat16)
    returned = lax.all_to_all(
        summed.reshape(experts, capacity, model_width),
        "expert",
        split_axis=0,
        concat_axis=0,
        tiled=True,
    ).reshape(slot_count, model_width)
    mixed_rows = tokens.astype(jnp.float32) + jnp.dot(
        combine, returned.astype(jnp.float32), precision=lax.Precision.HIGHEST
    )
    layer_full = mixed_rows.astype(jnp.bfloat16)
    logits = jnp.dot(layer_full, tag_weight, preferred_element_type=jnp.float32)
    logit_grad = tag_gradient(logits, tag_labels)
    upstream = jnp.dot(
        logit_grad, tag_weight.astype(jnp.float32).T, precision=lax.Precision.HIGHEST
    )
    slot_out = jnp.dot(combine.T, upstream, precision=lax.Precision.HIGHEST).astype(jnp.bfloat16)
    slot_grad = lax.all_to_all(
        slot_out.reshape(experts, capacity, model_width),
        "expert",
        split_axis=0,
        concat_axis=0,
        tiled=True,
    ).reshape(slot_count, model_width)
    layer_out = lax.dynamic_slice_in_dim(layer_full, column_start, share_width, 1)
    hidden_grad = contract_last(slot_grad, down_full)
    up_grad = (hidden_grad * activated).astype(jnp.bfloat16)
    out_local = adapter_scale * contract_first(low_rank, up_grad)
    low_grad = adapter_scale * contract_last(up_grad, adapter_out[0])
    in_local = lax.dot_general(
        low_grad,
        arrived.astype(jnp.float32),
        (((0,), (0,)), ((), ())),
        precision=lax.Precision.HIGHEST,
    )
    in_total = lax.psum(in_local.astype(jnp.bfloat16), ("dp", "tensor")).astype(jnp.float32)
    out_total = lax.psum(out_local.astype(jnp.bfloat16), "dp").astype(jnp.float32)
    return (layer_out, in_total[None], out_total[None])


def solution(mesh):
    in_specs = (
        P(("dp", "expert"), None),
        P(("dp", "expert"), None),
        P(("dp", "expert"), None),
        P(("dp", "expert")),
        P("expert", "dp", "tensor"),
        P("expert", "dp", "tensor"),
        P("expert", "tensor", "dp"),
        P("expert", None, None),
        P("expert", None, "tensor"),
        P(),
    )
    out_specs = (
        P(("dp", "expert"), "tensor"),
        P("expert", None, None),
        P("expert", None, "tensor"),
    )
    return jax.shard_map(local, mesh=mesh, in_specs=in_specs, out_specs=out_specs, check_vma=False)
```

profile of v0, /device:TPU:0, one launch (start us, length us, event | category | flops | bytes accessed | tf_op | source)
XLA Modules:
  0.0 668.6 jit_solution(2607973388467530566)
XLA Ops:
  8.0 0.7 all-gather.4.cloned.1.call-update
  9.9 1.2 reduce-window.6
  12.4 43.1 %all_to_all.15 = bf16[4,96,2048]{2,1,0:T(8,128)(2,1)S(1)} all-to-all(bf16[4,96,2048]{2,1,0:T(8,128)(2,1)S(1)} %bitcast.78), channel_id=1, replica_groups=mesh['dp'=4,'expert'=4,'tensor'=2] {'expert'}, dimensions={0} | all-to-all | bytes 3145728 | tf_op jit(solution)/shard_map/all_to_all | solution.py:58
  56.0 96.6 %all-gather.6.cloned.1.call-done = bf16[1,2048,3584]{2,1,0:T(8,128)(2,1)} async-done(((bf16[1,512,3584]{2,1,0:T(8,128)(2,1)}), bf16[1,2048,3584]{2,1,0:T(8,128)(2,1)}) %all-gather.6.cloned.1.call-update) | async-done | bytes 14680080 | tf_op jit(solution)/shard_map/all_gather | solution.py:72
  152.6 12.2 %fusion.4 = f32[384,3584]{1,0:T(8,128)} fusion(bf16[384,2048]{1,0:T(8,128)(2,1)S(1)} %bitcast.75, bf16[1,2048,3584]{2,1,0:T(8,128)(2,1)} %all-gather.6.cloned.1.call-done), kind=kOutput, calls=%fused_computation.4 | convolution fusion | flops 5637144576 | bytes 21757952 | tf_op jit(solution)/shard_map/dot_general | solution.py:70
  164.8 129.6 %all-gather.4.cloned.1.call-done = bf16[1,2048,3584]{2,1,0:T(8,128)(2,1)} async-done(((bf16[1,512,3584]{2,1,0:T(8,128)(2,1)}), bf16[1,2048,3584]{2,1,0:T(8,128)(2,1)}) %all-gather.4.cloned.1.call-update) | async-done | bytes 14680080 | tf_op jit(solution)/shard_map/all_gather | solution.py:67
  294.4 11.2 %divide_multiply_fusion = f32[384,3584]{1,0:T(8,128)} fusion(bf16[384,2048]{1,0:T(8,128)(2,1)S(1)} %bitcast.76, bf16[1,2048,3584]{2,1,0:T(8,128)(2,1)} %all-gather.4.cloned.1.call-done), kind=kOutput, calls=%fused_computation.14 | convolution fusion | flops 5642649600 | bytes 21757952 | tf_op jit(solution)/shard_map/dot_general | solution.py:65
  305.6 130.5 %all-gather.8.cloned.1.call-done = bf16[1,3584,2048]{2,1,0:T(8,128)(2,1)} async-done(((bf16[1,3584,512]{2,1,0:T(8,128)(2,1)}), bf16[1,3584,2048]{2,1,0:T(8,128)(2,1)}) %all-gather.8.cloned.1.call-update) | async-done | bytes 14680080 | tf_op jit(solution)/shard_map/all_gather | solution.py:81
  436.1 15.1 %fusion.2 = f32[384,2048]{1,0:T(8,128)} fusion(bf16[1,3584,2048]{2,1,0:T(8,128)(2,1)} %all-gather.8.cloned.1.call-done, f32[384,3584]{1,0:T(8,128)} %divide_multiply_fusion, f32[384,3584]{1,0:T(8,128)} %fusion.4, bf16[384,16]{0,1:T(8,128)(2,1)S(1)} %convolution_convert_fusion.3, bf16[1,16,3584]{2,1,0:T(8,128)(2,1)S(1)} %copy-done.4), kind=kOutput, calls=%fused_computation.2 | convolution fusion | flops 5686689792 | bytes 28962816 | tf_op jit(solution)/shard_map/dot_general | solution.py:82
  451.2 12.2 %all-reduce.7 = bf16[384,2048]{1,0:T(8,128)(2,1)S(1)} all-reduce(f32[384,2048]{1,0:T(8,128)} %fusion.2), channel_id=1, replica_groups=mesh['dp'=4,'expert'=4,'tensor'=2] {'tensor'}, use_global_device_ids=true, to_apply=%region_5.6 | all-reduce | flops 786432 | bytes 4718592 | tf_op jit(solution)/shard_map/psum | solution.py:84
  463.5 41.9 %all_to_all.16 = bf16[4,96,2048]{2,1,0:T(8,128)(2,1)S(1)} all-to-all(bf16[4,96,2048]{2,1,0:T(8,128)(2,1)S(1)} %bitcast.80), channel_id=1, replica_groups=mesh['dp'=4,'expert'=4,'tensor'=2] {'expert'}, dimensions={0} | all-to-all | bytes 3145728 | tf_op jit(solution)/shard_map/all_to_all | solution.py:85
  505.4 1.0 fusion.21
  507.4 3.7 convolution_convert_fusion
  511.1 4.4 all-to-all-start.2
  515.5 36.6 %all-to-all-done.2 = bf16[4,96,2048]{2,1,0:T(8,128)(2,1)} async-done(((bf16[4,96,2048]{2,1,0:T(8,128)(2,1)}), bf16[4,96,2048]{2,1,0:T(8,128)(2,1)}, u32[]{:S(2)}, u32[]{:S(2)}) %all-to-all-start.2) | async-done | bytes 1572896 | tf_op jit(solution)/shard_map/all_to_all | solution.py:102
  552.2 10.4 %fusion.13 = bf16[384,3584]{1,0:T(8,128)(2,1)S(1)} fusion(f32[384,3584]{1,0:T(8,128)} %divide_multiply_fusion, bf16[384,2048]{1,0:T(8,128)(2,1)} %bitcast.12, bf16[1,3584,2048]{2,1,0:T(8,128)(2,1)} %all-gather.8.cloned.1.call-done), kind=kOutput, calls=%fused_computation.12 | convolution fusion | flops 5639897088 | bytes 24510464 | tf_op jit(solution)/shard_map/dot_general | solution.py:10
  562.6 0.8 convolution_multiply_fusion.2
  564.0 1.4 fusion.22
  565.5 1.1 fusion.20
  566.6 0.7 constant_dynamic-slice_fusion
  567.3 48.8 %all-reduce.4.cloned.1.call-done = bf16[1,16,2048]{2,1,0:T(8,128)(2,1)} async-done(((bf16[1,16,2048]{2,1,0:T(8,128)(2,1)}), bf16[1,16,2048]{2,1,0:T(8,128)(2,1)}) %all-reduce.4.cloned.1.call-update) | async-done | bytes 65552 | tf_op jit(solution)/shard_map/psum | solution.py:120
  616.2 1.5 broadcast_in_dim.33
  617.7 42.8 %all-reduce.6.cloned.1.call-done = bf16[1,16,3584]{2,1,0:T(8,128)(2,1)} async-done(((bf16[1,16,3584]{2,1,0:T(8,128)(2,1)}), bf16[1,16,3584]{2,1,0:T(8,128)(2,1)}) %all-reduce.6.cloned.1.call-update) | async-done | bytes 114704 | tf_op jit(solution)/shard_map/psum | solution.py:121
  660.5 1.6 broadcast_in_dim.35
  (46 shorter events, 5.3 us)
Async XLA Ops:
  7.2 499.3 %copy-start = (bf16[2048,32]{0,1:T(8,128)(2,1)S(1)}, bf16[2048,32]{0,1:T(8,128)(2,1)}, u32[]{:S(2)}) copy-start(bf16[2048,32]{0,1:T(8,128)(2,1)} %param.19) | copy-start | bytes 393220
  7.2 145.4 %all-gather.6.cloned.1.call-start = ((), (), s32[]{:S(2)}) async-start(), calls=%async_computation.4 | async-start | bytes 18350080 | tf_op jit(solution)/shard_map/all_gather | solution.py:72
  7.9 1.5 copy-start.6
  7.9 3.8 copy-start.7
  7.9 3.9 copy-start.3
  7.9 286.5 %all-gather.4.cloned.1.call-start = ((), (), s32[]{:S(2)}) async-start(), calls=%async_computation.3 | async-start | bytes 18350080 | tf_op jit(solution)/shard_map/all_gather | solution.py:67
  8.7 427.4 %all-gather.8.cloned.1.call-start = ((), (), s32[]{:S(2)}) async-start(), calls=%async_computation.5 | async-start | bytes 18350080 | tf_op jit(solution)/shard_map/all_gather | solution.py:81
  9.4 46.0 %copy-start.5 = (bf16[1,16,2048]{2,1,0:T(8,128)(2,1)S(1)}, bf16[1,16,2048]{2,1,0:T(8,128)(2,1)}, u32[]{:S(2)}) copy-start(bf16[1,16,2048]{2,1,0:T(8,128)(2,1)} %param.17) | copy-start | bytes 196612
  55.5 238.9 %copy-start.1 = (bf16[4,96,2048]{2,1,0:T(8,128)(2,1)}, bf16[4,96,2048]{2,1,0:T(8,128)(2,1)S(1)}, u32[]{:S(2)}) copy-start(bf16[4,96,2048]{2,1,0:T(8,128)(2,1)S(1)} %all_to_all.15) | copy-start | bytes 4718596
  164.8 271.3 %copy-start.4 = (bf16[1,16,3584]{2,1,0:T(8,128)(2,1)S(1)}, bf16[1,16,3584]{2,1,0:T(8,128)(2,1)}, u32[]{:S(2)}) copy-start(bf16[1,16,3584]{2,1,0:T(8,128)(2,1)} %param.18) | copy-start | bytes 344068
  463.5 43.3 %copy-start.8 = (s32[128]{0:T(128)S(1)}, s32[128]{0:T(128)}, u32[]{:S(2)}) copy-start(s32[128]{0:T(128)} %param.13) | copy-start | bytes 1540
  511.1 41.1 %all-to-all-start.2 = ((bf16[4,96,2048]{2,1,0:T(8,128)(2,1)}), bf16[4,96,2048]{2,1,0:T(8,128)(2,1)}, u32[]{:S(2)}, u32[]{:S(2)}) async-start(bf16[4,96,2048]{2,1,0:T(8,128)(2,1)} %bitcast.11), calls=%async_computation.2 | async-start | bytes 3145728 | tf_op jit(solution)/shard_map/all_to_all | solution.py:102
  515.5 100.7 %all-reduce.4.cloned.1.call-start = ((), (), s32[]{:S(2)}) async-start(), calls=%async_computation.6 | async-start | bytes 131072 | tf_op jit(solution)/shard_map/psum | solution.py:120
  562.6 1.4 copy-start.2
  565.4 95.1 %all-reduce.6.cloned.1.call-start = ((), (), s32[]{:S(2)}) async-start(), calls=%async_computation.7 | async-start | bytes 229376 | tf_op jit(solution)/shard_map/psum | solution.py:121
Sparse Core Ops, SparseCore 0:
  9.9 142.6 all-gather.5
  154.4 139.9 all-gather.3
  296.2 139.8 all-gather.7
  565.5 50.5 all-reduce.3
  619.7 40.6 all-reduce.5
where the time goes:
time: 669 us
  waiting for transfers between devices  487 us (73%)
  blocking collectives  97.2 us (15%)
  matrix products  59 us (9%)
  between operations  14 us (2%)
    all_gather x1, waiting for transfers between devices, local(): down_full = lax.all_gather(w_down, 'dp', axis=2, tiled=True)[0]  130 us
    all_gather x1, waiting for transfers between devices, local(): lax.all_gather(w_gate, 'dp', axis=1, tiled=True)[0]  130 us
    all_gather x1, waiting for transfers between devices, local(): lax.all_gather(w_up, 'dp', axis=1, tiled=True)[0]  96.6 us
    psum x1, waiting for transfers between devices, local(): lax.psum(in_local.astype(jnp.bfloat16), ('dp', 'tensor'))  48.8 us
    all_to_all x1, blocking collectives, local(): lax.all_to_all(outgoing.reshape(experts, capacity, model_width), 'expert'...  43.1 us
    psum x1, waiting for transfers between devices, local(): lax.psum(out_local.astype(jnp.bfloat16), 'dp').astype(jnp.float32)  42.8 us
    all_to_all x1, blocking collectives, local(): lax.all_to_all(summed.reshape(experts, capacity, model_width), 'expert',...  41.9 us
    all_to_all x1, waiting for transfers between devices, local(): lax.all_to_all(slot_out.reshape(experts, capacity, model_width), 'expert'...  36.6 us
  transfers between devices with their start and end apart: 6, of which 6 were waited for; matrix products, arithmetic and copies ran while one was open for 5% of the time, Pallas kernels for 0%

commit v1 on v0

v1 whole, which is shorter than its diff:
```python
import jax
import jax.numpy as jnp
from jax import lax
from jax.sharding import PartitionSpec as P

adapter_scale = 2.0
f32 = jnp.float32
bf16 = jnp.bfloat16
highest = lax.Precision.HIGHEST


def partner(index, step, count):
    if count & (count - 1) == 0:
        return index ^ step, index ^ step
    return (index + step) % count, (index - step) % count


def send(value, axis, step):
    count = lax.axis_size(axis)
    return lax.ppermute(value, axis, [(i, partner(i, step, count)[0]) for i in range(count)])


def exchange(pieces, axis):
    count, me = lax.axis_size(axis), lax.axis_index(axis)
    own = lax.dynamic_slice_in_dim(pieces, me, 1, 0)
    result = lax.dynamic_update_slice_in_dim(jnp.zeros_like(pieces), own, me, 0)
    for step in range(1, count):
        target, source = partner(me, step, count)
        came = send(lax.dynamic_slice_in_dim(pieces, target, 1, 0), axis, step)
        result = lax.dynamic_update_slice_in_dim(result, came, source, 0)
    return result


def exchange_sum(pieces, axis):
    count, me = lax.axis_size(axis), lax.axis_index(axis)
    total = lax.dynamic_index_in_dim(pieces, me, 0, keepdims=False).astype(f32)
    for step in range(1, count):
        target, _ = partner(me, step, count)
        total = total + send(lax.dynamic_index_in_dim(pieces, target, 0, keepdims=False), axis, step).astype(f32)
    return total


def gather(value, axis):
    count, me = lax.axis_size(axis), lax.axis_index(axis)
    result = jnp.zeros((count,) + value.shape, value.dtype)
    result = lax.dynamic_update_slice_in_dim(result, value[None], me, 0)
    for step in range(1, count):
        _, source = partner(me, step, count)
        result = lax.dynamic_update_slice_in_dim(result, send(value, axis, step)[None], source, 0)
    return result


def gather_sum(value, axis):
    total = value.astype(f32)
    for step in range(1, lax.axis_size(axis)):
        total = total + send(value, axis, step).astype(f32)
    return total


def dot(left, right, left_dim, right_dim, **options):
    return lax.dot_general(
        left, right, (((left_dim,), (right_dim,)), ((), ())), preferred_element_type=f32, **options
    )


def local(
    tokens,
    expert_ids,
    gate_values,
    tag_labels,
    w_gate,
    w_up,
    w_down,
    adapter_in,
    adapter_out,
    tag_weight,
):
    experts = lax.axis_size("expert")
    shards = lax.axis_size("tensor")
    groups = lax.axis_size("dp")
    dp, tensor = lax.axis_index("dp"), lax.axis_index("tensor")
    tok_count, model_width = tokens.shape
    share_width = model_width // shards
    capacity = 3 * tok_count // experts
    feature_part = w_gate.shape[1]
    hidden_part = w_gate.shape[2] // groups
    tags = tag_weight.shape[1]
    rank = adapter_in.shape[1]
    slots = experts * groups * capacity

    member = expert_ids[None, :, :] == jnp.arange(experts, dtype=jnp.int32)[:, None, None]
    used = jnp.any(member, axis=2).astype(f32)
    weight = jnp.sum(jnp.where(member, gate_values[None], f32(0.0)), axis=2)
    upto = (jnp.arange(tok_count)[:, None] <= jnp.arange(tok_count)[None, :]).astype(f32)
    code = used * dot(used, upto, 1, 0)
    places = jnp.arange(1, capacity + 1, dtype=f32)
    own_match = code[:, None, :] == places[None, :, None]
    combine = jnp.where(own_match, weight[:, None, :], f32(0.0)).reshape(experts * capacity, tok_count)

    token_half = lax.dynamic_slice_in_dim(tokens, tensor * share_width, share_width, 1)
    code_rows = jnp.pad(code.astype(bf16), ((0, 16 - experts), (0, share_width - tok_count)))
    plane = gather(jnp.concatenate([token_half, code_rows], axis=0), "dp")
    plane_code = plane[:, tok_count : tok_count + experts, :tok_count].astype(f32)
    match = (plane_code[:, :, None, :] == places[None, None, :, None]).astype(bf16)
    outgoing = jnp.einsum(
        "gest,gtd->egsd", match, plane[:, :tok_count], preferred_element_type=f32
    ).astype(bf16)
    x_half = exchange(outgoing, "expert").reshape(slots, share_width)
    x_other = send(x_half, "tensor", 1)
    x = jnp.zeros((slots, model_width), bf16)
    x = lax.dynamic_update_slice_in_dim(x, x_half, tensor * share_width, 1)
    x = lax.dynamic_update_slice_in_dim(x, x_other, (1 - tensor) * share_width, 1)

    tag_part = lax.dynamic_slice_in_dim(tag_weight, dp * feature_part, feature_part, 0)
    tag_down = dot(tag_part, w_down[0], 0, 1).astype(bf16)
    tag_down = exchange_sum(tag_down.reshape(tags, groups, hidden_part).transpose(1, 0, 2), "dp").astype(bf16)

    gate_up = jnp.stack(
        [w_gate[0].reshape(feature_part, groups, hidden_part), w_up[0].reshape(feature_part, groups, hidden_part)], axis=2
    )
    gate_up = gate_up.reshape(feature_part, groups, 2 * hidden_part).transpose(1, 0, 2)
    gate_up = exchange(gate_up, "dp").reshape(model_width, 2 * hidden_part)
    down = exchange(w_down[0].reshape(groups, hidden_part, feature_part), "dp")
    adapter_part = lax.dynamic_slice_in_dim(adapter_out[0], dp * hidden_part, hidden_part, 1)

    product = dot(x, gate_up, 1, 0)
    low_rank = dot(x, adapter_in[0], 1, 1).astype(bf16)
    activated = jax.nn.silu(product[:, :hidden_part])
    hidden = (
        activated * (product[:, hidden_part:] + adapter_scale * dot(low_rank, adapter_part, 1, 0))
    ).astype(bf16)
    activated = activated.astype(bf16)

    slot_logits = dot(tag_down, hidden, 1, 1)
    slot_logits = slot_logits + send(slot_logits.astype(bf16), "tensor", 1).astype(f32)
    slot_logits = slot_logits.reshape(tags, experts, groups, capacity).transpose(2, 1, 0, 3).astype(bf16)
    slot_logits = exchange_sum(slot_logits, "dp").astype(bf16)
    slot_logits = exchange(slot_logits, "expert").transpose(1, 0, 2).reshape(tags, experts * capacity)
    logits = dot(tag_weight, tokens, 0, 1) + dot(slot_logits.astype(f32), combine, 1, 0, precision=highest)
    exp_logits = jnp.exp(logits)
    probability = exp_logits / jnp.sum(exp_logits, axis=0, keepdims=True)
    labels_hot = (tag_labels[None, :] == jnp.arange(tags, dtype=jnp.int32)[:, None]).astype(f32)
    logit_grad = probability - labels_hot
    slot_grad = dot(logit_grad, combine, 1, 1, precision=highest).astype(bf16)
    slot_grad = exchange(slot_grad.reshape(tags, experts, capacity).transpose(1, 0, 2), "expert")
    slot_grad = gather(slot_grad, "dp").transpose(2, 1, 0, 3).reshape(tags, slots)

    up_grad = (dot(slot_grad, tag_down, 0, 0) * activated.astype(f32)).astype(bf16)
    out_local = adapter_scale * dot(low_rank, up_grad, 0, 0)
    low_grad = (adapter_scale * dot(up_grad, adapter_part, 1, 1)).astype(bf16)
    in_local = dot(low_grad, x, 0, 0)
    in_local = in_local + send(in_local.astype(bf16), "tensor", 1).astype(f32)
    in_total = gather_sum(in_local.astype(bf16), "dp")
    out_total = gather(out_local, "dp").transpose(1, 0, 2).reshape(rank, groups * hidden_part)

    half = groups // shards
    down_own = lax.dynamic_slice_in_dim(down, tensor * half, half, 0)
    down_other = lax.dynamic_slice_in_dim(down, (1 - tensor) * half, half, 0)
    other = dot(hidden, down_other, 1, 1).astype(bf16)
    own = dot(hidden, down_own, 1, 1) + send(other, "tensor", 1).astype(f32)
    own = own.reshape(experts, groups, capacity, share_width).transpose(1, 0, 2, 3).astype(bf16)
    returned = exchange_sum(own, "dp").astype(bf16)
    returned = exchange(returned, "expert").reshape(experts * capacity, share_width)
    layer_out = token_half.astype(f32) + dot(combine, returned.astype(f32), 0, 0, precision=highest)
    return (layer_out.astype(bf16), in_total[None], out_total[None])


def solution(mesh):
    in_specs = (
        P(("dp", "expert"), None),
        P(("dp", "expert"), None),
        P(("dp", "expert"), None),
        P(("dp", "expert")),
        P("expert", "dp", "tensor"),
        P("expert", "dp", "tensor"),
        P("expert", "tensor", "dp"),
        P("expert", None, None),
        P("expert", None, "tensor"),
        P(),
    )
    out_specs = (
        P(("dp", "expert"), "tensor"),
        P("expert", None, None),
        P("expert", None, "tensor"),
    )
    return jax.shard_map(local, mesh=mesh, in_specs=in_specs, out_specs=out_specs, check_vma=False)
```

time: 669 us -> 407 us (0.61)
  waiting for transfers between devices: 487 us -> 180 us
  blocking collectives: 97.2 us -> 0 us
  local copies, waits for them, and re-layouts: 2.21 us -> 97.8 us
  starting transfers between devices: 4.56 us -> 61.1 us
  between operations: 14 us -> 1.87 us
  matrix products: 59 us -> 48.1 us
  other arithmetic: 4.58 us -> 11.7 us
    all_gather x3 -> x0, waiting for transfers between devices: 357 us -> none  [the longest x1 130 us: local(): down_full = lax.all_gather(w_down, 'dp', axis=2, tiled=True)[0]]
    ppermute x0 -> x43, waiting for transfers between devices: none -> 180 us  [send(): lax.ppermute(value, axis, [(i, partner(i, step, count)[0]) for i in range...]
    psum x2 -> x0, waiting for transfers between devices: 91.6 us -> none  [the longest x1 48.8 us: local(): lax.psum(in_local.astype(jnp.bfloat16), ('dp', 'tensor'))]
    all_to_all x2 -> x0, blocking collectives: 85 us -> none  [the longest x1 43.1 us: local(): lax.all_to_all(outgoing.reshape(experts, capacity, model_width), 'expert'...]
    ppermute x0 -> x43, starting transfers between devices: none -> 61.1 us  [send(): lax.ppermute(value, axis, [(i, partner(i, step, count)[0]) for i in range...]
    all_to_all x1 -> x0, waiting for transfers between devices: 36.6 us -> none  [local(): lax.all_to_all(slot_out.reshape(experts, capacity, model_width), 'expert'...]
    dynamic_update_slice x0 -> x34, local copies, waits for them, and re-layouts: none -> 27.3 us  [the longest x18 12.3 us: exchange(): result = lax.dynamic_update_slice_in_dim(result, came, source, 0)]
    convert_element_type x0 -> x3, local copies, waits for them, and re-layouts: none -> 20.7 us  [the longest x2 20.6 us: local(): own.reshape(experts, groups, capacity, share_width).transpose(1, 0, 2, 3)]
  transfers between devices with their start and end apart: 6 -> 43, of which waited for: 6 -> 20; matrix products, arithmetic and copies ran while one was open for 5% -> 37% of each run, Pallas kernels for 0% -> 0%
where the time goes in v1:
time: 407 us; the launch traced here: 400 us
  waiting for transfers between devices  180 us (44%)
  local copies, waits for them, and re-layouts  97.8 us (24%)
  starting transfers between devices  61.1 us (15%)
  matrix products  48.1 us (12%)
  other arithmetic  11.7 us (3%)
    ppermute x43, waiting for transfers between devices, send(): lax.ppermute(value, axis, [(i, partner(i, step, count)[0]) for i in range...  180 us
    ppermute x43, starting transfers between devices, send(): lax.ppermute(value, axis, [(i, partner(i, step, count)[0]) for i in range...  61.1 us
    dot_general x15, matrix products, dot(): lax.dot_general(left, right, (((left_dim,), (right_dim,)), ((), ())), pre...  47.1 us
    convert_element_type x2, local copies, waits for them, and re-layouts, local(): own.reshape(experts, groups, capacity, share_width).transpose(1, 0, 2, 3)  20.6 us
    unnamed x59, local copies, waits for them, and re-layouts  18.1 us
    another operation x9, local copies, waits for them, and re-layouts  16.9 us
    dynamic_update_slice x18, local copies, waits for them, and re-layouts, exchange(): result = lax.dynamic_update_slice_in_dim(result, came, source, 0)  12.3 us
  transfers between devices with their start and end apart: 43, of which 20 were waited for; matrix products, arithmetic and copies ran while one was open for 37% of the time, Pallas kernels for 0%

profile of v1, /device:TPU:0, one launch (start us, length us, event | category | flops | bytes accessed | tf_op | source)
XLA Modules:
  0.0 400.2 jit_solution(11877553363184620614)
XLA Ops:
  6.5 6.1 %collective-permute-done = bf16[144,1024]{1,0:T(8,128)(2,1)S(1)} collective-permute-done((bf16[144,1024]{1,0:T(8,128)(2,1)S(1)}, bf16[144,1024]{1,0:T(8,128)(2,1)S(1)}, u32[]{:S(2)}, u32[]{:S(2)}) %collective-permute-start) | collective-permute-done | bytes 294944 | tf_op jit(solution)/shard_map/ppermute | solution.py:20
  12.6 6.9 %collective-permute-done.1 = bf16[144,1024]{1,0:T(8,128)(2,1)S(1)} collective-permute-done((bf16[144,1024]{1,0:T(8,128)(2,1)S(1)}, bf16[144,1024]{1,0:T(8,128)(2,1)S(1)}, u32[]{:S(2)}, u32[]{:S(2)}) %collective-permute-start.1) | collective-permute-done | bytes 294944 | tf_op jit(solution)/shard_map/ppermute | solution.py:20
  25.3 5.9 %copy.114 = bf16[1,512,3584]{1,2,0:T(8,128)(2,1)} copy(bf16[1,512,3584]{2,1,0:T(8,128)(2,1)} %param.14) | data formatting | bytes 7340032 | tf_op args[4]
  31.3 5.9 %copy.115 = bf16[1,512,3584]{1,2,0:T(8,128)(2,1)} copy(bf16[1,512,3584]{2,1,0:T(8,128)(2,1)} %param.15) | data formatting | bytes 7340032 | tf_op args[5]
  40.0 6.7 %pad_maximum_fusion = bf16[512,4,2,896]{0,3,2,1:T(8,128)(2,1)} fusion(bf16[512,4,1,896]{0,3,2,1:T(8,128)(2,1)} %bitcast.177, bf16[512,4,1,896]{0,3,2,1:T(8,128)(2,1)} %bitcast.176), kind=kLoop, calls=%fused_computation | loop fusion | flops 3670016 | bytes 14680064 | tf_op jit(solution)/shard_map/stack | solution.py:118
  52.6 39.8 %collective-permute-done.4 = bf16[1,4,96,1024]{3,2,0,1:T(8,128)(2,1)S(1)} collective-permute-done((bf16[1,4,96,1024]{3,2,0,1:T(8,128)(2,1)}, bf16[1,4,96,1024]{3,2,0,1:T(8,128)(2,1)S(1)}, u32[]{:S(2)}, u32[]{:S(2)}) %collective-permute-start.4) | collective-permute-done | bytes 786464 | tf_op jit(solution)/shard_map/ppermute | solution.py:20
  96.9 3.9 copy.117
  117.9 26.7 %collective-permute-done.20 = bf16[32,896]{1,0:T(8,128)(2,1)S(1)} collective-permute-done((bf16[32,896]{1,0:T(8,128)(2,1)S(1)}, bf16[32,896]{1,0:T(8,128)(2,1)S(1)}, u32[]{:S(2)}, u32[]{:S(2)}) %collective-permute-start.20) | collective-permute-done | bytes 57376 | tf_op jit(solution)/shard_map/ppermute | solution.py:20
  146.1 4.5 %collective-permute-done.21 = bf16[32,896]{1,0:T(8,128)(2,1)S(1)} collective-permute-done((bf16[32,896]{1,0:T(8,128)(2,1)S(1)}, bf16[32,896]{1,0:T(8,128)(2,1)S(1)}, u32[]{:S(2)}, u32[]{:S(2)}) %collective-permute-start.21) | collective-permute-done | bytes 57376 | tf_op jit(solution)/shard_map/ppermute | solution.py:20
  163.0 11.7 %collective-permute-done.10 = bf16[1,896,512]{2,1,0:T(8,128)(2,1)S(1)} collective-permute-done((bf16[1,896,512]{2,1,0:T(8,128)(2,1)}, bf16[1,896,512]{2,1,0:T(8,128)(2,1)S(1)}, u32[]{:S(2)}, u32[]{:S(2)}) %collective-permute-start.10) | collective-permute-done | bytes 917536 | tf_op jit(solution)/shard_map/ppermute | solution.py:20
  184.6 29.9 %collective-permute-done.9 = bf16[1,512,1792]{2,1,0:T(8,128)(2,1)} collective-permute-done((bf16[1,512,1792]{2,1,0:T(8,128)(2,1)}, bf16[1,512,1792]{2,1,0:T(8,128)(2,1)}, u32[]{:S(2)}, u32[]{:S(2)}) %collective-permute-start.9) | collective-permute-done | bytes 1835040 | tf_op jit(solution)/shard_map/ppermute | solution.py:20
  218.5 12.1 %fusion.70 = f32[1536,1792]{1,0:T(8,128)S(1)} fusion(bf16[1536,2048]{1,0:T(8,128)(2,1)S(1)} %constant_dynamic-update-slice_fusion.17, bf16[2048,1792]{1,0:T(8,128)(2,1)S(1)} %bitcast.179), kind=kOutput, calls=%fused_computation.173 | convolution fusion | flops 11274289152 | bytes 24641536 | tf_op jit(solution)/shard_map/dot_general | solution.py:61
  238.6 12.8 %collective-permute-done.11 = bf16[1,896,512]{2,1,0:T(8,128)(2,1)S(1)} collective-permute-done((bf16[1,896,512]{2,1,0:T(8,128)(2,1)S(1)}, bf16[1,896,512]{2,1,0:T(8,128)(2,1)S(1)}, u32[]{:S(2)}, u32[]{:S(2)}) %collective-permute-start.11) | collective-permute-done | bytes 917536 | tf_op jit(solution)/shard_map/ppermute | solution.py:20
  259.5 14.3 %collective-permute-start.27 = (bf16[1,32,96]{2,1,0:T(8,128)(2,1)S(1)}, bf16[1,32,96]{2,1,0:T(8,128)(2,1)S(1)}, u32[]{:S(2)}, u32[]{:S(2)}) collective-permute-start(bf16[1,32,96]{2,1,0:T(8,128)(2,1)S(1)} %get-tuple-element.35), channel_id=1, source_target_pairs={{0,2},{2,0},{4,6},{6,4},{1,3},{3,1},{5,7},{7,5},{8,10},{10,8},{12,... | collective-permute-start | bytes 18440 | tf_op jit(solution)/shard_map/ppermute | solution.py:20
  273.8 6.2 %convolution_convert_fusion.1 = bf16[1536,2,512]{2,0,1:T(8,128)(2,1)} fusion(bf16[1536,896]{1,0:T(8,128)(2,1)S(1)} %fusion.1, bf16[4,896,512]{2,1,0:T(8,128)(2,1)} %constant_dynamic-update-slice_fusion.11, s32[]{:T(128)S(6)} %select_n.67), kind=kOutput, calls=%fused_computation.8 | convolution fusion | flops 2820145152 | bytes 7733252 | tf_op jit(solution)/shard_map/dot_general | solution.py:61
  307.2 4.1 %multiply_convert_fusion = bf16[1536,896]{1,0:T(8,128)(2,1)S(1)} fusion(bf16[32,1536]{1,0:T(8,128)(2,1)S(1)} %reshape.86, bf16[32,896]{1,0:T(8,128)(2,1)S(1)} %copy-done.11, f32[1536,1792]{1,0:T(8,128)} %copy-done.23), kind=kOutput, calls=%fused_computation.5 | convolution fusion | flops 99090432 | bytes 8413184 | tf_op jit(solution)/shard_map/dot_general | solution.py:61
  316.0 5.1 %fusion.67 = (bf16[16,2048]{1,0:T(8,128)(2,1)S(1)}, f32[16,2048]{1,0:T(8,128)}) fusion(bf16[1536,2048]{1,0:T(8,128)(2,1)} %copy-done.2, bf16[1536,896]{1,0:T(8,128)(2,1)S(1)} %multiply_convert_fusion, bf16[1,16,3584]{2,1,0:T(8,128)(2,1)} %param.18, s32[]{:T(128)S(6)} %select_n.65), kind=kOutput, calls=%fused_computation.172 | convolution fusion | flops 144785408 | bytes 9269252 | tf_op jit(solution)/shard_map/dot_general | solution.py:61
  321.1 6.7 %add_convert_fusion = bf16[1536,2,512]{2,0,1:T(8,128)(2,1)S(1)} fusion(bf16[1536,2,512]{2,0,1:T(8,128)(2,1)} %collective-permute-done.13, bf16[1536,896]{1,0:T(8,128)(2,1)} %copy-done.6, bf16[4,896,512]{2,1,0:T(8,128)(2,1)} %constant_dynamic-update-slice_fusion.11, s32[]{:T(128)S(6)} %select_n.66), kind=kOutput, calls=%fused_computation.1 | convolution fusion | flops 2823290880 | bytes 10878980 | tf_op jit(solution)/shard_map/dot_general | solution.py:61
  327.9 14.5 %copy.120 = bf16[1536,2,512]{2,1,0:T(2,128)(2,1)} copy(bf16[1536,2,512]{2,0,1:T(8,128)(2,1)S(1)} %add_convert_fusion) | data formatting | bytes 6291456 | tf_op jit(solution)/shard_map/convert_element_type | solution.py:161
  342.3 6.1 %convert_element_type.164 = bf16[4,4,96,1024]{3,2,1,0:T(8,128)(2,1)} reshape(bf16[1536,2,512]{2,1,0:T(2,128)(2,1)} %copy.120) | data formatting | bytes 6291456 | tf_op jit(solution)/shard_map/convert_element_type | solution.py:161
  359.6 12.6 %collective-permute-done.14 = bf16[4,96,1024]{2,1,0:T(8,128)(2,1)S(1)} collective-permute-done((bf16[4,96,1024]{2,1,0:T(8,128)(2,1)}, bf16[4,96,1024]{2,1,0:T(8,128)(2,1)S(1)}, u32[]{:S(2)}, u32[]{:S(2)}) %collective-permute-start.14) | collective-permute-done | bytes 786464 | tf_op jit(solution)/shard_map/ppermute | solution.py:20
  372.9 5.4 %collective-permute-done.15 = bf16[4,96,1024]{2,1,0:T(8,128)(2,1)S(1)} collective-permute-done((bf16[4,96,1024]{2,1,0:T(8,128)(2,1)}, bf16[4,96,1024]{2,1,0:T(8,128)(2,1)S(1)}, u32[]{:S(2)}, u32[]{:S(2)}) %collective-permute-start.15) | collective-permute-done | bytes 786464 | tf_op jit(solution)/shard_map/ppermute | solution.py:20
  378.3 6.8 %collective-permute-done.16 = bf16[4,96,1024]{2,1,0:T(8,128)(2,1)S(1)} collective-permute-done((bf16[4,96,1024]{2,1,0:T(8,128)(2,1)}, bf16[4,96,1024]{2,1,0:T(8,128)(2,1)S(1)}, u32[]{:S(2)}, u32[]{:S(2)}) %collective-permute-start.16) | collective-permute-done | bytes 786464 | tf_op jit(solution)/shard_map/ppermute | solution.py:20
  394.0 4.3 %collective-permute-done.18 = bf16[1,96,1024]{2,1,0:T(8,128)(2,1)S(1)} collective-permute-done((bf16[1,96,1024]{2,1,0:T(8,128)(2,1)S(1)}, bf16[1,96,1024]{2,1,0:T(8,128)(2,1)S(1)}, u32[]{:S(2)}, u32[]{:S(2)}) %collective-permute-start.18) | collective-permute-done | bytes 196640 | tf_op jit(solution)/shard_map/ppermute | solution.py:20
  (223 shorter events, 139.2 us)
Async XLA Ops:
  4.8 14.8 %collective-permute-start.1 = (bf16[144,1024]{1,0:T(8,128)(2,1)S(1)}, bf16[144,1024]{1,0:T(8,128)(2,1)S(1)}, u32[]{:S(2)}, u32[]{:S(2)}) collective-permute-start(bf16[144,1024]{1,0:T(8,128)(2,1)S(1)} %fusion.20), channel_id=1, source_target_pairs={{0,16},{8,24},{16,0},{24,8},{1,17},{9,25},{17,1},{25,9},{2,18},{10... | collective-permute-start | bytes 884744 | tf_op jit(solution)/shard_map/ppermute | solution.py:20
  23.8 27.9 %collective-permute-start.3 = (bf16[1,4,96,1024]{3,2,0,1:T(8,128)(2,1)}, bf16[1,4,96,1024]{3,2,0,1:T(8,128)(2,1)S(1)}, u32[]{:S(2)}, u32[]{:S(2)}) collective-permute-start(bf16[1,4,96,1024]{3,2,0,1:T(8,128)(2,1)} %get-tuple-element.16), channel_id=1, source_target_pairs={{0,2},{2,0},{4,6},{6,4},{1,3},{3,1},{5,7},{7,5},{8,10},{10,8},{12,... | collective-permute-start | bytes 2359304 | tf_op jit(solution)/shard_map/ppermute | solution.py:20
  37.2 55.3 %collective-permute-start.4 = (bf16[1,4,96,1024]{3,2,0,1:T(8,128)(2,1)}, bf16[1,4,96,1024]{3,2,0,1:T(8,128)(2,1)S(1)}, u32[]{:S(2)}, u32[]{:S(2)}) collective-permute-start(bf16[1,4,96,1024]{3,2,0,1:T(8,128)(2,1)} %get-tuple-element.15), channel_id=1, source_target_pairs={{0,4},{2,6},{4,0},{6,2},{1,5},{3,7},{5,1},{7,3},{8,12},{10,14},{12... | collective-permute-start | bytes 2359304 | tf_op jit(solution)/shard_map/ppermute | solution.py:20
  39.7 53.7 %collective-permute-start.5 = (bf16[1,4,96,1024]{3,2,0,1:T(8,128)(2,1)}, bf16[1,4,96,1024]{3,2,0,1:T(8,128)(2,1)S(1)}, u32[]{:S(2)}, u32[]{:S(2)}) collective-permute-start(bf16[1,4,96,1024]{3,2,0,1:T(8,128)(2,1)} %get-tuple-element.14), channel_id=1, source_target_pairs={{0,6},{2,4},{4,2},{6,0},{1,7},{3,5},{5,3},{7,1},{8,14},{10,12},{12... | collective-permute-start | bytes 2359304 | tf_op jit(solution)/shard_map/ppermute | solution.py:20
  94.4 121.8 %collective-permute-start.6 = (bf16[1536,1024]{1,0:T(8,128)(2,1)}, bf16[1536,1024]{1,0:T(8,128)(2,1)}, u32[]{:S(2)}, u32[]{:S(2)}) collective-permute-start(bf16[1536,1024]{1,0:T(8,128)(2,1)} %bitcast.14), channel_id=1, source_target_pairs={{0,1},{1,0},{2,3},{3,2},{4,5},{5,4},{6,7},{7,6},{8,9},{9,8},{10,11... | collective-permute-start | bytes 9437192 | tf_op jit(solution)/shard_map/ppermute | solution.py:20
  100.8 78.9 %collective-permute-start.7 = (bf16[1,512,1792]{2,1,0:T(8,128)(2,1)}, bf16[1,512,1792]{2,1,0:T(8,128)(2,1)}, u32[]{:S(2)}, u32[]{:S(2)}) collective-permute-start(bf16[1,512,1792]{2,1,0:T(8,128)(2,1)} %bitcast.181), channel_id=1, source_target_pairs={{0,8},{8,0},{16,24},{24,16},{1,9},{9,1},{17,25},{25,17},{2,10},{10... | collective-permute-start | bytes 5505032 | tf_op jit(solution)/shard_map/ppermute | solution.py:20
  105.8 77.1 %collective-permute-start.8 = (bf16[1,512,1792]{2,1,0:T(8,128)(2,1)}, bf16[1,512,1792]{2,1,0:T(8,128)(2,1)}, u32[]{:S(2)}, u32[]{:S(2)}) collective-permute-start(bf16[1,512,1792]{2,1,0:T(8,128)(2,1)} %bitcast.180), channel_id=1, source_target_pairs={{0,16},{8,24},{16,0},{24,8},{1,17},{9,25},{17,1},{25,9},{2,18},{10... | collective-permute-start | bytes 5505032 | tf_op jit(solution)/shard_map/ppermute | solution.py:20
  111.1 33.6 %collective-permute-start.20 = (bf16[32,896]{1,0:T(8,128)(2,1)S(1)}, bf16[32,896]{1,0:T(8,128)(2,1)S(1)}, u32[]{:S(2)}, u32[]{:S(2)}) collective-permute-start(bf16[32,896]{1,0:T(8,128)(2,1)S(1)} %bitcast.187), channel_id=1, source_target_pairs={{0,8},{8,0},{16,24},{24,16},{1,9},{9,1},{17,25},{25,17},{2,10},{10... | collective-permute-start | bytes 172040 | tf_op jit(solution)/shard_map/ppermute | solution.py:20
  111.7 38.9 %collective-permute-start.21 = (bf16[32,896]{1,0:T(8,128)(2,1)S(1)}, bf16[32,896]{1,0:T(8,128)(2,1)S(1)}, u32[]{:S(2)}, u32[]{:S(2)}) collective-permute-start(bf16[32,896]{1,0:T(8,128)(2,1)S(1)} %bitcast.186), channel_id=1, source_target_pairs={{0,16},{8,24},{16,0},{24,8},{1,17},{9,25},{17,1},{25,9},{2,18},{10... | collective-permute-start | bytes 172040 | tf_op jit(solution)/shard_map/ppermute | solution.py:20
  151.2 23.5 %collective-permute-start.10 = (bf16[1,896,512]{2,1,0:T(8,128)(2,1)}, bf16[1,896,512]{2,1,0:T(8,128)(2,1)S(1)}, u32[]{:S(2)}, u32[]{:S(2)}) collective-permute-start(bf16[1,896,512]{2,1,0:T(8,128)(2,1)} %get-tuple-element.9), channel_id=1, source_target_pairs={{0,8},{8,0},{16,24},{24,16},{1,9},{9,1},{17,25},{25,17},{2,10},{10... | collective-permute-start | bytes 2752520 | tf_op jit(solution)/shard_map/ppermute | solution.py:20
  155.5 59.1 %collective-permute-start.9 = (bf16[1,512,1792]{2,1,0:T(8,128)(2,1)}, bf16[1,512,1792]{2,1,0:T(8,128)(2,1)}, u32[]{:S(2)}, u32[]{:S(2)}) collective-permute-start(bf16[1,512,1792]{2,1,0:T(8,128)(2,1)} %bitcast.182), channel_id=1, source_target_pairs={{0,24},{8,16},{16,8},{24,0},{1,25},{9,17},{17,9},{25,1},{2,26},{10... | collective-permute-start | bytes 5505032 | tf_op jit(solution)/shard_map/ppermute | solution.py:20
  174.7 76.6 %collective-permute-start.11 = (bf16[1,896,512]{2,1,0:T(8,128)(2,1)S(1)}, bf16[1,896,512]{2,1,0:T(8,128)(2,1)S(1)}, u32[]{:S(2)}, u32[]{:S(2)}) collective-permute-start(bf16[1,896,512]{2,1,0:T(8,128)(2,1)S(1)} %copy-done.7), channel_id=1, source_target_pairs={{0,16},{8,24},{16,0},{24,8},{1,17},{9,25},{17,1},{25,9},{2,18},{10... | collective-permute-start | bytes 2752520 | tf_op jit(solution)/shard_map/ppermute | solution.py:20
  179.7 76.9 %collective-permute-start.12 = (bf16[1,896,512]{2,1,0:T(8,128)(2,1)}, bf16[1,896,512]{2,1,0:T(8,128)(2,1)}, u32[]{:S(2)}, u32[]{:S(2)}) collective-permute-start(bf16[1,896,512]{2,1,0:T(8,128)(2,1)} %get-tuple-element.7), channel_id=1, source_target_pairs={{0,24},{8,16},{16,8},{24,0},{1,25},{9,17},{17,9},{25,1},{2,26},{10... | collective-permute-start | bytes 2752520 | tf_op jit(solution)/shard_map/ppermute | solution.py:20
  259.5 23.0 %collective-permute-start.27 = (bf16[1,32,96]{2,1,0:T(8,128)(2,1)S(1)}, bf16[1,32,96]{2,1,0:T(8,128)(2,1)S(1)}, u32[]{:S(2)}, u32[]{:S(2)}) collective-permute-start(bf16[1,32,96]{2,1,0:T(8,128)(2,1)S(1)} %get-tuple-element.35), channel_id=1, source_target_pairs={{0,2},{2,0},{4,6},{6,4},{1,3},{3,1},{5,7},{7,5},{8,10},{10,8},{12,... | collective-permute-start | bytes 18440 | tf_op jit(solution)/shard_map/ppermute | solution.py:20
  280.0 41.1 %collective-permute-start.13 = (bf16[1536,2,512]{2,0,1:T(8,128)(2,1)}, bf16[1536,2,512]{2,0,1:T(8,128)(2,1)}, u32[]{:S(2)}, u32[]{:S(2)}) collective-permute-start(bf16[1536,2,512]{2,0,1:T(8,128)(2,1)} %convolution_convert_fusion.1), channel_id=1, source_target_pairs={{0,1},{1,0},{2,3},{3,2},{4,5},{5,4},{6,7},{7,6},{8,9},{9,8},{10,11... | collective-permute-start | bytes 9437192 | tf_op jit(solution)/shard_map/ppermute | solution.py:20
  312.5 40.2 %collective-permute-start.40 = (f32[16,896]{1,0:T(8,128)}, f32[16,896]{1,0:T(8,128)S(1)}, u32[]{:S(2)}, u32[]{:S(2)}) collective-permute-start(f32[16,896]{1,0:T(8,128)} %get-tuple-element.46), channel_id=1, source_target_pairs={{0,8},{8,0},{16,24},{24,16},{1,9},{9,1},{17,25},{25,17},{2,10},{10... | collective-permute-start | bytes 172040 | tf_op jit(solution)/shard_map/ppermute | solution.py:20
  312.7 42.3 %collective-permute-start.41 = (f32[16,896]{1,0:T(8,128)}, f32[16,896]{1,0:T(8,128)S(1)}, u32[]{:S(2)}, u32[]{:S(2)}) collective-permute-start(f32[16,896]{1,0:T(8,128)} %get-tuple-element.46), channel_id=1, source_target_pairs={{0,16},{8,24},{16,0},{24,8},{1,17},{9,25},{17,1},{25,9},{2,18},{10... | collective-permute-start | bytes 172040 | tf_op jit(solution)/shard_map/ppermute | solution.py:20
  313.8 41.4 %collective-permute-start.42 = (f32[16,896]{1,0:T(8,128)}, f32[16,896]{1,0:T(8,128)}, u32[]{:S(2)}, u32[]{:S(2)}) collective-permute-start(f32[16,896]{1,0:T(8,128)} %get-tuple-element.46), channel_id=1, source_target_pairs={{0,24},{8,16},{16,8},{24,0},{1,25},{9,17},{17,9},{25,1},{2,26},{10... | collective-permute-start | bytes 172040 | tf_op jit(solution)/shard_map/ppermute | solution.py:20
  351.5 20.7 %collective-permute-start.14 = (bf16[4,96,1024]{2,1,0:T(8,128)(2,1)}, bf16[4,96,1024]{2,1,0:T(8,128)(2,1)S(1)}, u32[]{:S(2)}, u32[]{:S(2)}) collective-permute-start(bf16[4,96,1024]{2,1,0:T(8,128)(2,1)} %get-tuple-element.11), channel_id=1, source_target_pairs={{0,8},{8,0},{16,24},{24,16},{1,9},{9,1},{17,25},{25,17},{2,10},{10... | collective-permute-start | bytes 2359304 | tf_op jit(solution)/shard_map/ppermute | solution.py:20
  351.7 26.6 %collective-permute-start.15 = (bf16[4,96,1024]{2,1,0:T(8,128)(2,1)}, bf16[4,96,1024]{2,1,0:T(8,128)(2,1)S(1)}, u32[]{:S(2)}, u32[]{:S(2)}) collective-permute-start(bf16[4,96,1024]{2,1,0:T(8,128)(2,1)} %get-tuple-element.13), channel_id=1, source_target_pairs={{0,16},{8,24},{16,0},{24,8},{1,17},{9,25},{17,1},{25,9},{2,18},{10... | collective-permute-start | bytes 2359304 | tf_op jit(solution)/shard_map/ppermute | solution.py:20
  352.8 32.4 %collective-permute-start.16 = (bf16[4,96,1024]{2,1,0:T(8,128)(2,1)}, bf16[4,96,1024]{2,1,0:T(8,128)(2,1)S(1)}, u32[]{:S(2)}, u32[]{:S(2)}) collective-permute-start(bf16[4,96,1024]{2,1,0:T(8,128)(2,1)} %get-tuple-element.12), channel_id=1, source_target_pairs={{0,24},{8,16},{16,8},{24,0},{1,25},{9,17},{17,9},{25,1},{2,26},{10... | collective-permute-start | bytes 2359304 | tf_op jit(solution)/shard_map/ppermute | solution.py:20
  358.3 31.5 %collective-permute-start.37 = (bf16[16,2048]{1,0:T(8,128)(2,1)S(1)}, bf16[16,2048]{1,0:T(8,128)(2,1)S(1)}, u32[]{:S(2)}, u32[]{:S(2)}) collective-permute-start(bf16[16,2048]{1,0:T(8,128)(2,1)S(1)} %add_convert_fusion.2), channel_id=1, source_target_pairs={{0,8},{8,0},{16,24},{24,16},{1,9},{9,1},{17,25},{25,17},{2,10},{10... | collective-permute-start | bytes 196616 | tf_op jit(solution)/shard_map/ppermute | solution.py:20
  358.5 31.2 %collective-permute-start.38 = (bf16[16,2048]{1,0:T(8,128)(2,1)S(1)}, bf16[16,2048]{1,0:T(8,128)(2,1)S(1)}, u32[]{:S(2)}, u32[]{:S(2)}) collective-permute-start(bf16[16,2048]{1,0:T(8,128)(2,1)S(1)} %add_convert_fusion.2), channel_id=1, source_target_pairs={{0,16},{8,24},{16,0},{24,8},{1,17},{9,25},{17,1},{25,9},{2,18},{10... | collective-permute-start | bytes 196616 | tf_op jit(solution)/shard_map/ppermute | solution.py:20
  372.2 17.6 %collective-permute-start.39 = (bf16[16,2048]{1,0:T(8,128)(2,1)S(1)}, bf16[16,2048]{1,0:T(8,128)(2,1)S(1)}, u32[]{:S(2)}, u32[]{:S(2)}) collective-permute-start(bf16[16,2048]{1,0:T(8,128)(2,1)S(1)} %add_convert_fusion.2), channel_id=1, source_target_pairs={{0,24},{8,16},{16,8},{24,0},{1,25},{9,17},{17,9},{25,1},{2,26},{10... | collective-permute-start | bytes 196616 | tf_op jit(solution)/shard_map/ppermute | solution.py:20
  (43 other events, 586.9 us)

commit v2 on v1

v2 whole, which is shorter than its diff:
```python
import functools

import jax
import jax.numpy as jnp
from jax import lax
from jax.experimental import pallas as pl
from jax.experimental.pallas import tpu as pltpu
from jax.sharding import PartitionSpec as P

adapter_scale = 2.0
f32 = jnp.float32
bf16 = jnp.bfloat16
highest = lax.Precision.HIGHEST
vmem_limit = 50 * 1024 * 1024


def partner(index, step, count):
    if count & (count - 1) == 0:
        return index ^ step, index ^ step
    return (index + step) % count, (index - step) % count


def send(value, axis, step):
    count = lax.axis_size(axis)
    return lax.ppermute(value, axis, [(i, partner(i, step, count)[0]) for i in range(count)])


def gather(value, axis):
    return [value] + [send(value, axis, step) for step in range(1, lax.axis_size(axis))]


def total(values):
    result = values[0].astype(f32)
    for value in values[1:]:
        result = result + value.astype(f32)
    return result


def dot(left, right, left_dim, right_dim, **options):
    return lax.dot_general(
        left, right, (((left_dim,), (right_dim,)), ((), ())), preferred_element_type=f32, **options
    )


def row_copies(place, own, other, scratch, sems, step, per_block, start):
    rows, width = scratch.shape[1], own[0].shape[1]
    slot = lax.rem(step, 2)
    first = pl.multiple_of(lax.rem(step, per_block) * rows, rows)

    def both(block):
        for half, (ref, side) in enumerate(((own[block], place[1]), (other[block], 1 - place[1]))):
            column = pl.multiple_of(side * width, width)
            copy = pltpu.make_async_copy(
                ref.at[pl.ds(first, rows)],
                scratch.at[slot, :, pl.ds(column, width)],
                sems.at[slot, half],
            )
            copy.start() if start else copy.wait()

    if start:
        for block in range(len(own)):
            pl.when(step // per_block == block)(functools.partial(both, block))
    else:
        both(0)


def forward_kernel(
    groups, experts, per_block, place, *refs
):
    refs = list(refs)
    own = [refs.pop(0) for _ in range(experts)]
    other = [refs.pop(0) for _ in range(experts)]
    gates = [refs.pop(0) for _ in range(groups)]
    ups = [refs.pop(0) for _ in range(groups)]
    adapter_in, adapter_part, tag_down = refs[:3]
    hidden, activated, low_rank, slot_logits = refs[3:7]
    gate, up, x_scratch, weight_sems, x_sems = refs[7:]
    step, steps = pl.program_id(0), pl.num_programs(0)
    depth = gates[0].shape[0]

    def weight_copies():
        for k in range(groups):
            _, source = partner(place[0], k, groups)
            row = pl.ds(pl.multiple_of(source * depth, depth), depth)
            yield pltpu.make_async_copy(gates[k], gate.at[row], weight_sems.at[0, k])
            yield pltpu.make_async_copy(ups[k], up.at[row], weight_sems.at[1, k])

    @pl.when(step == 0)
    def _():
        row_copies(place, own, other, x_scratch, x_sems, step, per_block, True)
        for copy in weight_copies():
            copy.start()

    @pl.when(step + 1 < steps)
    def _():
        row_copies(place, own, other, x_scratch, x_sems, step + 1, per_block, True)

    row_copies(place, own, other, x_scratch, x_sems, step, per_block, False)

    @pl.when(step == 0)
    def _():
        for copy in weight_copies():
            copy.wait()

    x = x_scratch[lax.rem(step, 2)]
    low = dot(x, adapter_in[...], 1, 1).astype(bf16)
    low_rank[...] = low
    gate_acc = dot(x, gate[...], 1, 0)
    act = gate_acc / (1.0 + jnp.exp(-gate_acc))
    activated[...] = act.astype(bf16)
    up_acc = dot(x, up[...], 1, 0) + adapter_scale * dot(low, adapter_part[...], 1, 0)
    value = (act * up_acc).astype(bf16)
    hidden[...] = value
    slot_logits[...] = dot(tag_down[...], value, 1, 1)


def forward(place, own, other, gates, ups, adapter_in, adapter_part, tag_down, rows):
    groups, experts = len(gates), len(own)
    block_rows, share = own[0].shape
    depth, width = gates[0].shape
    per_block = block_rows // rows
    slots = experts * block_rows
    tags, rank = tag_down.shape[0], adapter_in.shape[0]
    whole = lambda array: pl.BlockSpec(array.shape, lambda i, place: (0, 0))
    anywhere = pl.BlockSpec(memory_space=pl.ANY)
    return pl.pallas_call(
        functools.partial(forward_kernel, groups, experts, per_block),
        out_shape=(
            jax.ShapeDtypeStruct((slots, width), bf16),
            jax.ShapeDtypeStruct((slots, width), bf16),
            jax.ShapeDtypeStruct((slots, rank), bf16),
            jax.ShapeDtypeStruct((tags, slots), f32),
        ),
        grid_spec=pltpu.PrefetchScalarGridSpec(
            num_scalar_prefetch=1,
            grid=(slots // rows,),
            in_specs=[anywhere] * (2 * experts + 2 * groups)
            + [whole(adapter_in), whole(adapter_part), whole(tag_down)],
            out_specs=(
                pl.BlockSpec((rows, width), lambda i, place: (i, 0)),
                pl.BlockSpec((rows, width), lambda i, place: (i, 0)),
                pl.BlockSpec((rows, rank), lambda i, place: (i, 0)),
                pl.BlockSpec((tags, rows), lambda i, place: (0, i)),
            ),
            scratch_shapes=[
                pltpu.VMEM((groups * depth, width), bf16),
                pltpu.VMEM((groups * depth, width), bf16),
                pltpu.VMEM((2, rows, 2 * share), bf16),
                pltpu.SemaphoreType.DMA((2, groups)),
                pltpu.SemaphoreType.DMA((2, 2)),
            ],
        ),
        compiler_params=pltpu.CompilerParams(vmem_limit_bytes=vmem_limit),
        cost_estimate=pl.CostEstimate(
            flops=4 * slots * groups * depth * width,
            bytes_accessed=4 * groups * depth * width + 4 * slots * share + 4 * slots * width,
            transcendentals=slots * width,
        ),
        name="gate_up",
    )(place, *own, *other, *gates, *ups, adapter_in, adapter_part, tag_down)


def down_kernel(groups, add, place, hidden, *refs):
    refs = list(refs)
    downs = [refs.pop(0) for _ in range(groups)]
    came = refs.pop(0) if add else None
    weight, sems = refs[-2:]
    outs = refs[:-2]
    step = pl.program_id(0)
    half_count = groups // 2
    width = downs[0].shape[1]
    side = place[1] if add else 1 - place[1]

    @pl.when(step == 0)
    def _():
        for act in ("start", "wait"):
            for k in range(groups):
                _, source = partner(place[0], k, groups)
                column = pl.multiple_of(lax.rem(source, half_count) * width, width)
                copy = pltpu.make_async_copy(downs[k], weight.at[:, pl.ds(column, width)], sems.at[k])
                pl.when(source // half_count == side)(getattr(copy, act))

    value = dot(hidden[...], weight[...], 1, 0)
    if not add:
        outs[0][...] = value.astype(bf16)
        return
    value = (value + came[...].astype(f32)).astype(bf16)
    rows = outs[0].shape[0]
    per_step = value.shape[0] // rows
    for piece in range(groups):
        at = piece % per_step

        @pl.when(step == piece // per_step)
        def _():
            outs[piece][...] = value[at * rows : (at + 1) * rows]


def down(place, hidden, block, block_rows, rows, downs, came, capacity):
    groups = len(downs)
    width, part = downs[0].shape
    share = part * groups // 2
    per_block = block_rows // rows
    add = came is not None
    anywhere = pl.BlockSpec(memory_space=pl.ANY)
    if add:
        out_shape = [jax.ShapeDtypeStruct((capacity, share), bf16)] * groups
        out_specs = [pl.BlockSpec((capacity, share), lambda i, place: (0, 0))] * groups
    else:
        out_shape = jax.ShapeDtypeStruct((block_rows, share), bf16)
        out_specs = pl.BlockSpec((rows, share), lambda i, place: (i, 0))
    in_specs = [pl.BlockSpec((rows, width), lambda i, place: (block * per_block + i, 0))]
    in_specs += [anywhere] * groups
    if add:
        in_specs.append(pl.BlockSpec((rows, share), lambda i, place: (i, 0)))
    return pl.pallas_call(
        functools.partial(down_kernel, groups, add),
        out_shape=out_shape,
        grid_spec=pltpu.PrefetchScalarGridSpec(
            num_scalar_prefetch=1,
            grid=(per_block,),
            in_specs=in_specs,
            out_specs=out_specs,
            scratch_shapes=[pltpu.VMEM((width, share), bf16), pltpu.SemaphoreType.DMA((groups,))],
        ),
        compiler_params=pltpu.CompilerParams(vmem_limit_bytes=vmem_limit),
        cost_estimate=pl.CostEstimate(
            flops=2 * block_rows * width * share,
            bytes_accessed=2 * (block_rows * width + width * share + 2 * block_rows * share),
            transcendentals=0,
        ),
        name="down_own" if add else "down_other",
    )(place, hidden, *downs, *([came] if add else []))


def backward_kernel(experts, per_block, place, *refs):
    refs = list(refs)
    own = [refs.pop(0) for _ in range(experts)]
    other = [refs.pop(0) for _ in range(experts)]
    slot_grad, tag_down, activated, low_rank, adapter_part, out_grad, in_grad, x_scratch, x_sems = refs
    step, steps = pl.program_id(0), pl.num_programs(0)

    @pl.when(step == 0)
    def _():
        row_copies(place, own, other, x_scratch, x_sems, step, per_block, True)
        out_grad[...] = jnp.zeros_like(out_grad)
        in_grad[...] = jnp.zeros_like(in_grad)

    @pl.when(step + 1 < steps)
    def _():
        row_copies(place, own, other, x_scratch, x_sems, step + 1, per_block, True)

    hidden_grad = dot(slot_grad[...], tag_down[...], 0, 0)
    up_grad = (hidden_grad * activated[...].astype(f32)).astype(bf16)
    out_grad[...] += adapter_scale * dot(low_rank[...], up_grad, 0, 0)
    low_grad = (adapter_scale * dot(adapter_part[...], up_grad, 1, 1)).astype(bf16)
    row_copies(place, own, other, x_scratch, x_sems, step, per_block, False)
    in_grad[...] += dot(low_grad, x_scratch[lax.rem(step, 2)], 1, 0)


def backward(place, own, other, slot_grad, tag_down, activated, low_rank, adapter_part, rows):
    experts = len(own)
    block_rows, share = own[0].shape
    per_block = block_rows // rows
    tags, width = tag_down.shape
    slots, rank = low_rank.shape
    whole = lambda shape: pl.BlockSpec(shape, lambda i, place: (0, 0))
    anywhere = pl.BlockSpec(memory_space=pl.ANY)
    return pl.pallas_call(
        functools.partial(backward_kernel, experts, per_block),
        out_shape=(
            jax.ShapeDtypeStruct((rank, width), f32),
            jax.ShapeDtypeStruct((rank, 2 * share), f32),
        ),
        grid_spec=pltpu.PrefetchScalarGridSpec(
            num_scalar_prefetch=1,
            grid=(slots // rows,),
            in_specs=[anywhere] * (2 * experts)
            + [
                pl.BlockSpec((tags, rows), lambda i, place: (0, i)),
                whole(tag_down.shape),
                pl.BlockSpec((rows, width), lambda i, place: (i, 0)),
                pl.BlockSpec((rows, rank), lambda i, place: (i, 0)),
                whole(adapter_part.shape),
            ],
            out_specs=(whole((rank, width)), whole((rank, 2 * share))),
            scratch_shapes=[pltpu.VMEM((2, rows, 2 * share), bf16), pltpu.SemaphoreType.DMA((2, 2))],
        ),
        compiler_params=pltpu.CompilerParams(vmem_limit_bytes=vmem_limit),
        cost_estimate=pl.CostEstimate(
            flops=2 * slots * width * (tags + 2 * rank) + 4 * slots * share * rank,
            bytes_accessed=2 * slots * (width + 2 * share),
            transcendentals=0,
        ),
        name="adapter_grad",
    )(place, *own, *other, slot_grad, tag_down, activated, low_rank, adapter_part)


def local(
    tokens,
    expert_ids,
    gate_values,
    tag_labels,
    w_gate,
    w_up,
    w_down,
    adapter_in,
    adapter_out,
    tag_weight,
):
    experts = lax.axis_size("expert")
    groups = lax.axis_size("dp")
    dp, expert, tensor = lax.axis_index("dp"), lax.axis_index("expert"), lax.axis_index("tensor")
    place = jnp.stack([dp, tensor]).astype(jnp.int32)
    tok_count, model_width = tokens.shape
    share_width = model_width // lax.axis_size("tensor")
    capacity = 3 * tok_count // experts
    feature_part = w_gate.shape[1]
    hidden_part = w_gate.shape[2] // groups
    tags = tag_weight.shape[1]
    rank = adapter_in.shape[1]
    block_rows = groups * capacity
    rows = 4 * capacity

    member = expert_ids[None, :, :] == jnp.arange(experts, dtype=jnp.int32)[:, None, None]
    used = jnp.any(member, axis=2).astype(f32)
    weight = jnp.sum(jnp.where(member, gate_values[None], f32(0.0)), axis=2)
    upto = (jnp.arange(tok_count)[:, None] <= jnp.arange(tok_count)[None, :]).astype(f32)
    code = used * dot(used, upto, 1, 0)
    places = jnp.arange(1, capacity + 1, dtype=f32)
    order = jnp.stack([partner(expert, j, experts)[1] for j in range(experts)])
    ordered_code, ordered_weight = code[order], weight[order]
    own_match = ordered_code[:, None, :] == places[None, :, None]
    combine = jnp.where(own_match, ordered_weight[:, None, :], f32(0.0)).reshape(experts * capacity, tok_count)

    token_half = lax.dynamic_slice_in_dim(tokens, tensor * share_width, share_width, 1)
    plane_tokens = gather(token_half, "dp")
    code_rows = jnp.pad(code, ((0, 8 - experts), (0, 0)))
    plane_code = jnp.stack(gather(code_rows, "dp"))
    plane_tokens = jnp.stack(plane_tokens)
    x_own = []
    for j in range(experts):
        target, _ = partner(expert, j, experts)
        target_code = lax.dynamic_index_in_dim(plane_code, target, 1, keepdims=False)
        match = (target_code[:, None, :] == places[None, :, None]).astype(bf16)
        outgoing = jnp.einsum("gst,gtd->gsd", match, plane_tokens, preferred_element_type=f32).astype(bf16)
        outgoing = outgoing.reshape(block_rows, share_width)
        x_own.append(send(outgoing, "expert", j) if j else outgoing)
    x_other = [send(value, "tensor", 1) for value in x_own]

    tag_part = lax.dynamic_slice_in_dim(tag_weight, dp * feature_part, feature_part, 0)
    tag_down = dot(tag_part, w_down[0], 0, 1).astype(bf16)

    def spread(array, dim, size):
        pieces = []
        for k in range(groups):
            target, _ = partner(dp, k, groups)
            piece = lax.dynamic_slice_in_dim(array, target * size, size, dim)
            pieces.append(send(piece, "dp", k) if k else piece)
        return pieces

    tag_down = total(spread(tag_down, 1, hidden_part)).astype(bf16)
    gates = spread(w_gate[0], 1, hidden_part)
    ups = spread(w_up[0], 1, hidden_part)
    downs = spread(w_down[0], 0, hidden_part)
    adapter_part = lax.dynamic_slice_in_dim(adapter_out[0], dp * hidden_part, hidden_part, 1)

    hidden, activated, low_rank, slot_logits = forward(
        place, x_own, x_other, gates, ups, adapter_in[0], adapter_part, tag_down, rows
    )

    slot_logits = slot_logits + send(slot_logits.astype(bf16), "tensor", 1).astype(f32)
    slot_logits = slot_logits.reshape(tags, experts, groups, capacity).astype(bf16)
    pieces = [slot_logits[:, j] for j in range(experts)]
    pieces = [pieces[0]] + [send(pieces[j], "expert", j) for j in range(1, experts)]
    pieces = jnp.stack(pieces, axis=1)
    pieces = [pieces[:, :, k].reshape(tags, experts * capacity) for k in range(groups)]
    slot_logits = total([pieces[0]] + [send(pieces[k], "dp", k) for k in range(1, groups)])
    logits = dot(tag_weight, tokens, 0, 1) + dot(slot_logits, combine, 1, 0, precision=highest)
    exp_logits = jnp.exp(logits)
    probability = exp_logits / jnp.sum(exp_logits, axis=0, keepdims=True)
    labels_hot = (tag_labels[None, :] == jnp.arange(tags, dtype=jnp.int32)[:, None]).astype(f32)
    logit_grad = probability - labels_hot
    slot_grad = dot(logit_grad, combine, 1, 1, precision=highest).astype(bf16)
    slot_grad = slot_grad.reshape(tags, experts, capacity)
    slot_grad = [slot_grad[:, 0]] + [send(slot_grad[:, j], "expert", j) for j in range(1, experts)]
    slot_grad = gather(jnp.stack(slot_grad, axis=1).reshape(tags, experts * capacity), "dp")
    slot_grad = jnp.stack([value.reshape(tags, experts, capacity) for value in slot_grad], axis=2)
    slot_grad = slot_grad.reshape(tags, experts * block_rows)

    out_local, in_local = backward(
        place, x_own, x_other, slot_grad, tag_down, activated, low_rank, adapter_part, rows
    )
    in_local = in_local + send(in_local.astype(bf16), "tensor", 1).astype(f32)
    in_total = total(gather(in_local.astype(bf16), "dp"))
    out_total = jnp.zeros((rank, groups * hidden_part), f32)
    for k, value in enumerate(gather(out_local, "dp")):
        _, source = partner(dp, k, groups)
        out_total = lax.dynamic_update_slice_in_dim(out_total, value, source * hidden_part, 1)

    returned = [None] * experts
    for j in range(experts - 1, -1, -1):
        other = down(place, hidden, j, block_rows, rows, downs, None, capacity)
        pieces = down(place, hidden, j, block_rows, rows, downs, send(other, "tensor", 1), capacity)
        came = total([pieces[0]] + [send(pieces[k], "dp", k) for k in range(1, groups)]).astype(bf16)
        returned[j] = send(came, "expert", j) if j else came
    returned = jnp.concatenate(returned, axis=0)
    layer_out = token_half.astype(f32) + dot(combine, returned.astype(f32), 0, 0, precision=highest)
    return (layer_out.astype(bf16), in_total[None], out_total[None])


def solution(mesh):
    in_specs = (
        P(("dp", "expert"), None),
        P(("dp", "expert"), None),
        P(("dp", "expert"), None),
        P(("dp", "expert")),
        P("expert", "dp", "tensor"),
        P("expert", "dp", "tensor"),
        P("expert", "tensor", "dp"),
        P("expert", None, None),
        P("expert", None, "tensor"),
        P(),
    )
    out_specs = (
        P(("dp", "expert"), "tensor"),
        P("expert", None, None),
        P("expert", None, "tensor"),
    )
    return jax.shard_map(local, mesh=mesh, in_specs=in_specs, out_specs=out_specs, check_vma=False)
```

time: 407 us -> 320 us (0.79); the launches traced: 400 us -> 318 us
  local copies, waits for them, and re-layouts: 97.8 us -> 26.3 us
  Pallas kernels: 0 us -> 58.9 us
  waiting for transfers between devices: 180 us -> 126 us
  matrix products: 48.1 us -> 16.4 us
  starting transfers between devices: 61.1 us -> 82.9 us
  other arithmetic: 11.7 us -> 6.61 us
    pallas_call x0 -> x10, Pallas kernels: none -> 58.9 us  [the longest x8 30 us: down(): pl.pallas_call(functools.partial(down_kernel, groups, add), out_shape=out...]
    ppermute x43 -> x64, waiting for transfers between devices: 180 us -> 126 us  [send(): lax.ppermute(value, axis, [(i, partner(i, step, count)[0]) for i in range...]
    dot_general x15 -> x6, matrix products: 47.1 us -> 7.64 us  [dot(): lax.dot_general(left, right, (((left_dim,), (right_dim,)), ((), ())), pre...]
    dynamic_update_slice x34 -> x4, local copies, waits for them, and re-layouts: 27.3 us -> 0.03 us  [local(): lax.dynamic_update_slice_in_dim(out_total, value, source * hidden_part, 1)]
    ppermute x43 -> x64, starting transfers between devices: 61.1 us -> 82.9 us  [send(): lax.ppermute(value, axis, [(i, partner(i, step, count)[0]) for i in range...]
    convert_element_type x3, local copies, waits for them, and re-layouts: 20.7 us -> 3.27 us  [the longest x2 2.23 us: total(): result = values[0].astype(f32)]
    another operation x10 -> x13, local copies, waits for them, and re-layouts: 17.7 us -> 2.5 us  [the longest x3 2.09 us: local(): pieces[:, :, k].reshape(tags, experts * capacity)]
    unnamed x59 -> x76, local copies, waits for them, and re-layouts: 18.1 us -> 6.53 us
  transfers between devices with their start and end apart: 43 -> 64, of which waited for: 20 -> 17; matrix products, arithmetic and copies ran while one was open for 37% -> 13% of each run, Pallas kernels for 0% -> 19%
where the time goes in v2:
time: 320 us; the launch traced here: 318 us
  waiting for transfers between devices  126 us (39%)
  starting transfers between devices  82.9 us (26%)
  Pallas kernels  58.9 us (18%)
  local copies, waits for them, and re-layouts  26.3 us (8%)
  matrix products  16.4 us (5%)
  other arithmetic  6.61 us (2%)
    ppermute x64, waiting for transfers between devices, send(): lax.ppermute(value, axis, [(i, partner(i, step, count)[0]) for i in range...  126 us
    ppermute x64, starting transfers between devices, send(): lax.ppermute(value, axis, [(i, partner(i, step, count)[0]) for i in range...  82.9 us
    pallas_call x8, Pallas kernels, down(): pl.pallas_call(functools.partial(down_kernel, groups, add), out_shape=out...  30 us
    pallas_call x1, Pallas kernels, forward(): pl.pallas_call(functools.partial(forward_kernel, groups, experts, per_blo...  22.3 us
    dot_general x4, matrix products, local(): jnp.einsum('gst,gtd->gsd', match, plane_tokens, preferred_element_type=f32)  8.8 us
    dot_general x6, matrix products, dot(): lax.dot_general(left, right, (((left_dim,), (right_dim,)), ((), ())), pre...  7.64 us
    dynamic_slice x4, local copies, waits for them, and re-layouts, spread(): piece = lax.dynamic_slice_in_dim(array, target * size, size, dim)  7.37 us
    pallas_call x1, Pallas kernels, backward(): pl.pallas_call(functools.partial(backward_kernel, experts, per_block), ou...  6.67 us
  transfers between devices with their start and end apart: 64, of which 17 were waited for; matrix products, arithmetic and copies ran while one was open for 13% of the time, Pallas kernels for 19%

profile of v2, /device:TPU:0, one launch (start us, length us, event | category | flops | bytes accessed | tf_op | source)
XLA Modules:
  0.0 318.2 jit_solution(9359354869155466970)
XLA Ops:
  9.6 4.1 %dynamic-slice_bitcast_fusion.8 = (bf16[512,896]{1,0:T(8,128)(2,1)}, bf16[512,896]{1,0:T(8,128)(2,1)}, bf16[512,896]{1,0:T(8,128)(2,1)}, bf16[512,896]{1,0:T(8,128)(2,1)}) fusion(bf16[1,512,3584]{2,1,0:T(8,128)(2,1)} %param.14, s32[]{:T(128)S(6)} %select_n.79, s32[]{:T(128)S(6)} %select_n.77, s32[]{:T(128)S(6)} %select_n.76, s32[]{:T(128)S(6)} %select_n.78), kind=kLoop, calls=%fused_computation.23 | loop fusion | bytes 7340048 | tf_op jit(solution)/shard_map/dynamic_slice | solution.py:357
  15.3 3.2 %convolution_convert_fusion = bf16[32,3584]{1,0:T(8,128)(2,1)S(1)} fusion(bf16[1,3584,512]{2,1,0:T(8,128)(2,1)} %param.16, bf16[2048,32]{0,1:T(8,128)(2,1)S(1)} %copy-done.25, s32[]{:T(128)S(6)} %select_n.80), kind=kOutput, calls=%fused_computation.2 | convolution fusion | flops 117555200 | bytes 3932164 | tf_op jit(solution)/shard_map/dot_general | solution.py:40
  24.3 4.6 %collective-permute-done.5 = bf16[128,1024]{1,0:T(8,128)(2,1)} collective-permute-done((bf16[128,1024]{1,0:T(8,128)(2,1)S(1)}, bf16[128,1024]{1,0:T(8,128)(2,1)}, u32[]{:S(2)}, u32[]{:S(2)}) %collective-permute-start.5) | collective-permute-done | bytes 262176 | tf_op jit(solution)/shard_map/ppermute | solution.py:25
  31.9 34.0 %collective-permute-done.19 = bf16[32,896]{1,0:T(8,128)(2,1)S(1)} collective-permute-done((bf16[32,896]{1,0:T(8,128)(2,1)S(1)}, bf16[32,896]{1,0:T(8,128)(2,1)S(1)}, u32[]{:S(2)}, u32[]{:S(2)}) %collective-permute-start.19) | collective-permute-done | bytes 57376 | tf_op jit(solution)/shard_map/ppermute | solution.py:25
  82.8 6.6 %collective-permute-done.16.refs_13_ = bf16[512,896]{1,0:T(8,128)(2,1)} collective-permute-done((bf16[512,896]{1,0:T(8,128)(2,1)}, bf16[512,896]{1,0:T(8,128)(2,1)}, u32[]{:S(2)}, u32[]{:S(2)}) %collective-permute-start.16) | collective-permute-done | bytes 917536 | tf_op jit(solution)/shard_map/ppermute | solution.py:25
  90.9 20.5 %collective-permute-done.17.refs_14_ = bf16[512,896]{1,0:T(8,128)(2,1)} collective-permute-done((bf16[512,896]{1,0:T(8,128)(2,1)S(1)}, bf16[512,896]{1,0:T(8,128)(2,1)}, u32[]{:S(2)}, u32[]{:S(2)}) %collective-permute-start.17) | collective-permute-done | bytes 917536 | tf_op jit(solution)/shard_map/ppermute | solution.py:25
  111.9 20.7 %collective-permute-done.7.refs_2_ = bf16[384,1024]{1,0:T(8,128)(2,1)} collective-permute-done((bf16[384,1024]{1,0:T(8,128)(2,1)}, bf16[384,1024]{1,0:T(8,128)(2,1)}, u32[]{:S(2)}, u32[]{:S(2)}) %collective-permute-start.7) | collective-permute-done | bytes 786464 | tf_op jit(solution)/shard_map/ppermute | solution.py:25
  139.9 22.3 %gate_up.1 = (bf16[1536,896]{1,0:T(8,128)(2,1)}, bf16[1536,896]{1,0:T(8,128)(2,1)}, bf16[1536,16]{1,0:T(8,128)(2,1)S(1)}, f32[32,1536]{1,0:T(8,128)S(1)}) custom-call(s32[2]{0:T(128)S(1)} %pad_add_fusion.place, bf16[384,1024]{1,0:T(8,128)(2,1)S(1)} %bitcast.113, bf16[384,1024]{1,0:T(8,128)(2,1)} %collective-permute-done.6.refs_1_, ...), custom_call_target="tpu_custom_call" | custom-call | flops 11274289152 | bytes 19136512 | tf_op jit(solution)/shard_map/gate_up/pallas_call | solution.py:126
  171.0 11.2 %collective-permute-start.45 = (bf16[32,4,96]{2,0,1:T(8,128)(2,1)S(1)}, bf16[32,4,96]{2,0,1:T(8,128)(2,1)S(1)}, u32[]{:S(2)}, u32[]{:S(2)}) collective-permute-start(bf16[32,4,96]{2,0,1:T(8,128)(2,1)S(1)} %bitcast.116), channel_id=1, source_target_pairs={{0,2},{2,0},{4,6},{6,4},{1,3},{3,1},{5,7},{7,5},{8,10},{10,8},{12,... | collective-permute-start | bytes 73736 | tf_op jit(solution)/shard_map/ppermute | solution.py:25
  184.7 4.9 %down_other.4 = bf16[384,1024]{1,0:T(8,128)(2,1)} custom-call(s32[2]{0:T(128)S(1)} %pad_add_fusion.place, bf16[1536,896]{1,0:T(8,128)(2,1)} %get-tuple-element.25.hidden, bf16[896,512]{1,0:T(8,128)(2,1)S(1)} %get-tuple-element.49.refs_0_, bf16[896,512]{1,0:T(8,128)(2,1)S(1)} %collective-permute-done.22.refs_1_, ...), custom_call_target="tpu_custom_call" | custom-call | flops 704643072 | bytes 4096000 | tf_op jit(solution)/shard_map/down_other/pallas_call | solution.py:215
  196.1 5.0 %down_other.5 = bf16[384,1024]{1,0:T(8,128)(2,1)} custom-call(s32[2]{0:T(128)S(1)} %pad_add_fusion.place, bf16[1536,896]{1,0:T(8,128)(2,1)} %get-tuple-element.25.hidden, bf16[896,512]{1,0:T(8,128)(2,1)S(1)} %get-tuple-element.49.refs_0_, bf16[896,512]{1,0:T(8,128)(2,1)S(1)} %collective-permute-done.22.refs_1_, ...), custom_call_target="tpu_custom_call" | custom-call | flops 704643072 | bytes 4096000 | tf_op jit(solution)/shard_map/down_other/pallas_call | solution.py:215
  207.0 5.2 %collective-permute-start.51 = (bf16[32,96]{1,0:T(8,128)(2,1)S(1)}, bf16[32,96]{1,0:T(8,128)(2,1)S(1)}, u32[]{:S(2)}, u32[]{:S(2)}) collective-permute-start(bf16[32,96]{1,0:T(8,128)(2,1)S(1)} %bitcast.124), channel_id=1, source_target_pairs={{0,2},{2,0},{4,6},{6,4},{1,3},{3,1},{5,7},{7,5},{8,10},{10,8},{12,... | collective-permute-start | bytes 18440 | tf_op jit(solution)/shard_map/ppermute | solution.py:25
  214.9 3.9 %down_other.6 = bf16[384,1024]{1,0:T(8,128)(2,1)S(1)} custom-call(s32[2]{0:T(128)S(1)} %pad_add_fusion.place, bf16[1536,896]{1,0:T(8,128)(2,1)} %get-tuple-element.25.hidden, bf16[896,512]{1,0:T(8,128)(2,1)S(1)} %get-tuple-element.49.refs_0_, bf16[896,512]{1,0:T(8,128)(2,1)S(1)} %collective-permute-done.22.refs_1_, ...), custom_call_target="tpu_custom_call" | custom-call | flops 704643072 | bytes 4096000 | tf_op jit(solution)/shard_map/down_other/pallas_call | solution.py:215
  223.5 3.9 %down_other.7 = bf16[384,1024]{1,0:T(8,128)(2,1)S(1)} custom-call(s32[2]{0:T(128)S(1)} %pad_add_fusion.place, bf16[1536,896]{1,0:T(8,128)(2,1)} %get-tuple-element.25.hidden, bf16[896,512]{1,0:T(8,128)(2,1)S(1)} %get-tuple-element.49.refs_0_, bf16[896,512]{1,0:T(8,128)(2,1)S(1)} %collective-permute-done.22.refs_1_, ...), custom_call_target="tpu_custom_call" | custom-call | flops 704643072 | bytes 4096000 | tf_op jit(solution)/shard_map/down_other/pallas_call | solution.py:215
  231.1 6.7 %adapter_grad.1 = (f32[16,896]{1,0:T(8,128)S(1)}, f32[16,2048]{1,0:T(8,128)S(1)}) custom-call(s32[2]{0:T(128)S(1)} %pad_add_fusion.place, bf16[384,1024]{1,0:T(8,128)(2,1)S(1)} %bitcast.114, bf16[384,1024]{1,0:T(8,128)(2,1)} %collective-permute-done.6.refs_1_, bf16[384,1024]{1,0:T(8,128)(2,1)} %collective-permute-done.7.refs_2_, ...), custom_call_target="tpu_custom_call" | custom-call | flops 276824064 | bytes 9043968 | tf_op jit(solution)/shard_map/adapter_grad/pallas_call | solution.py:268
  244.3 3.4 %collective-permute-done.58 = bf16[16,2048]{1,0:T(8,128)(2,1)S(1)} collective-permute-done((bf16[16,2048]{1,0:T(8,128)(2,1)S(1)}, bf16[16,2048]{1,0:T(8,128)(2,1)S(1)}, u32[]{:S(2)}, u32[]{:S(2)}) %collective-permute-start.58) | collective-permute-done | bytes 65568 | tf_op jit(solution)/shard_map/ppermute | solution.py:25
  249.1 4.5 %collective-permute-done.60 = bf16[16,2048]{1,0:T(8,128)(2,1)S(1)} collective-permute-done((bf16[16,2048]{1,0:T(8,128)(2,1)S(1)}, bf16[16,2048]{1,0:T(8,128)(2,1)S(1)}, u32[]{:S(2)}, u32[]{:S(2)}) %collective-permute-start.60) | collective-permute-done | bytes 65568 | tf_op jit(solution)/shard_map/ppermute | solution.py:25
  254.3 3.2 down_own.5
  261.0 3.2 down_own.4
  268.5 3.6 %collective-permute-start.27 = (bf16[96,1024]{1,0:T(8,128)(2,1)S(1)}, bf16[96,1024]{1,0:T(8,128)(2,1)S(1)}, u32[]{:S(2)}, u32[]{:S(2)}) collective-permute-start(bf16[96,1024]{1,0:T(8,128)(2,1)S(1)} %get-tuple-element.28), channel_id=1, source_target_pairs={{0,16},{8,24},{16,0},{24,8},{1,17},{9,25},{17,1},{25,9},{2,18},{10... | collective-permute-start | bytes 589832 | tf_op jit(solution)/shard_map/ppermute | solution.py:25
  278.7 4.1 %collective-permute-done.35 = bf16[96,1024]{1,0:T(8,128)(2,1)S(1)} collective-permute-done((bf16[96,1024]{1,0:T(8,128)(2,1)S(1)}, bf16[96,1024]{1,0:T(8,128)(2,1)S(1)}, u32[]{:S(2)}, u32[]{:S(2)}) %collective-permute-start.35) | collective-permute-done | bytes 196640 | tf_op jit(solution)/shard_map/ppermute | solution.py:25
  292.8 6.0 %collective-permute-done.41 = bf16[96,1024]{1,0:T(8,128)(2,1)S(1)} collective-permute-done((bf16[96,1024]{1,0:T(8,128)(2,1)S(1)}, bf16[96,1024]{1,0:T(8,128)(2,1)S(1)}, u32[]{:S(2)}, u32[]{:S(2)}) %collective-permute-start.41) | collective-permute-done | bytes 196640 | tf_op jit(solution)/shard_map/ppermute | solution.py:25
  303.5 5.0 %collective-permute-done.33 = bf16[96,1024]{1,0:T(8,128)(2,1)S(1)} collective-permute-done((bf16[96,1024]{1,0:T(8,128)(2,1)S(1)}, bf16[96,1024]{1,0:T(8,128)(2,1)S(1)}, u32[]{:S(2)}, u32[]{:S(2)}) %collective-permute-start.33) | collective-permute-done | bytes 196640 | tf_op jit(solution)/shard_map/ppermute | solution.py:25
  308.5 8.3 %collective-permute-done.38 = bf16[96,1024]{1,0:T(8,128)(2,1)S(1)} collective-permute-done((bf16[96,1024]{1,0:T(8,128)(2,1)S(1)}, bf16[96,1024]{1,0:T(8,128)(2,1)S(1)}, u32[]{:S(2)}, u32[]{:S(2)}) %collective-permute-start.38) | collective-permute-done | bytes 196640 | tf_op jit(solution)/shard_map/ppermute | solution.py:25
  (262 shorter events, 118.7 us)
Async XLA Ops:
  18.8 56.8 %collective-permute-start.13 = (bf16[512,896]{1,0:T(8,128)(2,1)}, bf16[512,896]{1,0:T(8,128)(2,1)S(1)}, u32[]{:S(2)}, u32[]{:S(2)}) collective-permute-start(bf16[512,896]{1,0:T(8,128)(2,1)} %get-tuple-element.56), channel_id=1, source_target_pairs={{0,8},{8,0},{16,24},{24,16},{1,9},{9,1},{17,25},{25,17},{2,10},{10... | collective-permute-start | bytes 2752520 | tf_op jit(solution)/shard_map/ppermute | solution.py:25
  20.8 56.4 %collective-permute-start.14 = (bf16[512,896]{1,0:T(8,128)(2,1)}, bf16[512,896]{1,0:T(8,128)(2,1)S(1)}, u32[]{:S(2)}, u32[]{:S(2)}) collective-permute-start(bf16[512,896]{1,0:T(8,128)(2,1)} %get-tuple-element.58), channel_id=1, source_target_pairs={{0,16},{8,24},{16,0},{24,8},{1,17},{9,25},{17,1},{25,9},{2,18},{10... | collective-permute-start | bytes 2752520 | tf_op jit(solution)/shard_map/ppermute | solution.py:25
  22.3 57.5 %collective-permute-start.15 = (bf16[512,896]{1,0:T(8,128)(2,1)}, bf16[512,896]{1,0:T(8,128)(2,1)S(1)}, u32[]{:S(2)}, u32[]{:S(2)}) collective-permute-start(bf16[512,896]{1,0:T(8,128)(2,1)} %get-tuple-element.55), channel_id=1, source_target_pairs={{0,24},{8,16},{16,8},{24,0},{1,25},{9,17},{17,9},{25,1},{2,26},{10... | collective-permute-start | bytes 2752520 | tf_op jit(solution)/shard_map/ppermute | solution.py:25
  22.4 43.5 %collective-permute-start.19 = (bf16[32,896]{1,0:T(8,128)(2,1)S(1)}, bf16[32,896]{1,0:T(8,128)(2,1)S(1)}, u32[]{:S(2)}, u32[]{:S(2)}) collective-permute-start(bf16[32,896]{1,0:T(8,128)(2,1)S(1)} %get-tuple-element.59), channel_id=1, source_target_pairs={{0,8},{8,0},{16,24},{24,16},{1,9},{9,1},{17,25},{25,17},{2,10},{10... | collective-permute-start | bytes 172040 | tf_op jit(solution)/shard_map/ppermute | solution.py:25
  29.0 38.5 %collective-permute-start.20 = (bf16[32,896]{1,0:T(8,128)(2,1)S(1)}, bf16[32,896]{1,0:T(8,128)(2,1)S(1)}, u32[]{:S(2)}, u32[]{:S(2)}) collective-permute-start(bf16[32,896]{1,0:T(8,128)(2,1)S(1)} %get-tuple-element.61), channel_id=1, source_target_pairs={{0,16},{8,24},{16,0},{24,8},{1,17},{9,25},{17,1},{25,9},{2,18},{10... | collective-permute-start | bytes 172040 | tf_op jit(solution)/shard_map/ppermute | solution.py:25
  67.4 21.9 %collective-permute-start.16 = (bf16[512,896]{1,0:T(8,128)(2,1)}, bf16[512,896]{1,0:T(8,128)(2,1)}, u32[]{:S(2)}, u32[]{:S(2)}) collective-permute-start(bf16[512,896]{1,0:T(8,128)(2,1)} %get-tuple-element.52), channel_id=1, source_target_pairs={{0,8},{8,0},{16,24},{24,16},{1,9},{9,1},{17,25},{25,17},{2,10},{10... | collective-permute-start | bytes 2752520 | tf_op jit(solution)/shard_map/ppermute | solution.py:25
  71.6 39.7 %collective-permute-start.17 = (bf16[512,896]{1,0:T(8,128)(2,1)S(1)}, bf16[512,896]{1,0:T(8,128)(2,1)}, u32[]{:S(2)}, u32[]{:S(2)}) collective-permute-start(bf16[512,896]{1,0:T(8,128)(2,1)S(1)} %get-tuple-element.54), channel_id=1, source_target_pairs={{0,16},{8,24},{16,0},{24,8},{1,17},{9,25},{17,1},{25,9},{2,18},{10... | collective-permute-start | bytes 2752520 | tf_op jit(solution)/shard_map/ppermute | solution.py:25
  75.6 35.8 %collective-permute-start.6 = (bf16[384,1024]{1,0:T(8,128)(2,1)}, bf16[384,1024]{1,0:T(8,128)(2,1)}, u32[]{:S(2)}, u32[]{:S(2)}) collective-permute-start(bf16[384,1024]{1,0:T(8,128)(2,1)} %bitcast.20), channel_id=1, source_target_pairs={{0,2},{2,0},{4,6},{6,4},{1,3},{3,1},{5,7},{7,5},{8,10},{10,8},{12,... | collective-permute-start | bytes 2359304 | tf_op jit(solution)/shard_map/ppermute | solution.py:25
  77.2 55.4 %collective-permute-start.7 = (bf16[384,1024]{1,0:T(8,128)(2,1)}, bf16[384,1024]{1,0:T(8,128)(2,1)}, u32[]{:S(2)}, u32[]{:S(2)}) collective-permute-start(bf16[384,1024]{1,0:T(8,128)(2,1)} %bitcast.22), channel_id=1, source_target_pairs={{0,4},{2,6},{4,0},{6,2},{1,5},{3,7},{5,1},{7,3},{8,12},{10,14},{12... | collective-permute-start | bytes 2359304 | tf_op jit(solution)/shard_map/ppermute | solution.py:25
  79.8 52.8 %collective-permute-start.8 = (bf16[384,1024]{1,0:T(8,128)(2,1)}, bf16[384,1024]{1,0:T(8,128)(2,1)}, u32[]{:S(2)}, u32[]{:S(2)}) collective-permute-start(bf16[384,1024]{1,0:T(8,128)(2,1)} %bitcast.24), channel_id=1, source_target_pairs={{0,6},{2,4},{4,2},{6,0},{1,7},{3,5},{5,3},{7,1},{8,14},{10,12},{12... | collective-permute-start | bytes 2359304 | tf_op jit(solution)/shard_map/ppermute | solution.py:25
  89.4 45.8 %collective-permute-start.18 = (bf16[512,896]{1,0:T(8,128)(2,1)S(1)}, bf16[512,896]{1,0:T(8,128)(2,1)S(1)}, u32[]{:S(2)}, u32[]{:S(2)}) collective-permute-start(bf16[512,896]{1,0:T(8,128)(2,1)S(1)} %get-tuple-element.51), channel_id=1, source_target_pairs={{0,24},{8,16},{16,8},{24,0},{1,25},{9,17},{17,9},{25,1},{2,26},{10... | collective-permute-start | bytes 2752520 | tf_op jit(solution)/shard_map/ppermute | solution.py:25
  111.4 24.4 %collective-permute-start.9 = (bf16[384,1024]{1,0:T(8,128)(2,1)S(1)}, bf16[384,1024]{1,0:T(8,128)(2,1)S(1)}, u32[]{:S(2)}, u32[]{:S(2)}) collective-permute-start(bf16[384,1024]{1,0:T(8,128)(2,1)S(1)} %bitcast.112), channel_id=1, source_target_pairs={{0,1},{1,0},{2,3},{3,2},{4,5},{5,4},{6,7},{7,6},{8,9},{9,8},{10,11... | collective-permute-start | bytes 2359304 | tf_op jit(solution)/shard_map/ppermute | solution.py:25
  111.4 24.8 %collective-permute-start.10 = (bf16[384,1024]{1,0:T(8,128)(2,1)}, bf16[384,1024]{1,0:T(8,128)(2,1)S(1)}, u32[]{:S(2)}, u32[]{:S(2)}) collective-permute-start(bf16[384,1024]{1,0:T(8,128)(2,1)} %collective-permute-done.6.refs_1_), channel_id=1, source_target_pairs={{0,1},{1,0},{2,3},{3,2},{4,5},{5,4},{6,7},{7,6},{8,9},{9,8},{10,11... | collective-permute-start | bytes 2359304 | tf_op jit(solution)/shard_map/ppermute | solution.py:25
  135.2 48.1 %collective-permute-start.22 = (bf16[896,512]{1,0:T(8,128)(2,1)}, bf16[896,512]{1,0:T(8,128)(2,1)S(1)}, u32[]{:S(2)}, u32[]{:S(2)}) collective-permute-start(bf16[896,512]{1,0:T(8,128)(2,1)} %get-tuple-element.48), channel_id=1, source_target_pairs={{0,8},{8,0},{16,24},{24,16},{1,9},{9,1},{17,25},{25,17},{2,10},{10... | collective-permute-start | bytes 2752520 | tf_op jit(solution)/shard_map/ppermute | solution.py:25
  135.8 48.9 %collective-permute-start.23 = (bf16[896,512]{1,0:T(8,128)(2,1)}, bf16[896,512]{1,0:T(8,128)(2,1)S(1)}, u32[]{:S(2)}, u32[]{:S(2)}) collective-permute-start(bf16[896,512]{1,0:T(8,128)(2,1)} %get-tuple-element.50), channel_id=1, source_target_pairs={{0,16},{8,24},{16,0},{24,8},{1,17},{9,25},{17,1},{25,9},{2,18},{10... | collective-permute-start | bytes 2752520 | tf_op jit(solution)/shard_map/ppermute | solution.py:25
  136.2 48.5 %collective-permute-start.24 = (bf16[896,512]{1,0:T(8,128)(2,1)}, bf16[896,512]{1,0:T(8,128)(2,1)}, u32[]{:S(2)}, u32[]{:S(2)}) collective-permute-start(bf16[896,512]{1,0:T(8,128)(2,1)} %get-tuple-element.47), channel_id=1, source_target_pairs={{0,24},{8,16},{16,8},{24,0},{1,25},{9,17},{17,9},{25,1},{2,26},{10... | collective-permute-start | bytes 2752520 | tf_op jit(solution)/shard_map/ppermute | solution.py:25
  171.0 18.7 %collective-permute-start.45 = (bf16[32,4,96]{2,0,1:T(8,128)(2,1)S(1)}, bf16[32,4,96]{2,0,1:T(8,128)(2,1)S(1)}, u32[]{:S(2)}, u32[]{:S(2)}) collective-permute-start(bf16[32,4,96]{2,0,1:T(8,128)(2,1)S(1)} %bitcast.116), channel_id=1, source_target_pairs={{0,2},{2,0},{4,6},{6,4},{1,3},{3,1},{5,7},{7,5},{8,10},{10,8},{12,... | collective-permute-start | bytes 73736 | tf_op jit(solution)/shard_map/ppermute | solution.py:25
  189.6 70.4 %collective-permute-start.25 = (bf16[384,1024]{1,0:T(8,128)(2,1)}, bf16[384,1024]{1,0:T(8,128)(2,1)}, u32[]{:S(2)}, u32[]{:S(2)}) collective-permute-start(bf16[384,1024]{1,0:T(8,128)(2,1)} %down_other.4), channel_id=1, source_target_pairs={{0,1},{1,0},{2,3},{3,2},{4,5},{5,4},{6,7},{7,6},{8,9},{9,8},{10,11... | collective-permute-start | bytes 2359304 | tf_op jit(solution)/shard_map/ppermute | solution.py:25
  201.1 53.2 %collective-permute-start.29 = (bf16[384,1024]{1,0:T(8,128)(2,1)}, bf16[384,1024]{1,0:T(8,128)(2,1)}, u32[]{:S(2)}, u32[]{:S(2)}) collective-permute-start(bf16[384,1024]{1,0:T(8,128)(2,1)} %down_other.5), channel_id=1, source_target_pairs={{0,1},{1,0},{2,3},{3,2},{4,5},{5,4},{6,7},{7,6},{8,9},{9,8},{10,11... | collective-permute-start | bytes 2359304 | tf_op jit(solution)/shard_map/ppermute | solution.py:25
  244.2 20.0 %collective-permute-start.34 = (bf16[384,1024]{1,0:T(8,128)(2,1)S(1)}, bf16[384,1024]{1,0:T(8,128)(2,1)S(1)}, u32[]{:S(2)}, u32[]{:S(2)}) collective-permute-start(bf16[384,1024]{1,0:T(8,128)(2,1)S(1)} %copy-done.5), channel_id=1, source_target_pairs={{0,1},{1,0},{2,3},{3,2},{4,5},{5,4},{6,7},{7,6},{8,9},{9,8},{10,11... | collective-permute-start | bytes 2359304 | tf_op jit(solution)/shard_map/ppermute | solution.py:25
  247.6 20.8 %collective-permute-start.39 = (bf16[384,1024]{1,0:T(8,128)(2,1)S(1)}, bf16[384,1024]{1,0:T(8,128)(2,1)S(1)}, u32[]{:S(2)}, u32[]{:S(2)}) collective-permute-start(bf16[384,1024]{1,0:T(8,128)(2,1)S(1)} %copy-done.7), channel_id=1, source_target_pairs={{0,1},{1,0},{2,3},{3,2},{4,5},{5,4},{6,7},{7,6},{8,9},{9,8},{10,11... | collective-permute-start | bytes 2359304 | tf_op jit(solution)/shard_map/ppermute | solution.py:25
  257.5 17.6 %collective-permute-start.30 = (bf16[96,1024]{1,0:T(8,128)(2,1)S(1)}, bf16[96,1024]{1,0:T(8,128)(2,1)S(1)}, u32[]{:S(2)}, u32[]{:S(2)}) collective-permute-start(bf16[96,1024]{1,0:T(8,128)(2,1)S(1)} %get-tuple-element.31), channel_id=1, source_target_pairs={{0,8},{8,0},{16,24},{24,16},{1,9},{9,1},{17,25},{25,17},{2,10},{10... | collective-permute-start | bytes 589832 | tf_op jit(solution)/shard_map/ppermute | solution.py:25
  264.2 37.7 %collective-permute-start.26 = (bf16[96,1024]{1,0:T(8,128)(2,1)S(1)}, bf16[96,1024]{1,0:T(8,128)(2,1)S(1)}, u32[]{:S(2)}, u32[]{:S(2)}) collective-permute-start(bf16[96,1024]{1,0:T(8,128)(2,1)S(1)} %get-tuple-element.27), channel_id=1, source_target_pairs={{0,8},{8,0},{16,24},{24,16},{1,9},{9,1},{17,25},{25,17},{2,10},{10... | collective-permute-start | bytes 589832 | tf_op jit(solution)/shard_map/ppermute | solution.py:25
  268.5 34.9 %collective-permute-start.27 = (bf16[96,1024]{1,0:T(8,128)(2,1)S(1)}, bf16[96,1024]{1,0:T(8,128)(2,1)S(1)}, u32[]{:S(2)}, u32[]{:S(2)}) collective-permute-start(bf16[96,1024]{1,0:T(8,128)(2,1)S(1)} %get-tuple-element.28), channel_id=1, source_target_pairs={{0,16},{8,24},{16,0},{24,8},{1,17},{9,25},{17,1},{25,9},{2,18},{10... | collective-permute-start | bytes 589832 | tf_op jit(solution)/shard_map/ppermute | solution.py:25
  (74 other events, 953.8 us)

commit v3 on v2

v3 whole, which is shorter than its diff:
```python
import functools

import jax
import jax.numpy as jnp
from jax import lax
from jax.experimental import pallas as pl
from jax.experimental.pallas import tpu as pltpu
from jax.sharding import PartitionSpec as P

adapter_scale = 2.0
f32 = jnp.float32
bf16 = jnp.bfloat16
highest = lax.Precision.HIGHEST
vmem_limit = 50 * 1024 * 1024
lanes = 128


def send(value, axis, step):
    return lax.ppermute(value, axis, [(i, i ^ step) for i in range(lax.axis_size(axis))])


def gather(value, axis):
    return [value] + [send(value, axis, step) for step in range(1, lax.axis_size(axis))]


def swap(values, axis):
    return [values[0]] + [send(values[step], axis, step) for step in range(1, len(values))]


def after(value, *others):
    return lax.optimization_barrier((value, *others))[0]


def total(values):
    result = values[0].astype(f32)
    for value in values[1:]:
        result = result + value.astype(f32)
    return result


def dot(left, right, left_dim, right_dim, **options):
    return lax.dot_general(
        left, right, (((left_dim,), (right_dim,)), ((), ())), preferred_element_type=f32, **options
    )


def row_copies(place, own, other, scratch, sems, step, per_block):
    rows, width = scratch.shape[1], own[0].shape[1]
    slot = lax.rem(step, 2)
    first = pl.multiple_of(lax.rem(step, per_block) * rows, rows)

    def both(block):
        return [
            pltpu.make_async_copy(
                ref.at[pl.ds(first, rows)],
                scratch.at[slot, :, pl.ds(pl.multiple_of(side * width, width), width)],
                sems.at[slot, half],
            )
            for half, (ref, side) in enumerate(((own[block], place[1]), (other[block], 1 - place[1])))
        ]

    return [both(block) for block in range(len(own))]


def start_rows(place, own, other, scratch, sems, step, per_block):
    for block, copies in enumerate(row_copies(place, own, other, scratch, sems, step, per_block)):
        pl.when(step // per_block == block)(functools.partial(start, copies))


def wait_rows(place, own, other, scratch, sems, step, per_block):
    wait(row_copies(place, own, other, scratch, sems, step, per_block)[0])


def start(copies):
    for copy in copies:
        copy.start()


def wait(copies):
    for copy in copies:
        copy.wait()


def low_kernel(experts, per_block, place, *refs):
    own, other, refs = refs[:experts], refs[experts : 2 * experts], refs[2 * experts :]
    adapter_in, out, x_scratch, x_sems = refs
    step, steps = pl.program_id(0), pl.num_programs(0)
    pl.when(step == 0)(lambda: start_rows(place, own, other, x_scratch, x_sems, step, per_block))
    pl.when(step + 1 < steps)(lambda: start_rows(place, own, other, x_scratch, x_sems, step + 1, per_block))
    wait_rows(place, own, other, x_scratch, x_sems, step, per_block)
    out[...] = dot(x_scratch[lax.rem(step, 2)], adapter_in[...], 1, 1).astype(bf16)


def low(place, own, other, adapter_in, rows):
    experts = len(own)
    block_rows, share = own[0].shape
    rank = adapter_in.shape[0]
    return pl.pallas_call(
        functools.partial(low_kernel, experts, block_rows // rows),
        out_shape=jax.ShapeDtypeStruct((experts * block_rows, rank), bf16),
        grid_spec=pltpu.PrefetchScalarGridSpec(
            num_scalar_prefetch=1,
            grid=(experts * block_rows // rows,),
            in_specs=[pl.BlockSpec(memory_space=pl.ANY)] * (2 * experts)
            + [pl.BlockSpec(adapter_in.shape, lambda i, place: (0, 0))],
            out_specs=pl.BlockSpec((rows, rank), lambda i, place: (i, 0)),
            scratch_shapes=[pltpu.VMEM((2, rows, 2 * share), bf16), pltpu.SemaphoreType.DMA((2, 2))],
        ),
        compiler_params=pltpu.CompilerParams(vmem_limit_bytes=vmem_limit),
        name="low_rank",
    )(place, *own, *other, adapter_in)


def forward_kernel(experts, per_block, capacity, place, *refs):
    own, other, refs = refs[:experts], refs[experts : 2 * experts], refs[2 * experts :]
    low_rank, adapter_part, parts, refs = refs[0], refs[1], refs[2], refs[3:]
    groups = parts.shape[0]
    hidden, activated, slot_logits, tag_down = refs[:4]
    weight, tag_parts, x_scratch, added, weight_sems, tag_sems, x_sems = refs[4:]
    step, steps = pl.program_id(0), pl.num_programs(0)
    chunks, depth, pair = weight.shape[0], weight.shape[1] // groups, weight.shape[2]
    width, half = pair // 2, tag_parts.shape[2]
    copy = pltpu.make_async_copy

    def weight_copies(chunk):
        for k in range(groups):
            source = parts.at[k, chunk, pl.ds(0, depth)]
            yield copy(source, weight.at[chunk, pl.ds(k * depth, depth)], weight_sems.at[k, chunk])

    def tag_copies():
        for k in range(groups):
            yield copy(parts.at[k, :, pl.ds(depth, half)], tag_parts.at[k], tag_sems.at[k])

    def work(first):
        x = x_scratch[lax.rem(step, 2)]
        added[...] = adapter_scale * dot(low_rank[...], adapter_part[...], 1, 0)
        for chunk in range(chunks):
            if first:
                wait(weight_copies(chunk))
            columns = slice(chunk * width, (chunk + 1) * width)
            both = dot(x, weight[chunk], 1, 0)
            gate_acc = both[:, :width]
            act = gate_acc / (1.0 + jnp.exp(-gate_acc))
            activated[:, columns] = act.astype(bf16)
            hidden[:, columns] = (act * (both[:, width:] + added[:, columns])).astype(bf16)
        if first:
            wait(tag_copies())
            summed = jnp.sum(tag_parts[...].astype(f32), axis=0).astype(bf16)
            for chunk in range(chunks):
                columns = slice(chunk * width, (chunk + 1) * width)
                tag_down[:half, columns] = summed[chunk, :, :width]
                tag_down[half:, columns] = summed[chunk, :, width:]
        slot_logits[...] = jnp.zeros_like(slot_logits)
        logits = dot(tag_down[...], hidden[...], 1, 1).astype(bf16)
        for piece in range(x.shape[0] // capacity):
            slot_logits[:, piece * lanes : piece * lanes + capacity] = logits[
                :, piece * capacity : (piece + 1) * capacity
            ]

    @pl.when(step == 0)
    def _():
        start_rows(place, own, other, x_scratch, x_sems, step, per_block)
        for chunk in range(chunks):
            start(weight_copies(chunk))
        start(tag_copies())

    @pl.when(step + 1 < steps)
    def _():
        start_rows(place, own, other, x_scratch, x_sems, step + 1, per_block)

    wait_rows(place, own, other, x_scratch, x_sems, step, per_block)
    pl.when(step == 0)(lambda: work(True))
    pl.when(step > 0)(lambda: work(False))


def forward(place, own, other, parts, low_rank, adapter_part, tags, rows, capacity):
    groups, chunks, part_rows, pair = parts.shape
    width, depth = chunks * pair // 2, part_rows - tags // 2
    experts = len(own)
    block_rows, share = own[0].shape
    slots = experts * block_rows
    rank = low_rank.shape[1]
    wide = rows // capacity * lanes
    whole = lambda array: pl.BlockSpec(array.shape, lambda i, place: (0, 0))
    anywhere = pl.BlockSpec(memory_space=pl.ANY)
    return pl.pallas_call(
        functools.partial(forward_kernel, experts, block_rows // rows, capacity),
        out_shape=(
            jax.ShapeDtypeStruct((slots, width), bf16),
            jax.ShapeDtypeStruct((slots, width), bf16),
            jax.ShapeDtypeStruct((tags, slots // capacity * lanes), bf16),
            jax.ShapeDtypeStruct((tags, width), bf16),
        ),
        grid_spec=pltpu.PrefetchScalarGridSpec(
            num_scalar_prefetch=1,
            grid=(slots // rows,),
            in_specs=[anywhere] * (2 * experts)
            + [pl.BlockSpec((rows, rank), lambda i, place: (i, 0)), whole(adapter_part), anywhere],
            out_specs=(
                pl.BlockSpec((rows, width), lambda i, place: (i, 0)),
                pl.BlockSpec((rows, width), lambda i, place: (i, 0)),
                pl.BlockSpec((tags, wide), lambda i, place: (0, i)),
                pl.BlockSpec((tags, width), lambda i, place: (0, 0)),
            ),
            scratch_shapes=[
                pltpu.VMEM((chunks, groups * depth, pair), bf16),
                pltpu.VMEM((groups, chunks, tags // 2, pair), bf16),
                pltpu.VMEM((2, rows, 2 * share), bf16),
                pltpu.VMEM((rows, width), f32),
                pltpu.SemaphoreType.DMA((groups, chunks)),
                pltpu.SemaphoreType.DMA((groups,)),
                pltpu.SemaphoreType.DMA((2, 2)),
            ],
        ),
        compiler_params=pltpu.CompilerParams(vmem_limit_bytes=vmem_limit),
        name="gate_up",
    )(place, *own, *other, low_rank, adapter_part, parts)


def tag_kernel(pieces, *refs):
    parts, (token_logits, combine, labels, slot_grad) = refs[:pieces], refs[pieces:]
    slot_logits = total([part[...] for part in parts])
    logits = token_logits[...] + dot(slot_logits, combine[...], 1, 0, precision=highest)
    exp_logits = jnp.exp(logits)
    probability = exp_logits / jnp.sum(exp_logits, axis=0, keepdims=True)
    hot = labels[...] == lax.broadcasted_iota(jnp.int32, logits.shape, 0)
    logit_grad = probability - jnp.where(hot, f32(1.0), f32(0.0))
    slot_grad[...] = dot(logit_grad, combine[...], 1, 1, precision=highest).astype(bf16)


def fetch_down(groups, place, downs, weight, sems, side):
    half, width = groups // 2, weight.shape[1] // (groups // 2)
    for act in ("start", "wait"):
        for k in range(groups):
            source = place[0] ^ k
            column = pl.multiple_of(lax.rem(source, half) * width, width)
            copy = pltpu.make_async_copy(downs[k], weight.at[:, pl.ds(column, width)], sems.at[k])
            pl.when(source // half == side)(getattr(copy, act))


def other_kernel(groups, place, hidden, *refs):
    downs, (out, weight, sems) = refs[:-3], refs[-3:]
    pl.when(pl.program_id(0) == 0)(lambda: fetch_down(groups, place, downs, weight, sems, 1 - place[1]))
    out[...] = dot(hidden[...], weight[...], 1, 0).astype(bf16)


def own_kernel(groups, capacity, place, hidden, *refs):
    downs, (came, out, weight, sems) = refs[:-4], refs[-4:]
    step = pl.program_id(0)
    pl.when(step == 0)(lambda: fetch_down(groups, place, downs, weight, sems, place[1]))
    value = (dot(hidden[...], weight[...], 1, 0) + came[...].astype(f32)).astype(bf16)
    per_step = value.shape[0] // capacity
    for piece in range(out.shape[1] // capacity * groups):
        block, k = divmod(piece, groups)
        at = piece % per_step

        @pl.when(step == piece // per_step)
        def _():
            out[place[0] ^ k, block * capacity : (block + 1) * capacity] = value[
                at * capacity : (at + 1) * capacity
            ]


def down(place, hidden, groups, first, count, rows, downs, came, capacity):
    width, part = downs[0].shape[-2:]
    share = part * groups // 2
    if came is None:
        out_shape = jax.ShapeDtypeStruct((count, share), bf16)
        out_specs = pl.BlockSpec((rows, share), lambda i, place: (i, 0))
        kernel = functools.partial(other_kernel, groups)
    else:
        out_shape = jax.ShapeDtypeStruct((groups, count // groups, share), bf16)
        out_specs = pl.BlockSpec((groups, count // groups, share), lambda i, place: (0, 0, 0))
        kernel = functools.partial(own_kernel, groups, capacity)
    return pl.pallas_call(
        kernel,
        out_shape=out_shape,
        grid_spec=pltpu.PrefetchScalarGridSpec(
            num_scalar_prefetch=1,
            grid=(count // rows,),
            in_specs=[pl.BlockSpec((rows, width), lambda i, place: (first // rows + i, 0))]
            + [pl.BlockSpec(memory_space=pl.ANY)] * len(downs)
            + ([] if came is None else [pl.BlockSpec((rows, share), lambda i, place: (i, 0))]),
            out_specs=out_specs,
            scratch_shapes=[pltpu.VMEM((width, share), bf16), pltpu.SemaphoreType.DMA((groups,))],
        ),
        compiler_params=pltpu.CompilerParams(vmem_limit_bytes=vmem_limit),
        name="down_other" if came is None else "down_own",
    )(place, hidden, *downs, *([] if came is None else [came]))


def pack_kernel(place, gate, up, down, tag_part, out):
    depth, width = gate.shape
    product = dot(tag_part[...], down[...], 0, 1).astype(bf16)
    half = product.shape[0] // 2
    for chunk in range(width // lanes):
        columns = slice(chunk * lanes, (chunk + 1) * lanes)
        out[0, chunk, :depth, :lanes] = gate[:, columns]
        out[0, chunk, :depth, lanes:] = up[:, columns]
        out[0, chunk, depth:, :lanes] = product[:half, columns]
        out[0, chunk, depth:, lanes:] = product[half:, columns]


def pack(place, gate, up, down, tag_weight, groups):
    depth, width = gate.shape
    part, tags = width // groups, tag_weight.shape[1]
    if part % lanes:
        tag_part = lax.dynamic_slice_in_dim(tag_weight, place[0] * depth, depth, 0)
        product = dot(tag_part, down, 0, 1).astype(bf16)
        rows = [jnp.concatenate([gate, product[: tags // 2]]), jnp.concatenate([up, product[tags // 2 :]])]
        rows = jnp.stack(rows).reshape(2, depth + tags // 2, groups, part)
        return rows.transpose(2, 1, 0, 3).reshape(groups, 1, depth + tags // 2, 2 * part)
    return pl.pallas_call(
        pack_kernel,
        out_shape=jax.ShapeDtypeStruct((groups, part // lanes, depth + tags // 2, 2 * lanes), bf16),
        grid_spec=pltpu.PrefetchScalarGridSpec(
            num_scalar_prefetch=1,
            grid=(groups,),
            in_specs=[
                pl.BlockSpec((depth, part), lambda i, place: (0, i)),
                pl.BlockSpec((depth, part), lambda i, place: (0, i)),
                pl.BlockSpec((part, depth), lambda i, place: (i, 0)),
                pl.BlockSpec((depth, tags), lambda i, place: (place[0], 0)),
            ],
            out_specs=pl.BlockSpec((1, part // lanes, depth + tags // 2, 2 * lanes), lambda i, place: (i, 0, 0, 0)),
        ),
        compiler_params=pltpu.CompilerParams(vmem_limit_bytes=vmem_limit),
        name="pack",
    )(place, gate, up, down, tag_weight)


def backward_kernel(experts, per_block, capacity, place, *refs):
    own, other, refs = refs[:experts], refs[experts : 2 * experts], refs[2 * experts :]
    *slot_grad, tag_down, activated, low_rank, adapter_part, out_grad, in_grad, grads, x_scratch, x_sems = refs
    step, steps = pl.program_id(0), pl.num_programs(0)

    @pl.when(step == 0)
    def _():
        start_rows(place, own, other, x_scratch, x_sems, step, per_block)
        out_grad[...] = jnp.zeros_like(out_grad)
        in_grad[...] = jnp.zeros_like(in_grad)

    @pl.when(step + 1 < steps)
    def _():
        start_rows(place, own, other, x_scratch, x_sems, step + 1, per_block)

    pieces = activated.shape[0] // capacity
    for part in range(per_block):

        @pl.when(lax.rem(step, per_block) == part)
        def _():
            for piece in range(pieces):
                grads[piece] = slot_grad[part * pieces + piece][...]

    hidden_grad = jnp.concatenate([dot(grads[piece][:, :capacity], tag_down[...], 0, 0) for piece in range(pieces)])
    up_grad = (hidden_grad * activated[...].astype(f32)).astype(bf16)
    out_grad[...] += adapter_scale * dot(low_rank[...], up_grad, 0, 0)
    low_grad = (adapter_scale * dot(adapter_part[...], up_grad, 1, 1)).astype(bf16)
    wait_rows(place, own, other, x_scratch, x_sems, step, per_block)
    in_grad[...] += dot(low_grad, x_scratch[lax.rem(step, 2)], 1, 0)


def backward(place, own, other, slot_grad, tag_down, activated, low_rank, adapter_part, rows, capacity):
    experts = len(own)
    block_rows, share = own[0].shape
    per_block = block_rows // rows
    tags, width = tag_down.shape
    slots, rank = low_rank.shape
    whole = lambda shape: pl.BlockSpec(shape, lambda i, place: (0, 0))
    anywhere = pl.BlockSpec(memory_space=pl.ANY)
    return pl.pallas_call(
        functools.partial(backward_kernel, experts, per_block, capacity),
        out_shape=(
            jax.ShapeDtypeStruct((rank, width), f32),
            jax.ShapeDtypeStruct((rank, 2 * share), f32),
        ),
        grid_spec=pltpu.PrefetchScalarGridSpec(
            num_scalar_prefetch=1,
            grid=(slots // rows,),
            in_specs=[anywhere] * (2 * experts)
            + [
                *[pl.BlockSpec((tags, lanes), lambda i, place: (0, i // per_block))] * len(slot_grad),
                whole(tag_down.shape),
                pl.BlockSpec((rows, width), lambda i, place: (i, 0)),
                pl.BlockSpec((rows, rank), lambda i, place: (i, 0)),
                whole(adapter_part.shape),
            ],
            out_specs=(whole((rank, width)), whole((rank, 2 * share))),
            scratch_shapes=[
                pltpu.VMEM((rows // capacity, tags, lanes), bf16),
                pltpu.VMEM((2, rows, 2 * share), bf16),
                pltpu.SemaphoreType.DMA((2, 2)),
            ],
        ),
        compiler_params=pltpu.CompilerParams(vmem_limit_bytes=vmem_limit),
        name="adapter_grad",
    )(place, *own, *other, *slot_grad, tag_down, activated, low_rank, adapter_part)


def local(
    tokens,
    expert_ids,
    gate_values,
    tag_labels,
    w_gate,
    w_up,
    w_down,
    adapter_in,
    adapter_out,
    tag_weight,
):
    experts = lax.axis_size("expert")
    groups = lax.axis_size("dp")
    dp, expert, tensor = lax.axis_index("dp"), lax.axis_index("expert"), lax.axis_index("tensor")
    place = jnp.stack([dp, tensor]).astype(jnp.int32)
    tok_count, model_width = tokens.shape
    share_width = model_width // lax.axis_size("tensor")
    capacity = 3 * tok_count // experts
    feature_part = w_gate.shape[1]
    hidden_part = w_gate.shape[2] // groups
    tags = tag_weight.shape[1]
    rank = adapter_in.shape[1]
    block_rows = groups * capacity
    rows = 4 * capacity

    member = expert_ids[None, :, :] == jnp.arange(experts, dtype=jnp.int32)[:, None, None]
    used = jnp.any(member, axis=2).astype(f32)
    weight = jnp.sum(jnp.where(member, gate_values[None], f32(0.0)), axis=2)
    upto = (jnp.arange(tok_count)[:, None] <= jnp.arange(tok_count)[None, :]).astype(f32)
    code = used * dot(used, upto, 1, 0)
    order = jnp.arange(experts, dtype=jnp.int32) ^ expert
    places = jnp.arange(1, lanes + 1, dtype=jnp.int32).astype(f32)
    own_match = code[order][:, None, :] == places[None, :, None]
    combine = jnp.where(own_match, weight[order][:, None, :], f32(0.0)).reshape(experts * lanes, tok_count)

    token_half = lax.dynamic_slice_in_dim(tokens, tensor * share_width, share_width, 1)
    code_rows = jnp.pad(code.astype(bf16), ((0, 8 - experts), (0, share_width - tok_count)))
    plane = gather(jnp.concatenate([token_half, code_rows], axis=0), "dp")
    parts = pack(place, w_gate[0], w_up[0], w_down[0], tag_weight, groups)
    plane_parts = plane
    plane = jnp.stack(plane)
    plane_code = plane[:, tok_count : tok_count + experts, :tok_count].astype(f32)
    plane_tokens = plane[:, :tok_count]
    downs = [lax.dynamic_slice_in_dim(w_down[0], (dp ^ k) * hidden_part, hidden_part, 0) for k in range(groups)]
    plane_tokens = after(plane_tokens, parts, *downs)
    parts = lax.all_to_all(after(parts, *plane_parts), "dp", split_axis=0, concat_axis=0, tiled=True)
    x_own = []
    for j in range(experts):
        target_code = lax.dynamic_index_in_dim(plane_code, expert ^ j, 1, keepdims=False)
        match = (target_code[:, None, :] == places[None, :capacity, None]).astype(bf16)
        outgoing = jnp.einsum("gst,gtd->gsd", match, plane_tokens, preferred_element_type=f32).astype(bf16)
        x_own.append(outgoing.reshape(block_rows, share_width))
    x_own = swap(x_own, "expert")
    x_other = [send(value, "tensor", 1) for value in x_own]
    low_rank = low(place, x_own, x_other, adapter_in[0], rows)
    parts = after(parts, low_rank)
    downs = swap([after(piece, parts) for piece in downs], "dp")
    adapter_part = lax.dynamic_slice_in_dim(adapter_out[0], dp * hidden_part, hidden_part, 1)

    hidden, activated, slot_logits, tag_down = forward(
        place, x_own, x_other, parts, low_rank, adapter_part, tags, rows, capacity
    )

    slot_logits = (slot_logits.astype(f32) + send(slot_logits, "tensor", 1).astype(f32)).astype(bf16)
    plane_lanes = groups * lanes
    pieces = [slot_logits[:, j * plane_lanes : (j + 1) * plane_lanes] for j in range(experts)]
    pieces = swap(pieces, "expert")

    chunks = [(experts // 2, experts // 2), (0, experts // 2)]

    def product(chunk, came):
        first, count = chunks[chunk]
        return down(place, hidden, groups, first * block_rows, count * block_rows, rows, downs, came, capacity)

    hidden = after(hidden, *pieces)
    others, mine = [], []
    for chunk in range(len(chunks)):
        others.append(send(product(chunk, None), "tensor", 1))
        mine.append(product(chunk, others[chunk]))
        hidden = after(hidden, mine[chunk])
    came = [lax.all_to_all(part, "dp", split_axis=0, concat_axis=0, tiled=True) for part in mine]
    pieces = [
        jnp.concatenate([piece[:, k * lanes : (k + 1) * lanes] for piece in pieces], axis=1) for k in range(groups)
    ]
    pieces = swap(pieces, "dp")
    slot_grad = pl.pallas_call(
        functools.partial(tag_kernel, groups),
        out_shape=jax.ShapeDtypeStruct((tags, experts * lanes), bf16),
        compiler_params=pltpu.CompilerParams(vmem_limit_bytes=vmem_limit),
        name="tag_grad",
    )(*pieces, dot(tag_weight, tokens, 0, 1), combine, tag_labels[None, :])
    slot_grad = after(slot_grad, mine[-1])
    slot_grad = swap([slot_grad[:, j * lanes : (j + 1) * lanes] for j in range(experts)], "expert")
    slot_grad = gather(jnp.concatenate(slot_grad, axis=1), "dp")

    tag_down = after(tag_down, came[0])
    out_local, in_local = backward(
        place, x_own, x_other, slot_grad, tag_down, activated, low_rank, adapter_part, rows, capacity
    )
    in_local = in_local + send(in_local.astype(bf16), "tensor", 1).astype(f32)
    both = gather(jnp.concatenate([in_local, out_local], axis=1).astype(bf16), "dp")
    in_total = total([value[:, :model_width] for value in both])
    out_total = jnp.zeros((rank, groups * hidden_part), f32)
    for k, value in enumerate(both):
        out_total = lax.dynamic_update_slice_in_dim(
            out_total, value[:, model_width:].astype(f32), (dp ^ k) * hidden_part, 1
        )

    returned = [None] * experts
    for (first, count), value in zip(chunks, came):
        if first == 0:
            value = after(value, *returned[count:])
        value = jnp.sum(value.astype(f32), axis=0).astype(bf16)
        for j in range(first, first + count):
            kept = value[(j - first) * capacity : (j - first + 1) * capacity]
            returned[j] = send(kept, "expert", j) if j else kept
    layer_out = token_half.astype(f32)
    for j in range(experts):
        kept = combine[j * lanes : j * lanes + capacity]
        layer_out = layer_out + dot(kept, returned[j].astype(f32), 0, 0, precision=highest)
    layer_out = layer_out.astype(bf16)
    return (layer_out, in_total[None], out_total[None])


def solution(mesh):
    in_specs = (
        P(("dp", "expert"), None),
        P(("dp", "expert"), None),
        P(("dp", "expert"), None),
        P(("dp", "expert")),
        P("expert", "dp", "tensor"),
        P("expert", "dp", "tensor"),
        P("expert", "tensor", "dp"),
        P("expert", None, None),
        P("expert", None, "tensor"),
        P(),
    )
    out_specs = (
        P(("dp", "expert"), "tensor"),
        P("expert", None, None),
        P("expert", None, "tensor"),
    )
    return jax.shard_map(local, mesh=mesh, in_specs=in_specs, out_specs=out_specs, check_vma=False)
```

time: 320 us -> 264 us (0.82)
  waiting for transfers between devices: 126 us -> 94.8 us
  starting transfers between devices: 82.9 us -> 58.5 us
  matrix products: 16.4 us -> 7.13 us
  Pallas kernels: 58.9 us -> 64.4 us
    ppermute x64 -> x35, waiting for transfers between devices: 126 us -> 86.5 us  [send(): lax.ppermute(value, axis, [(i, i ^ step) for i in range(lax.axis_size(axi...]
    ppermute x64 -> x35, starting transfers between devices: 82.9 us -> 44.3 us  [send(): lax.ppermute(value, axis, [(i, i ^ step) for i in range(lax.axis_size(axi...]
    unnamed x76 -> x101, local copies, waits for them, and re-layouts: 6.53 us -> 21.2 us
    all_to_all x0 -> x3, starting transfers between devices: none -> 14.2 us  [the longest x2 8.72 us: local(): lax.all_to_all(part, 'dp', split_axis=0, concat_axis=0, tiled=True)]
    all_to_all x0 -> x3, waiting for transfers between devices: none -> 8.33 us  [the longest x1 8.32 us: local(): lax.all_to_all(after(parts, *plane_parts), 'dp', split_axis=0, concat_axi...]
    dot_general x4, matrix products: 8.8 us -> 1.67 us  [local(): jnp.einsum('gst,gtd->gsd', match, plane_tokens, preferred_element_type=f32)]
    pallas_call x10 -> x9, Pallas kernels: 58.9 us -> 64.4 us  [the longest x1 22.3 us: forward(): pl.pallas_call(functools.partial(forward_kernel, experts, block_rows // r...]
    reduce_sum x0 -> x2, other arithmetic: none -> 4.3 us  [local(): value = jnp.sum(value.astype(f32), axis=0).astype(bf16)]
  transfers between devices with their start and end apart: 64 -> 38, of which waited for: 17 -> 17; matrix products, arithmetic and copies ran while one was open for 13% -> 7% of each run, Pallas kernels for 19% -> 21%
where the time goes in v3:
time: 264 us; the launch traced here: 262 us
  waiting for transfers between devices  94.8 us (36%)
  Pallas kernels  64.4 us (24%)
  starting transfers between devices  58.5 us (22%)
  local copies, waits for them, and re-layouts  29.3 us (11%)
  matrix products  7.13 us (3%)
  other arithmetic  6.92 us (3%)
    ppermute x35, waiting for transfers between devices, send(): lax.ppermute(value, axis, [(i, i ^ step) for i in range(lax.axis_size(axi...  86.5 us
    ppermute x35, starting transfers between devices, send(): lax.ppermute(value, axis, [(i, i ^ step) for i in range(lax.axis_size(axi...  44.3 us
    pallas_call x1, Pallas kernels, forward(): pl.pallas_call(functools.partial(forward_kernel, experts, block_rows // r...  22.3 us
    unnamed x101, local copies, waits for them, and re-layouts  21.2 us
    pallas_call x4, Pallas kernels, down(): pl.pallas_call(kernel, out_shape=out_shape, grid_spec=pltpu.PrefetchScala...  21 us
    all_to_all x2, starting transfers between devices, local(): lax.all_to_all(part, 'dp', split_axis=0, concat_axis=0, tiled=True)  8.72 us
    pallas_call x1, Pallas kernels, pack(): pl.pallas_call(pack_kernel, out_shape=jax.ShapeDtypeStruct((groups, part...  8.71 us
    all_to_all x1, waiting for transfers between devices, local(): lax.all_to_all(after(parts, *plane_parts), 'dp', split_axis=0, concat_axi...  8.32 us
  transfers between devices with their start and end apart: 38, of which 17 were waited for; matrix products, arithmetic and copies ran while one was open for 7% of the time, Pallas kernels for 21%

profile of v3, /device:TPU:0, one launch (start us, length us, event | category | flops | bytes accessed | tf_op | source)
XLA Modules:
  0.0 262.5 jit_solution(4678074867539134106)
XLA Ops:
  1.8 4.0 %collective-permute-start.2 = (bf16[136,1024]{1,0:T(8,128)(2,1)S(1)}, bf16[136,1024]{1,0:T(8,128)(2,1)S(1)}, u32[]{:S(2)}, u32[]{:S(2)}) collective-permute-start(bf16[136,1024]{1,0:T(8,128)(2,1)S(1)} %get-tuple-element.48), channel_id=1, source_target_pairs={{0,24},{8,16},{16,8},{24,0},{1,25},{9,17},{17,9},{25,1},{2,26},{10... | collective-permute-start | bytes 835592 | tf_op jit(solution)/shard_map/ppermute | solution.py:19
  7.7 8.7 %pack.1 = bf16[4,7,528,256]{3,2,1,0:T(8,128)(2,1)} custom-call(s32[2]{0:T(128)S(1)} %pad_add_fusion.place, bf16[512,3584]{1,0:T(8,128)(2,1)} %bitcast.78, bf16[512,3584]{1,0:T(8,128)(2,1)} %bitcast.79, bf16[3584,512]{1,0:T(8,128)(2,1)} %bitcast.77, bf16[2048,32]{1,0:T(8,128)(2,1)S(1)} %copy.16.tag_part), custom_call_target="tpu_custom_call" | custom-call | tf_op jit(solution)/shard_map/pack/pallas_call | solution.py:313
  18.7 5.5 %all-to-all-start = ((bf16[4,7,528,256]{3,2,1,0:T(8,128)(2,1)}), bf16[4,7,528,256]{3,2,1,0:T(8,128)(2,1)}, u32[]{:S(2)}, u32[]{:S(2)}) async-start(bf16[4,7,528,256]{3,2,1,0:T(8,128)(2,1)} %pack.1), calls=%async_computation | async-start | bytes 15138816 | tf_op jit(solution)/shard_map/all_to_all | solution.py:446
  24.2 3.6 %dynamic-slice_bitcast_fusion = (bf16[896,512]{1,0:T(8,128)(2,1)}, bf16[896,512]{1,0:T(8,128)(2,1)}, bf16[896,512]{1,0:T(8,128)(2,1)S(1)}, bf16[896,512]{1,0:T(8,128)(2,1)}) fusion(bf16[1,3584,512]{2,1,0:T(8,128)(2,1)} %param.16, s32[]{:T(128)S(6)} %select_n.61, s32[]{:T(128)S(6)} %select_n.59, s32[]{:T(128)S(6)} %select_n.58, s32[]{:T(128)S(6)} %select_n.60), kind=kLoop, calls=%fused_computation.15 | loop fusion | bytes 7340048 | tf_op jit(solution)/shard_map/dynamic_slice | solution.py:444
  30.9 2.6 collective-permute-start.4
  34.2 30.4 %collective-permute-done.3.refs_1_ = bf16[384,1024]{1,0:T(8,128)(2,1)S(1)} collective-permute-done((bf16[384,1024]{1,0:T(8,128)(2,1)S(1)}, bf16[384,1024]{1,0:T(8,128)(2,1)S(1)}, u32[]{:S(2)}, u32[]{:S(2)}) %collective-permute-start.3) | collective-permute-done | bytes 786464 | tf_op jit(solution)/shard_map/ppermute | solution.py:19
  64.6 21.3 %collective-permute-done.4.refs_2_ = bf16[384,1024]{1,0:T(8,128)(2,1)S(1)} collective-permute-done((bf16[384,1024]{1,0:T(8,128)(2,1)S(1)}, bf16[384,1024]{1,0:T(8,128)(2,1)S(1)}, u32[]{:S(2)}, u32[]{:S(2)}) %collective-permute-start.4) | collective-permute-done | bytes 786464 | tf_op jit(solution)/shard_map/ppermute | solution.py:19
  90.2 4.9 %low_rank.1.refs_8_.refs_14_ = bf16[1536,16]{1,0:T(8,128)(2,1)S(1)} custom-call(s32[2]{0:T(128)S(1)} %pad_add_fusion.place, bf16[384,1024]{1,0:T(8,128)(2,1)S(1)} %bitcast.72, bf16[384,1024]{1,0:T(8,128)(2,1)S(1)} %collective-permute-done.3.refs_1_, bf16[384,1024]{1,0:T(8,128)(2,1)S(1)} %collective-permute-done.4.refs_2_, ...), custom_call_target="tpu_custom_call" | custom-call | tf_op jit(solution)/shard_map/low_rank/pallas_call | solution.py:98
  99.5 8.3 %all-to-all-done.refs_10_ = bf16[4,7,528,256]{3,2,1,0:T(8,128)(2,1)} async-done(((bf16[4,7,528,256]{3,2,1,0:T(8,128)(2,1)}), bf16[4,7,528,256]{3,2,1,0:T(8,128)(2,1)}, u32[]{:S(2)}, u32[]{:S(2)}) %all-to-all-start) | async-done | bytes 7569440 | tf_op jit(solution)/shard_map/all_to_all | solution.py:446
  117.6 22.3 %gate_up.1 = (bf16[1536,896]{1,0:T(8,128)(2,1)}, bf16[1536,896]{1,0:T(8,128)(2,1)}, bf16[32,2048]{1,0:T(8,128)(2,1)S(1)}, bf16[32,896]{1,0:T(8,128)(2,1)S(1)}) custom-call(s32[2]{0:T(128)S(1)} %pad_add_fusion.place, bf16[384,1024]{1,0:T(8,128)(2,1)S(1)} %bitcast.73, bf16[384,1024]{1,0:T(8,128)(2,1)S(1)} %copy-done.9, bf16[384,1024]{1,0:T(8,128)(2,1)S(1)} %copy-done.12, ...), custom_call_target="tpu_custom_call" | custom-call | tf_op jit(solution)/shard_map/gate_up/pallas_call | solution.py:186
  141.5 3.9 %collective-permute-start.13 = (bf16[32,512]{1,0:T(8,128)(2,1)S(1)}, bf16[32,512]{1,0:T(8,128)(2,1)S(1)}, u32[]{:S(2)}, u32[]{:S(2)}) collective-permute-start(bf16[32,512]{1,0:T(8,128)(2,1)S(1)} %get-tuple-element.53), channel_id=1, source_target_pairs={{0,6},{2,4},{4,2},{6,0},{1,7},{3,5},{5,3},{7,1},{8,14},{10,12},{12... | collective-permute-start | bytes 98312 | tf_op jit(solution)/shard_map/ppermute | solution.py:19
  145.4 4.3 %collective-permute-start.12 = (bf16[32,512]{1,0:T(8,128)(2,1)S(1)}, bf16[32,512]{1,0:T(8,128)(2,1)S(1)}, u32[]{:S(2)}, u32[]{:S(2)}) collective-permute-start(bf16[32,512]{1,0:T(8,128)(2,1)S(1)} %get-tuple-element.54), channel_id=1, source_target_pairs={{0,4},{2,6},{4,0},{6,2},{1,5},{3,7},{5,1},{7,3},{8,12},{10,14},{12... | collective-permute-start | bytes 98312 | tf_op jit(solution)/shard_map/ppermute | solution.py:19
  154.1 4.9 %down_other.2 = bf16[768,1024]{1,0:T(8,128)(2,1)} custom-call(s32[2]{0:T(128)S(1)} %pad_add_fusion.place, bf16[1536,896]{1,0:T(8,128)(2,1)} %get-tuple-element.31.hidden, bf16[896,512]{1,0:T(8,128)(2,1)S(1)} %get-tuple-element.27.refs_0_, bf16[896,512]{1,0:T(8,128)(2,1)S(1)} %collective-permute-done.14.refs_1_, ...), custom_call_target="tpu_custom_call" | custom-call | tf_op jit(solution)/shard_map/down_other/pallas_call | solution.py:275
  164.7 5.7 %down_own.2 = bf16[4,192,1024]{2,1,0:T(8,128)(2,1)} custom-call(s32[2]{0:T(128)S(1)} %copy-done.28, bf16[1536,896]{1,0:T(8,128)(2,1)} %get-tuple-element.31.hidden, bf16[896,512]{1,0:T(8,128)(2,1)S(1)} %get-tuple-element.27.refs_0_, bf16[896,512]{1,0:T(8,128)(2,1)S(1)} %collective-permute-done.14.refs_1_, ...), custom_call_target="tpu_custom_call" | custom-call | tf_op jit(solution)/shard_map/down_own/pallas_call | solution.py:275
  170.4 4.4 %all-to-all-start.2 = ((bf16[4,192,1024]{2,1,0:T(8,128)(2,1)}), bf16[4,192,1024]{2,1,0:T(8,128)(2,1)}, u32[]{:S(2)}, u32[]{:S(2)}) async-start(bf16[4,192,1024]{2,1,0:T(8,128)(2,1)} %down_own.2), calls=%async_computation.2 | async-start | bytes 3145728 | tf_op jit(solution)/shard_map/all_to_all | solution.py:481
  176.7 4.8 %down_other.3 = bf16[768,1024]{1,0:T(8,128)(2,1)} custom-call(s32[2]{0:T(128)S(1)} %copy-done.29, bf16[1536,896]{1,0:T(8,128)(2,1)} %get-tuple-element.31.hidden, bf16[896,512]{1,0:T(8,128)(2,1)S(1)} %get-tuple-element.27.refs_0_, bf16[896,512]{1,0:T(8,128)(2,1)S(1)} %collective-permute-done.14.refs_1_, ...), custom_call_target="tpu_custom_call" | custom-call | tf_op jit(solution)/shard_map/down_other/pallas_call | solution.py:275
  186.2 9.4 %collective-permute-done.22.refs_1_ = bf16[32,512]{1,0:T(8,128)(2,1)S(1)} collective-permute-done((bf16[32,512]{1,0:T(8,128)(2,1)S(1)}, bf16[32,512]{1,0:T(8,128)(2,1)S(1)}, u32[]{:S(2)}, u32[]{:S(2)}) %collective-permute-start.22) | collective-permute-done | bytes 32800 | tf_op jit(solution)/shard_map/ppermute | solution.py:19
  202.4 2.8 %collective-permute-start.20 = (bf16[96,1024]{1,0:T(8,128)(2,1)S(1)}, bf16[96,1024]{1,0:T(8,128)(2,1)S(1)}, u32[]{:S(2)}, u32[]{:S(2)}) collective-permute-start(bf16[96,1024]{1,0:T(8,128)(2,1)S(1)} %get-tuple-element.46), channel_id=1, source_target_pairs={{0,6},{2,4},{4,2},{6,0},{1,7},{3,5},{5,3},{7,1},{8,14},{10,12},{12... | collective-permute-start | bytes 589832 | tf_op jit(solution)/shard_map/ppermute | solution.py:19
  207.1 5.5 %down_own.3 = bf16[4,192,1024]{2,1,0:T(8,128)(2,1)} custom-call(s32[2]{0:T(128)S(1)} %copy-done.30, bf16[1536,896]{1,0:T(8,128)(2,1)} %get-tuple-element.31.hidden, bf16[896,512]{1,0:T(8,128)(2,1)S(1)} %get-tuple-element.27.refs_0_, bf16[896,512]{1,0:T(8,128)(2,1)S(1)} %collective-permute-done.14.refs_1_, ...), custom_call_target="tpu_custom_call" | custom-call | tf_op jit(solution)/shard_map/down_own/pallas_call | solution.py:275
  213.8 3.3 %collective-permute-start.26 = (bf16[32,128]{1,0:T(8,128)(2,1)S(1)}, bf16[32,128]{1,0:T(8,128)(2,1)S(1)}, u32[]{:S(2)}, u32[]{:S(2)}) collective-permute-start(bf16[32,128]{1,0:T(8,128)(2,1)S(1)} %get-tuple-element.58), channel_id=1, source_target_pairs={{0,4},{2,6},{4,0},{6,2},{1,5},{3,7},{5,1},{7,3},{8,12},{10,14},{12... | collective-permute-start | bytes 24584 | tf_op jit(solution)/shard_map/ppermute | solution.py:19
  226.0 4.4 %all-to-all-start.1 = ((bf16[4,192,1024]{2,1,0:T(8,128)(2,1)}), bf16[4,192,1024]{2,1,0:T(8,128)(2,1)}, u32[]{:S(2)}, u32[]{:S(2)}) async-start(bf16[4,192,1024]{2,1,0:T(8,128)(2,1)} %down_own.3), calls=%async_computation.1 | async-start | bytes 3145728 | tf_op jit(solution)/shard_map/all_to_all | solution.py:481
  233.2 6.9 %adapter_grad.1 = (f32[16,896]{1,0:T(8,128)S(1)}, f32[16,2048]{1,0:T(8,128)S(1)}) custom-call(s32[2]{0:T(128)S(1)} %copy-done.31, bf16[384,1024]{1,0:T(8,128)(2,1)S(1)} %bitcast.74, bf16[384,1024]{1,0:T(8,128)(2,1)S(1)} %copy-done.10, bf16[384,1024]{1,0:T(8,128)(2,1)S(1)} %copy-done.13, bf16[384,1024]{1,0:T(8,128)(2,1)S(1)} %copy-done.16, ...), custom_call_target="tpu_custom_call" | custom-call | tf_op jit(solution)/shard_map/adapter_grad/pallas_call | solution.py:371
  248.5 4.0 %collective-permute-done.33 = bf16[16,2944]{1,0:T(8,128)(2,1)S(1)} collective-permute-done((bf16[16,2944]{1,0:T(8,128)(2,1)S(1)}, bf16[16,2944]{1,0:T(8,128)(2,1)S(1)}, u32[]{:S(2)}, u32[]{:S(2)}) %collective-permute-start.33) | collective-permute-done | bytes 94240 | tf_op jit(solution)/shard_map/ppermute | solution.py:19
  255.8 5.5 %collective-permute-done.21 = bf16[96,1024]{1,0:T(8,128)(2,1)S(1)} collective-permute-done((bf16[96,1024]{1,0:T(8,128)(2,1)S(1)}, bf16[96,1024]{1,0:T(8,128)(2,1)S(1)}, u32[]{:S(2)}, u32[]{:S(2)}) %collective-permute-start.21) | collective-permute-done | bytes 196640 | tf_op jit(solution)/shard_map/ppermute | solution.py:19
  (214 shorter events, 79.6 us)
Async XLA Ops:
  1.8 14.6 %collective-permute-start.2 = (bf16[136,1024]{1,0:T(8,128)(2,1)S(1)}, bf16[136,1024]{1,0:T(8,128)(2,1)S(1)}, u32[]{:S(2)}, u32[]{:S(2)}) collective-permute-start(bf16[136,1024]{1,0:T(8,128)(2,1)S(1)} %get-tuple-element.48), channel_id=1, source_target_pairs={{0,24},{8,16},{16,8},{24,0},{1,25},{9,17},{17,9},{25,1},{2,26},{10... | collective-permute-start | bytes 835592 | tf_op jit(solution)/shard_map/ppermute | solution.py:19
  5.7 12.6 %collective-permute-start.1 = (bf16[136,1024]{1,0:T(8,128)(2,1)S(1)}, bf16[136,1024]{1,0:T(8,128)(2,1)S(1)}, u32[]{:S(2)}, u32[]{:S(2)}) collective-permute-start(bf16[136,1024]{1,0:T(8,128)(2,1)S(1)} %get-tuple-element.48), channel_id=1, source_target_pairs={{0,16},{8,24},{16,0},{24,8},{1,17},{9,25},{17,1},{25,9},{2,18},{10... | collective-permute-start | bytes 835592 | tf_op jit(solution)/shard_map/ppermute | solution.py:19
  6.3 12.4 %collective-permute-start = (bf16[136,1024]{1,0:T(8,128)(2,1)S(1)}, bf16[136,1024]{1,0:T(8,128)(2,1)S(1)}, u32[]{:S(2)}, u32[]{:S(2)}) collective-permute-start(bf16[136,1024]{1,0:T(8,128)(2,1)S(1)} %get-tuple-element.48), channel_id=1, source_target_pairs={{0,8},{8,0},{16,24},{24,16},{1,9},{9,1},{17,25},{25,17},{2,10},{10... | collective-permute-start | bytes 835592 | tf_op jit(solution)/shard_map/ppermute | solution.py:19
  18.7 89.2 %all-to-all-start = ((bf16[4,7,528,256]{3,2,1,0:T(8,128)(2,1)}), bf16[4,7,528,256]{3,2,1,0:T(8,128)(2,1)}, u32[]{:S(2)}, u32[]{:S(2)}) async-start(bf16[4,7,528,256]{3,2,1,0:T(8,128)(2,1)} %pack.1), calls=%async_computation | async-start | bytes 15138816 | tf_op jit(solution)/shard_map/all_to_all | solution.py:446
  29.2 35.4 %collective-permute-start.3 = (bf16[384,1024]{1,0:T(8,128)(2,1)S(1)}, bf16[384,1024]{1,0:T(8,128)(2,1)S(1)}, u32[]{:S(2)}, u32[]{:S(2)}) collective-permute-start(bf16[384,1024]{1,0:T(8,128)(2,1)S(1)} %bitcast.88), channel_id=1, source_target_pairs={{0,2},{2,0},{4,6},{6,4},{1,3},{3,1},{5,7},{7,5},{8,10},{10,8},{12,... | collective-permute-start | bytes 2359304 | tf_op jit(solution)/shard_map/ppermute | solution.py:19
  30.9 55.1 %collective-permute-start.4 = (bf16[384,1024]{1,0:T(8,128)(2,1)S(1)}, bf16[384,1024]{1,0:T(8,128)(2,1)S(1)}, u32[]{:S(2)}, u32[]{:S(2)}) collective-permute-start(bf16[384,1024]{1,0:T(8,128)(2,1)S(1)} %bitcast.87), channel_id=1, source_target_pairs={{0,4},{2,6},{4,0},{6,2},{1,5},{3,7},{5,1},{7,3},{8,12},{10,14},{12... | collective-permute-start | bytes 2359304 | tf_op jit(solution)/shard_map/ppermute | solution.py:19
  33.4 52.5 %collective-permute-start.5 = (bf16[384,1024]{1,0:T(8,128)(2,1)S(1)}, bf16[384,1024]{1,0:T(8,128)(2,1)S(1)}, u32[]{:S(2)}, u32[]{:S(2)}) collective-permute-start(bf16[384,1024]{1,0:T(8,128)(2,1)S(1)} %bitcast.86), channel_id=1, source_target_pairs={{0,6},{2,4},{4,2},{6,0},{1,7},{3,5},{5,3},{7,1},{8,14},{10,12},{12... | collective-permute-start | bytes 2359304 | tf_op jit(solution)/shard_map/ppermute | solution.py:19
  34.1 52.3 %collective-permute-start.6 = (bf16[384,1024]{1,0:T(8,128)(2,1)S(1)}, bf16[384,1024]{1,0:T(8,128)(2,1)S(1)}, u32[]{:S(2)}, u32[]{:S(2)}) collective-permute-start(bf16[384,1024]{1,0:T(8,128)(2,1)S(1)} %bitcast.71), channel_id=1, source_target_pairs={{0,1},{1,0},{2,3},{3,2},{4,5},{5,4},{6,7},{7,6},{8,9},{9,8},{10,11... | collective-permute-start | bytes 2359304 | tf_op jit(solution)/shard_map/ppermute | solution.py:19
  64.6 21.8 %collective-permute-start.7 = (bf16[384,1024]{1,0:T(8,128)(2,1)S(1)}, bf16[384,1024]{1,0:T(8,128)(2,1)S(1)}, u32[]{:S(2)}, u32[]{:S(2)}) collective-permute-start(bf16[384,1024]{1,0:T(8,128)(2,1)S(1)} %collective-permute-done.3.refs_1_), channel_id=1, source_target_pairs={{0,1},{1,0},{2,3},{3,2},{4,5},{5,4},{6,7},{7,6},{8,9},{9,8},{10,11... | collective-permute-start | bytes 2359304 | tf_op jit(solution)/shard_map/ppermute | solution.py:19
  107.9 46.2 %collective-permute-start.14 = (bf16[896,512]{1,0:T(8,128)(2,1)}, bf16[896,512]{1,0:T(8,128)(2,1)S(1)}, u32[]{:S(2)}, u32[]{:S(2)}) collective-permute-start(bf16[896,512]{1,0:T(8,128)(2,1)} %get-tuple-element.28), channel_id=1, source_target_pairs={{0,8},{8,0},{16,24},{24,16},{1,9},{9,1},{17,25},{25,17},{2,10},{10... | collective-permute-start | bytes 2752520 | tf_op jit(solution)/shard_map/ppermute | solution.py:19
  109.3 44.7 %collective-permute-start.15 = (bf16[896,512]{1,0:T(8,128)(2,1)}, bf16[896,512]{1,0:T(8,128)(2,1)S(1)}, u32[]{:S(2)}, u32[]{:S(2)}) collective-permute-start(bf16[896,512]{1,0:T(8,128)(2,1)} %get-tuple-element.29), channel_id=1, source_target_pairs={{0,16},{8,24},{16,0},{24,8},{1,17},{9,25},{17,1},{25,9},{2,18},{10... | collective-permute-start | bytes 2752520 | tf_op jit(solution)/shard_map/ppermute | solution.py:19
  109.9 44.2 %collective-permute-start.16 = (bf16[896,512]{1,0:T(8,128)(2,1)}, bf16[896,512]{1,0:T(8,128)(2,1)S(1)}, u32[]{:S(2)}, u32[]{:S(2)}) collective-permute-start(bf16[896,512]{1,0:T(8,128)(2,1)} %get-tuple-element.30), channel_id=1, source_target_pairs={{0,24},{8,16},{16,8},{24,0},{1,25},{9,17},{17,9},{25,1},{2,26},{10... | collective-permute-start | bytes 2752520 | tf_op jit(solution)/shard_map/ppermute | solution.py:19
  141.5 8.2 %collective-permute-start.13 = (bf16[32,512]{1,0:T(8,128)(2,1)S(1)}, bf16[32,512]{1,0:T(8,128)(2,1)S(1)}, u32[]{:S(2)}, u32[]{:S(2)}) collective-permute-start(bf16[32,512]{1,0:T(8,128)(2,1)S(1)} %get-tuple-element.53), channel_id=1, source_target_pairs={{0,6},{2,4},{4,2},{6,0},{1,7},{3,5},{5,3},{7,1},{8,14},{10,12},{12... | collective-permute-start | bytes 98312 | tf_op jit(solution)/shard_map/ppermute | solution.py:19
  170.4 27.6 %all-to-all-start.2 = ((bf16[4,192,1024]{2,1,0:T(8,128)(2,1)}), bf16[4,192,1024]{2,1,0:T(8,128)(2,1)}, u32[]{:S(2)}, u32[]{:S(2)}) async-start(bf16[4,192,1024]{2,1,0:T(8,128)(2,1)} %down_own.2), calls=%async_computation.2 | async-start | bytes 3145728 | tf_op jit(solution)/shard_map/all_to_all | solution.py:481
  181.5 23.7 %collective-permute-start.18 = (bf16[768,1024]{1,0:T(8,128)(2,1)}, bf16[768,1024]{1,0:T(8,128)(2,1)}, u32[]{:S(2)}, u32[]{:S(2)}) collective-permute-start(bf16[768,1024]{1,0:T(8,128)(2,1)} %down_other.3), channel_id=1, source_target_pairs={{0,1},{1,0},{2,3},{3,2},{4,5},{5,4},{6,7},{7,6},{8,9},{9,8},{10,11... | collective-permute-start | bytes 4718600 | tf_op jit(solution)/shard_map/ppermute | solution.py:19
  182.6 13.0 %collective-permute-start.22 = (bf16[32,512]{1,0:T(8,128)(2,1)S(1)}, bf16[32,512]{1,0:T(8,128)(2,1)S(1)}, u32[]{:S(2)}, u32[]{:S(2)}) collective-permute-start(bf16[32,512]{1,0:T(8,128)(2,1)S(1)} %pad_maximum_fusion.5), channel_id=1, source_target_pairs={{0,8},{8,0},{16,24},{24,16},{1,9},{9,1},{17,25},{25,17},{2,10},{10... | collective-permute-start | bytes 98312 | tf_op jit(solution)/shard_map/ppermute | solution.py:19
  184.5 11.1 %collective-permute-start.23 = (bf16[32,512]{1,0:T(8,128)(2,1)S(1)}, bf16[32,512]{1,0:T(8,128)(2,1)S(1)}, u32[]{:S(2)}, u32[]{:S(2)}) collective-permute-start(bf16[32,512]{1,0:T(8,128)(2,1)S(1)} %pad_maximum_fusion.6), channel_id=1, source_target_pairs={{0,16},{8,24},{16,0},{24,8},{1,17},{9,25},{17,1},{25,9},{2,18},{10... | collective-permute-start | bytes 98312 | tf_op jit(solution)/shard_map/ppermute | solution.py:19
  186.0 10.8 %collective-permute-start.24 = (bf16[32,512]{1,0:T(8,128)(2,1)S(1)}, bf16[32,512]{1,0:T(8,128)(2,1)S(1)}, u32[]{:S(2)}, u32[]{:S(2)}) collective-permute-start(bf16[32,512]{1,0:T(8,128)(2,1)S(1)} %pad_maximum_fusion.7), channel_id=1, source_target_pairs={{0,24},{8,16},{16,8},{24,0},{1,25},{9,17},{17,9},{25,1},{2,26},{10... | collective-permute-start | bytes 98312 | tf_op jit(solution)/shard_map/ppermute | solution.py:19
  202.4 22.4 %collective-permute-start.20 = (bf16[96,1024]{1,0:T(8,128)(2,1)S(1)}, bf16[96,1024]{1,0:T(8,128)(2,1)S(1)}, u32[]{:S(2)}, u32[]{:S(2)}) collective-permute-start(bf16[96,1024]{1,0:T(8,128)(2,1)S(1)} %get-tuple-element.46), channel_id=1, source_target_pairs={{0,6},{2,4},{4,2},{6,0},{1,7},{3,5},{5,3},{7,1},{8,14},{10,12},{12... | collective-permute-start | bytes 589832 | tf_op jit(solution)/shard_map/ppermute | solution.py:19
  217.2 26.4 %collective-permute-start.19 = (bf16[96,1024]{1,0:T(8,128)(2,1)}, bf16[96,1024]{1,0:T(8,128)(2,1)}, u32[]{:S(2)}, u32[]{:S(2)}) collective-permute-start(bf16[96,1024]{1,0:T(8,128)(2,1)} %get-tuple-element.45), channel_id=1, source_target_pairs={{0,4},{2,6},{4,0},{6,2},{1,5},{3,7},{5,1},{7,3},{8,12},{10,14},{12... | collective-permute-start | bytes 589832 | tf_op jit(solution)/shard_map/ppermute | solution.py:19
  221.3 9.1 %collective-permute-start.30 = (bf16[32,512]{1,0:T(8,128)(2,1)}, bf16[32,512]{1,0:T(8,128)(2,1)}, u32[]{:S(2)}, u32[]{:S(2)}) collective-permute-start(bf16[32,512]{1,0:T(8,128)(2,1)} %pad_maximum_fusion.8.refs_8_), channel_id=1, source_target_pairs={{0,24},{8,16},{16,8},{24,0},{1,25},{9,17},{17,9},{25,1},{2,26},{10... | collective-permute-start | bytes 98312 | tf_op jit(solution)/shard_map/ppermute | solution.py:19
  222.4 8.0 %collective-permute-start.29 = (bf16[32,512]{1,0:T(8,128)(2,1)}, bf16[32,512]{1,0:T(8,128)(2,1)}, u32[]{:S(2)}, u32[]{:S(2)}) collective-permute-start(bf16[32,512]{1,0:T(8,128)(2,1)} %pad_maximum_fusion.8.refs_8_), channel_id=1, source_target_pairs={{0,16},{8,24},{16,0},{24,8},{1,17},{9,25},{17,1},{25,9},{2,18},{10... | collective-permute-start | bytes 98312 | tf_op jit(solution)/shard_map/ppermute | solution.py:19
  226.0 27.3 %all-to-all-start.1 = ((bf16[4,192,1024]{2,1,0:T(8,128)(2,1)}), bf16[4,192,1024]{2,1,0:T(8,128)(2,1)}, u32[]{:S(2)}, u32[]{:S(2)}) async-start(bf16[4,192,1024]{2,1,0:T(8,128)(2,1)} %down_own.3), calls=%async_computation.1 | async-start | bytes 3145728 | tf_op jit(solution)/shard_map/all_to_all | solution.py:481
  244.9 7.7 %collective-permute-start.34 = (bf16[16,2944]{1,0:T(8,128)(2,1)S(1)}, bf16[16,2944]{1,0:T(8,128)(2,1)S(1)}, u32[]{:S(2)}, u32[]{:S(2)}) collective-permute-start(bf16[16,2944]{1,0:T(8,128)(2,1)S(1)} %pad_maximum_fusion.3), channel_id=1, source_target_pairs={{0,24},{8,16},{16,8},{24,0},{1,25},{9,17},{17,9},{25,1},{2,26},{10... | collective-permute-start | bytes 282632 | tf_op jit(solution)/shard_map/ppermute | solution.py:19
  (64 other events, 573.9 us)

commit v4 on v3

--- a/solution.py
+++ b/solution.py
@@ -11,7 +11,7 @@
 f32 = jnp.float32
 bf16 = jnp.bfloat16
 highest = lax.Precision.HIGHEST
-vmem_limit = 50 * 1024 * 1024
+vmem_limit = 52 * 1024 * 1024
 lanes = 128
 
 
@@ -131,32 +131,6 @@
         for k in range(groups):
             yield copy(parts.at[k, :, pl.ds(depth, half)], tag_parts.at[k], tag_sems.at[k])
 
-    def work(first):
-        x = x_scratch[lax.rem(step, 2)]
-        added[...] = adapter_scale * dot(low_rank[...], adapter_part[...], 1, 0)
-        for chunk in range(chunks):
-            if first:
-                wait(weight_copies(chunk))
-            columns = slice(chunk * width, (chunk + 1) * width)
-            both = dot(x, weight[chunk], 1, 0)
-            gate_acc = both[:, :width]
-            act = gate_acc / (1.0 + jnp.exp(-gate_acc))
-            activated[:, columns] = act.astype(bf16)
-            hidden[:, columns] = (act * (both[:, width:] + added[:, columns])).astype(bf16)
-        if first:
-            wait(tag_copies())
-            summed = jnp.sum(tag_parts[...].astype(f32), axis=0).astype(bf16)
-            for chunk in range(chunks):
-                columns = slice(chunk * width, (chunk + 1) * width)
-                tag_down[:half, columns] = summed[chunk, :, :width]
-                tag_down[half:, columns] = summed[chunk, :, width:]
-        slot_logits[...] = jnp.zeros_like(slot_logits)
-        logits = dot(tag_down[...], hidden[...], 1, 1).astype(bf16)
-        for piece in range(x.shape[0] // capacity):
-            slot_logits[:, piece * lanes : piece * lanes + capacity] = logits[
-                :, piece * capacity : (piece + 1) * capacity
-            ]
-
     @pl.when(step == 0)
     def _():
         start_rows(place, own, other, x_scratch, x_sems, step, per_block)
@@ -168,9 +142,33 @@
     def _():
         start_rows(place, own, other, x_scratch, x_sems, step + 1, per_block)
 
+    @pl.when(step == 0)
+    def _():
+        for chunk in range(chunks):
+            wait(weight_copies(chunk))
+        wait(tag_copies())
+        summed = jnp.sum(tag_parts[...].astype(f32), axis=0).astype(bf16)
+        for chunk in range(chunks):
+            columns = slice(chunk * width, (chunk + 1) * width)
+            tag_down[:half, columns] = summed[chunk, :, :width]
+            tag_down[half:, columns] = summed[chunk, :, width:]
+
+    added[...] = adapter_scale * dot(low_rank[...], adapter_part[...], 1, 0)
     wait_rows(place, own, other, x_scratch, x_sems, step, per_block)
-    pl.when(step == 0)(lambda: work(True))
-    pl.when(step > 0)(lambda: work(False))
+    slot = lax.rem(step, 2)
+    for chunk in range(chunks):
+        columns = slice(chunk * width, (chunk + 1) * width)
+        both = dot(x_scratch[slot], weight[chunk], 1, 0)
+        gate_acc = both[:, :width]
+        act = gate_acc / (1.0 + jnp.exp(-gate_acc))
+        activated[:, columns] = act.astype(bf16)
+        hidden[:, columns] = (act * (both[:, width:] + added[:, columns])).astype(bf16)
+    slot_logits[...] = jnp.zeros_like(slot_logits)
+    logits = dot(tag_down[...], hidden[...], 1, 1).astype(bf16)
+    for piece in range(logits.shape[1] // capacity):
+        slot_logits[:, piece * lanes : piece * lanes + capacity] = logits[
+            :, piece * capacity : (piece + 1) * capacity
+        ]
 
 
 def forward(place, own, other, parts, low_rank, adapter_part, tags, rows, capacity):
@@ -238,55 +236,84 @@
             pl.when(source // half == side)(getattr(copy, act))
 
 
+def column_chunks(count):
+    size = min(count, 2 * lanes)
+    return [slice(at, at + size) for at in range(0, count, size)]
+
+
 def other_kernel(groups, place, hidden, *refs):
-    downs, (out, weight, sems) = refs[:-3], refs[-3:]
-    pl.when(pl.program_id(0) == 0)(lambda: fetch_down(groups, place, downs, weight, sems, 1 - place[1]))
-    out[...] = dot(hidden[...], weight[...], 1, 0).astype(bf16)
+    downs, outs, (weight, sems) = refs[:groups], refs[groups:-2], refs[-2:]
+    step, steps = pl.program_id(0), pl.num_programs(0)
+    pl.when(step == 0)(lambda: fetch_down(groups, place, downs, weight, sems, 1 - place[1]))
+    for out, ref in enumerate(outs):
+
+        @pl.when(step // (steps // len(outs)) == out)
+        def _():
+            for columns in column_chunks(ref.shape[1]):
+                ref[:, columns] = dot(hidden[...], weight[:, columns], 1, 0).astype(bf16)
 
 
 def own_kernel(groups, capacity, place, hidden, *refs):
-    downs, (came, out, weight, sems) = refs[:-4], refs[-4:]
+    downs, (came, out, weight, sems) = refs[:groups], refs[groups:]
     step = pl.program_id(0)
     pl.when(step == 0)(lambda: fetch_down(groups, place, downs, weight, sems, place[1]))
-    value = (dot(hidden[...], weight[...], 1, 0) + came[...].astype(f32)).astype(bf16)
-    per_step = value.shape[0] // capacity
-    for piece in range(out.shape[1] // capacity * groups):
-        block, k = divmod(piece, groups)
-        at = piece % per_step
-
-        @pl.when(step == piece // per_step)
-        def _():
-            out[place[0] ^ k, block * capacity : (block + 1) * capacity] = value[
-                at * capacity : (at + 1) * capacity
+    per_step = hidden.shape[0] // capacity
+    per_block = groups // per_step
+    row = pl.ds(pl.multiple_of(step // per_block * capacity, capacity), capacity)
+    for columns in column_chunks(out.shape[2]):
+        value = (dot(hidden[...], weight[:, columns], 1, 0) + came[:, columns].astype(f32)).astype(bf16)
+        for piece in range(per_step):
+            k = lax.rem(step, per_block) * per_step + piece
+            out[place[0] ^ k, row, columns] = value[piece * capacity : (piece + 1) * capacity]
+
+
+def chunk_block(first, count, step, place):
+    return jnp.clip(step - first, 0, count - 1), 0
+
+
+def down_other(place, hidden, groups, rows, downs, chunks):
+    slots, (width, part) = hidden.shape[0], downs[0].shape
+    share = part * groups // 2
+    half = slots // chunks // rows
+    return pl.pallas_call(
+        functools.partial(other_kernel, groups),
+        out_shape=[jax.ShapeDtypeStruct((slots // chunks, share), bf16)] * chunks,
+        grid_spec=pltpu.PrefetchScalarGridSpec(
+            num_scalar_prefetch=1,
+            grid=(slots // rows,),
+            in_specs=[
+                pl.BlockSpec((rows, width), lambda i, place: ((chunks - 1 - i // half) * half + lax.rem(i, half), 0))
             ]
-
-
-def down(place, hidden, groups, first, count, rows, downs, came, capacity):
-    width, part = downs[0].shape[-2:]
-    share = part * groups // 2
-    if came is None:
-        out_shape = jax.ShapeDtypeStruct((count, share), bf16)
-        out_specs = pl.BlockSpec((rows, share), lambda i, place: (i, 0))
-        kernel = functools.partial(other_kernel, groups)
-    else:
-        out_shape = jax.ShapeDtypeStruct((groups, count // groups, share), bf16)
-        out_specs = pl.BlockSpec((groups, count // groups, share), lambda i, place: (0, 0, 0))
-        kernel = functools.partial(own_kernel, groups, capacity)
+            + [pl.BlockSpec(memory_space=pl.ANY)] * groups,
+            out_specs=[
+                pl.BlockSpec((rows, share), functools.partial(chunk_block, chunk * half, half)) for chunk in range(chunks)
+            ],
+            scratch_shapes=[pltpu.VMEM((width, share), bf16), pltpu.SemaphoreType.DMA((groups,))],
+        ),
+        compiler_params=pltpu.CompilerParams(vmem_limit_bytes=62 * 1024 * 1024),
+        name="down_other",
+    )(place, hidden, *downs)
+
+
+def down_own(place, hidden, groups, first, rows, downs, came, capacity):
+    count, share = came.shape
+    width = hidden.shape[1]
+    shape = (groups, count // groups, share)
     return pl.pallas_call(
-        kernel,
-        out_shape=out_shape,
+        functools.partial(own_kernel, groups, capacity),
+        out_shape=jax.ShapeDtypeStruct(shape, bf16),
         grid_spec=pltpu.PrefetchScalarGridSpec(
             num_scalar_prefetch=1,
             grid=(count // rows,),
             in_specs=[pl.BlockSpec((rows, width), lambda i, place: (first // rows + i, 0))]
-            + [pl.BlockSpec(memory_space=pl.ANY)] * len(downs)
-            + ([] if came is None else [pl.BlockSpec((rows, share), lambda i, place: (i, 0))]),
-            out_specs=out_specs,
+            + [pl.BlockSpec(memory_space=pl.ANY)] * groups
+            + [pl.BlockSpec((rows, share), lambda i, place: (i, 0))],
+            out_specs=pl.BlockSpec(shape, lambda i, place: (0, 0, 0)),
             scratch_shapes=[pltpu.VMEM((width, share), bf16), pltpu.SemaphoreType.DMA((groups,))],
         ),
-        compiler_params=pltpu.CompilerParams(vmem_limit_bytes=vmem_limit),
-        name="down_other" if came is None else "down_own",
-    )(place, hidden, *downs, *([] if came is None else [came]))
+        compiler_params=pltpu.CompilerParams(vmem_limit_bytes=62 * 1024 * 1024),
+        name="down_own",
+    )(place, hidden, *downs, came)
 
 
 def pack_kernel(place, gate, up, down, tag_part, out):
@@ -395,6 +422,40 @@
         compiler_params=pltpu.CompilerParams(vmem_limit_bytes=vmem_limit),
         name="adapter_grad",
     )(place, *own, *other, *slot_grad, tag_down, activated, low_rank, adapter_part)
+
+
+def finish_kernel(place, *refs):
+    both, (in_total, out_total) = refs[:-2], refs[-2:]
+    width = in_total.shape[1]
+    in_total[...] = total([ref[:, :width] for ref in both])
+    part = both[0].shape[1] - width
+    for k, ref in enumerate(both):
+        column = pl.multiple_of((place[0] ^ k) * part, part)
+        out_total[:, pl.ds(column, part)] = ref[:, width:].astype(f32)
+
+
+def finish(place, both, width):
+    rank, part, groups = both[0].shape[0], both[0].shape[1] - width, len(both)
+    if part % lanes:
+        out_total = jnp.zeros((rank, groups * part), f32)
+        for k, value in enumerate(both):
+            value = value[:, width:].astype(f32)
+            out_total = lax.dynamic_update_slice_in_dim(out_total, value, (place[0] ^ k) * part, 1)
+        return total([value[:, :width] for value in both]), out_total
+    whole = lambda shape: pl.BlockSpec(shape, lambda i, place: (0, 0))
+    shapes = (rank, width), (rank, groups * part)
+    return pl.pallas_call(
+        finish_kernel,
+        out_shape=[jax.ShapeDtypeStruct(shape, f32) for shape in shapes],
+        grid_spec=pltpu.PrefetchScalarGridSpec(
+            num_scalar_prefetch=1,
+            grid=(1,),
+            in_specs=[whole(value.shape) for value in both],
+            out_specs=[whole(shape) for shape in shapes],
+        ),
+        compiler_params=pltpu.CompilerParams(vmem_limit_bytes=vmem_limit),
+        name="finish",
+    )(place, *both)
 
 
 def local(
@@ -453,7 +514,8 @@
     x_own = swap(x_own, "expert")
     x_other = [send(value, "tensor", 1) for value in x_own]
     low_rank = low(place, x_own, x_other, adapter_in[0], rows)
-    parts = after(parts, low_rank)
+    token_logits = dot(tag_weight, tokens, 0, 1)
+    parts = after(parts, low_rank, combine, token_logits)
     downs = swap([after(piece, parts) for piece in downs], "dp")
     adapter_part = lax.dynamic_slice_in_dim(adapter_out[0], dp * hidden_part, hidden_part, 1)
 
@@ -466,54 +528,58 @@
     pieces = [slot_logits[:, j * plane_lanes : (j + 1) * plane_lanes] for j in range(experts)]
     pieces = swap(pieces, "expert")
 
-    chunks = [(experts // 2, experts // 2), (0, experts // 2)]
-
-    def product(chunk, came):
-        first, count = chunks[chunk]
-        return down(place, hidden, groups, first * block_rows, count * block_rows, rows, downs, came, capacity)
-
     hidden = after(hidden, *pieces)
-    others, mine = [], []
-    for chunk in range(len(chunks)):
-        others.append(send(product(chunk, None), "tensor", 1))
-        mine.append(product(chunk, others[chunk]))
-        hidden = after(hidden, mine[chunk])
-    came = [lax.all_to_all(part, "dp", split_axis=0, concat_axis=0, tiled=True) for part in mine]
     pieces = [
         jnp.concatenate([piece[:, k * lanes : (k + 1) * lanes] for piece in pieces], axis=1) for k in range(groups)
     ]
     pieces = swap(pieces, "dp")
+
+    chunks = [(experts // 2, experts // 2), (0, experts // 2)]
+
+    def own(chunk, came):
+        return down_own(place, hidden, groups, chunks[chunk][0] * block_rows, rows, downs, came, capacity)
+
+    def change(part):
+        return lax.all_to_all(part, "dp", split_axis=0, concat_axis=0, tiled=True)
+
+    others = down_other(place, hidden, groups, rows, downs, len(chunks))
+    others = [send(other, "tensor", 1) for other in others]
+    first = own(0, after(others[0], *pieces))
+
+    pieces[0] = after(pieces[0], first)
     slot_grad = pl.pallas_call(
         functools.partial(tag_kernel, groups),
         out_shape=jax.ShapeDtypeStruct((tags, experts * lanes), bf16),
         compiler_params=pltpu.CompilerParams(vmem_limit_bytes=vmem_limit),
         name="tag_grad",
-    )(*pieces, dot(tag_weight, tokens, 0, 1), combine, tag_labels[None, :])
-    slot_grad = after(slot_grad, mine[-1])
+    )(*pieces, token_logits, combine, tag_labels[None, :])
     slot_grad = swap([slot_grad[:, j * lanes : (j + 1) * lanes] for j in range(experts)], "expert")
+    second = own(1, after(others[1], *slot_grad))
+    slot_grad[0] = after(slot_grad[0], second)
     slot_grad = gather(jnp.concatenate(slot_grad, axis=1), "dp")
-
-    tag_down = after(tag_down, came[0])
+    came = [change(first), change(after(second, *slot_grad[1:]))]
+
+    sums = [jnp.sum(came[0].astype(f32), axis=0).astype(bf16)]
+    slot_grad[0] = after(slot_grad[0], sums[0])
     out_local, in_local = backward(
         place, x_own, x_other, slot_grad, tag_down, activated, low_rank, adapter_part, rows, capacity
     )
+    returned = [None] * experts
+
+    def give_back(chunk):
+        first, count = chunks[chunk]
+        for j in range(first, first + count):
+            kept = sums[chunk][(j - first) * capacity : (j - first + 1) * capacity]
+            returned[j] = send(kept, "expert", j) if j else kept
+
+    give_back(0)
+    in_local = after(in_local, *returned[chunks[0][0] :])
     in_local = in_local + send(in_local.astype(bf16), "tensor", 1).astype(f32)
     both = gather(jnp.concatenate([in_local, out_local], axis=1).astype(bf16), "dp")
-    in_total = total([value[:, :model_width] for value in both])
-    out_total = jnp.zeros((rank, groups * hidden_part), f32)
-    for k, value in enumerate(both):
-        out_total = lax.dynamic_update_slice_in_dim(
-            out_total, value[:, model_width:].astype(f32), (dp ^ k) * hidden_part, 1
-        )
-
-    returned = [None] * experts
-    for (first, count), value in zip(chunks, came):
-        if first == 0:
-            value = after(value, *returned[count:])
-        value = jnp.sum(value.astype(f32), axis=0).astype(bf16)
-        for j in range(first, first + count):
-            kept = value[(j - first) * capacity : (j - first + 1) * capacity]
-            returned[j] = send(kept, "expert", j) if j else kept
+    sums.append(jnp.sum(came[1].astype(f32), axis=0).astype(bf16))
+    give_back(1)
+    both[0] = after(both[0], sums[-1])
+    in_total, out_total = finish(place, both, model_width)
     layer_out = token_half.astype(f32)
     for j in range(experts):
         kept = combine[j * lanes : j * lanes + capacity]

time: 264 us -> 242 us (0.917)
  local copies, waits for them, and re-layouts: 29.3 us -> 8.21 us
  waiting for transfers between devices: 94.8 us -> 99.3 us
    unnamed x101 -> x26, local copies, waits for them, and re-layouts: 21.2 us -> 1.43 us
    all_to_all x1, waiting for transfers between devices: 8.32 us -> 12.6 us  [local(): lax.all_to_all(after(parts, *plane_parts), 'dp', split_axis=0, concat_axi...]
    pallas_call x4, Pallas kernels: 21 us -> 24 us  [the longest x2 13.8 us: down_own(): pl.pallas_call(functools.partial(own_kernel, groups, capacity), out_shape...]
    all_to_all x2, waiting for transfers between devices: 0.01 us -> 2.81 us  [change(): return lax.all_to_all(part, 'dp', split_axis=0, concat_axis=0, tiled=True)]
    ppermute x35, starting transfers between devices: 44.3 us -> 41.6 us  [send(): lax.ppermute(value, axis, [(i, i ^ step) for i in range(lax.axis_size(axi...]
    ppermute x35, waiting for transfers between devices: 86.5 us -> 83.8 us  [send(): lax.ppermute(value, axis, [(i, i ^ step) for i in range(lax.axis_size(axi...]
  transfers between devices with their start and end apart: 38 -> 38, of which waited for: 17 -> 26; matrix products, arithmetic and copies ran while one was open for 7% -> 7% of each run, Pallas kernels for 21% -> 24%
where the time goes in v4:
time: 242 us; the launch traced here: 241 us
  waiting for transfers between devices  99.3 us (41%)
  Pallas kernels  66.8 us (28%)
  starting transfers between devices  56 us (23%)
  local copies, waits for them, and re-layouts  8.21 us (3%)
  other arithmetic  4.7 us (2%)
  matrix products  4.52 us (2%)
    ppermute x35, waiting for transfers between devices, send(): lax.ppermute(value, axis, [(i, i ^ step) for i in range(lax.axis_size(axi...  83.8 us
    ppermute x35, starting transfers between devices, send(): lax.ppermute(value, axis, [(i, i ^ step) for i in range(lax.axis_size(axi...  41.6 us
    pallas_call x1, Pallas kernels, forward(): pl.pallas_call(functools.partial(forward_kernel, experts, block_rows // r...  21.7 us
    pallas_call x2, Pallas kernels, down_own(): pl.pallas_call(functools.partial(own_kernel, groups, capacity), out_shape...  13.8 us
    all_to_all x1, waiting for transfers between devices, local(): lax.all_to_all(after(parts, *plane_parts), 'dp', split_axis=0, concat_axi...  12.6 us
    pallas_call x1, Pallas kernels, down_other(): pl.pallas_call(functools.partial(other_kernel, groups), out_shape=[jax.Sh...  8.9 us
    all_to_all x2, starting transfers between devices, change(): return lax.all_to_all(part, 'dp', split_axis=0, concat_axis=0, tiled=True)  8.87 us
    pallas_call x1, Pallas kernels, pack(): pl.pallas_call(pack_kernel, out_shape=jax.ShapeDtypeStruct((groups, part...  8.69 us
  transfers between devices with their start and end apart: 38, of which 26 were waited for; matrix products, arithmetic and copies ran while one was open for 7% of the time, Pallas kernels for 24%

profile of v4, /device:TPU:0, one launch (start us, length us, event | category | flops | bytes accessed | tf_op | source)
XLA Modules:
  0.0 240.6 jit_solution(980550702941754944)
XLA Ops:
  1.8 4.0 %collective-permute-start.2 = (bf16[136,1024]{1,0:T(8,128)(2,1)S(1)}, bf16[136,1024]{1,0:T(8,128)(2,1)S(1)}, u32[]{:S(2)}, u32[]{:S(2)}) collective-permute-start(bf16[136,1024]{1,0:T(8,128)(2,1)S(1)} %get-tuple-element.62), channel_id=1, source_target_pairs={{0,24},{8,16},{16,8},{24,0},{1,25},{9,17},{17,9},{25,1},{2,26},{10... | collective-permute-start | bytes 835592 | tf_op jit(solution)/shard_map/ppermute | solution.py:19
  7.7 8.7 %pack.1 = bf16[4,7,528,256]{3,2,1,0:T(8,128)(2,1)} custom-call(s32[2]{0:T(128)S(1)} %pad_add_fusion.place, bf16[512,3584]{1,0:T(8,128)(2,1)} %bitcast.60, bf16[512,3584]{1,0:T(8,128)(2,1)} %bitcast.61, bf16[3584,512]{1,0:T(8,128)(2,1)} %bitcast.59, bf16[2048,32]{1,0:T(8,128)(2,1)S(1)} %copy.16.tag_part), custom_call_target="tpu_custom_call" | custom-call | tf_op jit(solution)/shard_map/pack/pallas_call | solution.py:340
  18.7 5.5 %all-to-all-start = ((bf16[4,7,528,256]{3,2,1,0:T(8,128)(2,1)}), bf16[4,7,528,256]{3,2,1,0:T(8,128)(2,1)}, u32[]{:S(2)}, u32[]{:S(2)}) async-start(bf16[4,7,528,256]{3,2,1,0:T(8,128)(2,1)} %pack.1), calls=%async_computation | async-start | bytes 15138816 | tf_op jit(solution)/shard_map/all_to_all | solution.py:507
  24.2 4.0 %dynamic-slice_bitcast_fusion = (bf16[896,512]{1,0:T(8,128)(2,1)}, bf16[896,512]{1,0:T(8,128)(2,1)}, bf16[896,512]{1,0:T(8,128)(2,1)}, bf16[896,512]{1,0:T(8,128)(2,1)}) fusion(bf16[1,3584,512]{2,1,0:T(8,128)(2,1)} %param.16, s32[]{:T(128)S(6)} %select_n.57, s32[]{:T(128)S(6)} %select_n.55, s32[]{:T(128)S(6)} %select_n.54, s32[]{:T(128)S(6)} %select_n.56), kind=kLoop, calls=%fused_computation.15 | loop fusion | bytes 7340048 | tf_op jit(solution)/shard_map/dynamic_slice | solution.py:505
  31.4 2.6 %collective-permute-start.4 = (bf16[384,1024]{1,0:T(8,128)(2,1)S(1)}, bf16[384,1024]{1,0:T(8,128)(2,1)}, u32[]{:S(2)}, u32[]{:S(2)}) collective-permute-start(bf16[384,1024]{1,0:T(8,128)(2,1)S(1)} %bitcast.69), channel_id=1, source_target_pairs={{0,4},{2,6},{4,0},{6,2},{1,5},{3,7},{5,1},{7,3},{8,12},{10,14},{12... | collective-permute-start | bytes 2359304 | tf_op jit(solution)/shard_map/ppermute | solution.py:19
  34.7 30.6 %collective-permute-done.3.refs_1_ = bf16[384,1024]{1,0:T(8,128)(2,1)} collective-permute-done((bf16[384,1024]{1,0:T(8,128)(2,1)S(1)}, bf16[384,1024]{1,0:T(8,128)(2,1)}, u32[]{:S(2)}, u32[]{:S(2)}) %collective-permute-start.3) | collective-permute-done | bytes 786464 | tf_op jit(solution)/shard_map/ppermute | solution.py:19
  65.2 21.3 %collective-permute-done.4.refs_2_ = bf16[384,1024]{1,0:T(8,128)(2,1)} collective-permute-done((bf16[384,1024]{1,0:T(8,128)(2,1)S(1)}, bf16[384,1024]{1,0:T(8,128)(2,1)}, u32[]{:S(2)}, u32[]{:S(2)}) %collective-permute-start.4) | collective-permute-done | bytes 786464 | tf_op jit(solution)/shard_map/ppermute | solution.py:19
  90.3 5.0 %low_rank.1.refs_8_.refs_14_ = bf16[1536,16]{1,0:T(8,128)(2,1)S(1)} custom-call(s32[2]{0:T(128)S(1)} %pad_add_fusion.place, bf16[384,1024]{1,0:T(8,128)(2,1)S(1)} %bitcast.54, bf16[384,1024]{1,0:T(8,128)(2,1)} %collective-permute-done.3.refs_1_, bf16[384,1024]{1,0:T(8,128)(2,1)} %collective-permute-done.4.refs_2_, ...), custom_call_target="tpu_custom_call" | custom-call | tf_op jit(solution)/shard_map/low_rank/pallas_call | solution.py:98
  95.3 12.6 %all-to-all-done.refs_10_ = bf16[4,7,528,256]{3,2,1,0:T(8,128)(2,1)} async-done(((bf16[4,7,528,256]{3,2,1,0:T(8,128)(2,1)}), bf16[4,7,528,256]{3,2,1,0:T(8,128)(2,1)}, u32[]{:S(2)}, u32[]{:S(2)}) %all-to-all-start) | async-done | bytes 7569440 | tf_op jit(solution)/shard_map/all_to_all | solution.py:507
  112.2 21.7 %gate_up.1 = (bf16[1536,896]{1,0:T(8,128)(2,1)}, bf16[1536,896]{1,0:T(8,128)(2,1)}, bf16[32,2048]{1,0:T(8,128)(2,1)S(1)}, bf16[32,896]{1,0:T(8,128)(2,1)S(1)}) custom-call(s32[2]{0:T(128)S(1)} %pad_add_fusion.place, bf16[384,1024]{1,0:T(8,128)(2,1)S(1)} %bitcast.55, bf16[384,1024]{1,0:T(8,128)(2,1)} %collective-permute-done.3.refs_1_, ...), custom_call_target="tpu_custom_call" | custom-call | tf_op jit(solution)/shard_map/gate_up/pallas_call | solution.py:184
  135.3 3.9 %collective-permute-start.13 = (bf16[32,512]{1,0:T(8,128)(2,1)S(1)}, bf16[32,512]{1,0:T(8,128)(2,1)S(1)}, u32[]{:S(2)}, u32[]{:S(2)}) collective-permute-start(bf16[32,512]{1,0:T(8,128)(2,1)S(1)} %get-tuple-element.67), channel_id=1, source_target_pairs={{0,6},{2,4},{4,2},{6,0},{1,7},{3,5},{5,3},{7,1},{8,14},{10,12},{12... | collective-permute-start | bytes 98312 | tf_op jit(solution)/shard_map/ppermute | solution.py:19
  145.1 5.1 %collective-permute-done.15.refs_2_ = bf16[896,512]{1,0:T(8,128)(2,1)} collective-permute-done((bf16[896,512]{1,0:T(8,128)(2,1)}, bf16[896,512]{1,0:T(8,128)(2,1)}, u32[]{:S(2)}, u32[]{:S(2)}) %collective-permute-start.15) | collective-permute-done | bytes 917536 | tf_op jit(solution)/shard_map/ppermute | solution.py:19
  150.1 8.9 %down_other.1 = (bf16[768,1024]{1,0:T(8,128)(2,1)}, bf16[768,1024]{1,0:T(8,128)(2,1)}) custom-call(s32[2]{0:T(128)} %copy-done.3, bf16[1536,896]{1,0:T(8,128)(2,1)} %get-tuple-element.34.hidden, bf16[896,512]{1,0:T(8,128)(2,1)} %get-tuple-element.35.refs_0_, bf16[896,512]{1,0:T(8,128)(2,1)} %collective-permute-done.14.refs_1_, ...), custom_call_target="tpu_custom_call" | custom-call | tf_op jit(solution)/shard_map/down_other/pallas_call | solution.py:278
  167.4 6.9 %down_own.2 = bf16[4,192,1024]{2,1,0:T(8,128)(2,1)} custom-call(s32[2]{0:T(128)} %copy-done.3, bf16[1536,896]{1,0:T(8,128)(2,1)} %get-tuple-element.34.hidden, bf16[896,512]{1,0:T(8,128)(2,1)} %get-tuple-element.35.refs_0_, bf16[896,512]{1,0:T(8,128)(2,1)} %collective-permute-done.14.refs_1_, bf16[896,512]{1,0:T(8,128)(2,1)} %collective-permute-done.15.refs_2_, ...), custom_call_target="tpu_custom_call" | custom-call | tf_op jit(solution)/shard_map/down_own/pallas_call | solution.py:302
  174.3 4.5 %all-to-all-start.2 = ((bf16[4,192,1024]{2,1,0:T(8,128)(2,1)}), bf16[4,192,1024]{2,1,0:T(8,128)(2,1)}, u32[]{:S(2)}, u32[]{:S(2)}) async-start(bf16[4,192,1024]{2,1,0:T(8,128)(2,1)} %down_own.2), calls=%async_computation.2 | async-start | bytes 3145728 | tf_op jit(solution)/shard_map/all_to_all | solution.py:543
  179.5 4.1 %collective-permute-start.24 = (bf16[32,128]{1,0:T(8,128)(2,1)S(1)}, bf16[32,128]{1,0:T(8,128)(2,1)S(1)}, u32[]{:S(2)}, u32[]{:S(2)}) collective-permute-start(bf16[32,128]{1,0:T(8,128)(2,1)S(1)} %get-tuple-element.70), channel_id=1, source_target_pairs={{0,6},{2,4},{4,2},{6,0},{1,7},{3,5},{5,3},{7,1},{8,14},{10,12},{12... | collective-permute-start | bytes 24584 | tf_op jit(solution)/shard_map/ppermute | solution.py:19
  185.4 2.8 %collective-permute-done.23 = bf16[32,128]{1,0:T(8,128)(2,1)S(1)} collective-permute-done((bf16[32,128]{1,0:T(8,128)(2,1)S(1)}, bf16[32,128]{1,0:T(8,128)(2,1)S(1)}, u32[]{:S(2)}, u32[]{:S(2)}) %collective-permute-start.23) | collective-permute-done | bytes 8224 | tf_op jit(solution)/shard_map/ppermute | solution.py:19
  188.9 6.9 %down_own.3 = bf16[4,192,1024]{2,1,0:T(8,128)(2,1)} custom-call(s32[2]{0:T(128)} %copy-done.3, bf16[1536,896]{1,0:T(8,128)(2,1)} %get-tuple-element.34.hidden, bf16[896,512]{1,0:T(8,128)(2,1)} %get-tuple-element.35.refs_0_, bf16[896,512]{1,0:T(8,128)(2,1)} %collective-permute-done.14.refs_1_, bf16[896,512]{1,0:T(8,128)(2,1)} %collective-permute-done.15.refs_2_, ...), custom_call_target="tpu_custom_call" | custom-call | tf_op jit(solution)/shard_map/down_own/pallas_call | solution.py:302
  195.8 2.8 %collective-permute-start.27 = (bf16[32,512]{1,0:T(8,128)(2,1)S(1)}, bf16[32,512]{1,0:T(8,128)(2,1)S(1)}, u32[]{:S(2)}, u32[]{:S(2)}) collective-permute-start(bf16[32,512]{1,0:T(8,128)(2,1)S(1)} %constant_dynamic-update-slice_fusion.refs_8_), channel_id=1, source_target_pairs={{0,24},{8,16},{16,8},{24,0},{1,25},{9,17},{17,9},{25,1},{2,26},{10... | collective-permute-start | bytes 98312 | tf_op jit(solution)/shard_map/ppermute | solution.py:19
  203.1 4.3 %all-to-all-start.1 = ((bf16[4,192,1024]{2,1,0:T(8,128)(2,1)}), bf16[4,192,1024]{2,1,0:T(8,128)(2,1)}, u32[]{:S(2)}, u32[]{:S(2)}) async-start(bf16[4,192,1024]{2,1,0:T(8,128)(2,1)} %down_own.3), calls=%async_computation.1 | async-start | bytes 3145728 | tf_op jit(solution)/shard_map/all_to_all | solution.py:543
  209.2 6.9 %adapter_grad.1 = (f32[16,896]{1,0:T(8,128)S(1)}, f32[16,2048]{1,0:T(8,128)S(1)}) custom-call(s32[2]{0:T(128)S(1)} %copy-done.4, bf16[384,1024]{1,0:T(8,128)(2,1)S(1)} %bitcast.56, bf16[384,1024]{1,0:T(8,128)(2,1)} %collective-permute-done.3.refs_1_, bf16[384,1024]{1,0:T(8,128)(2,1)} %collective-permute-done.4.refs_2_, ...), custom_call_target="tpu_custom_call" | custom-call | tf_op jit(solution)/shard_map/adapter_grad/pallas_call | solution.py:398
  219.5 2.8 %all-to-all-done.1 = bf16[4,192,1024]{2,1,0:T(8,128)(2,1)} async-done(((bf16[4,192,1024]{2,1,0:T(8,128)(2,1)}), bf16[4,192,1024]{2,1,0:T(8,128)(2,1)}, u32[]{:S(2)}, u32[]{:S(2)}) %all-to-all-start.1) | async-done | bytes 1572896 | tf_op jit(solution)/shard_map/all_to_all | solution.py:543
  224.1 3.0 %collective-permute-start.28 = (bf16[96,1024]{1,0:T(8,128)(2,1)S(1)}, bf16[96,1024]{1,0:T(8,128)(2,1)S(1)}, u32[]{:S(2)}, u32[]{:S(2)}) collective-permute-start(bf16[96,1024]{1,0:T(8,128)(2,1)S(1)} %slice.180), channel_id=1, source_target_pairs={{0,2},{2,0},{4,6},{6,4},{1,3},{3,1},{5,7},{7,5},{8,10},{10,8},{12,... | collective-permute-start | bytes 589832 | tf_op jit(solution)/shard_map/ppermute | solution.py:19
  231.3 2.7 %collective-permute-start.34 = (bf16[16,2944]{1,0:T(8,128)(2,1)S(1)}, bf16[16,2944]{1,0:T(8,128)(2,1)S(1)}, u32[]{:S(2)}, u32[]{:S(2)}) collective-permute-start(bf16[16,2944]{1,0:T(8,128)(2,1)S(1)} %pad_maximum_fusion.3.refs_0_), channel_id=1, source_target_pairs={{0,24},{8,16},{16,8},{24,0},{1,25},{9,17},{17,9},{25,1},{2,26},{10... | collective-permute-start | bytes 282632 | tf_op jit(solution)/shard_map/ppermute | solution.py:19
  (134 shorter events, 58.1 us)
Async XLA Ops:
  1.8 14.6 %collective-permute-start.2 = (bf16[136,1024]{1,0:T(8,128)(2,1)S(1)}, bf16[136,1024]{1,0:T(8,128)(2,1)S(1)}, u32[]{:S(2)}, u32[]{:S(2)}) collective-permute-start(bf16[136,1024]{1,0:T(8,128)(2,1)S(1)} %get-tuple-element.62), channel_id=1, source_target_pairs={{0,24},{8,16},{16,8},{24,0},{1,25},{9,17},{17,9},{25,1},{2,26},{10... | collective-permute-start | bytes 835592 | tf_op jit(solution)/shard_map/ppermute | solution.py:19
  5.7 12.6 %collective-permute-start.1 = (bf16[136,1024]{1,0:T(8,128)(2,1)S(1)}, bf16[136,1024]{1,0:T(8,128)(2,1)S(1)}, u32[]{:S(2)}, u32[]{:S(2)}) collective-permute-start(bf16[136,1024]{1,0:T(8,128)(2,1)S(1)} %get-tuple-element.62), channel_id=1, source_target_pairs={{0,16},{8,24},{16,0},{24,8},{1,17},{9,25},{17,1},{25,9},{2,18},{10... | collective-permute-start | bytes 835592 | tf_op jit(solution)/shard_map/ppermute | solution.py:19
  6.2 12.4 %collective-permute-start = (bf16[136,1024]{1,0:T(8,128)(2,1)S(1)}, bf16[136,1024]{1,0:T(8,128)(2,1)S(1)}, u32[]{:S(2)}, u32[]{:S(2)}) collective-permute-start(bf16[136,1024]{1,0:T(8,128)(2,1)S(1)} %get-tuple-element.62), channel_id=1, source_target_pairs={{0,8},{8,0},{16,24},{24,16},{1,9},{9,1},{17,25},{25,17},{2,10},{10... | collective-permute-start | bytes 835592 | tf_op jit(solution)/shard_map/ppermute | solution.py:19
  18.7 89.3 %all-to-all-start = ((bf16[4,7,528,256]{3,2,1,0:T(8,128)(2,1)}), bf16[4,7,528,256]{3,2,1,0:T(8,128)(2,1)}, u32[]{:S(2)}, u32[]{:S(2)}) async-start(bf16[4,7,528,256]{3,2,1,0:T(8,128)(2,1)} %pack.1), calls=%async_computation | async-start | bytes 15138816 | tf_op jit(solution)/shard_map/all_to_all | solution.py:507
  29.7 35.5 %collective-permute-start.3 = (bf16[384,1024]{1,0:T(8,128)(2,1)S(1)}, bf16[384,1024]{1,0:T(8,128)(2,1)}, u32[]{:S(2)}, u32[]{:S(2)}) collective-permute-start(bf16[384,1024]{1,0:T(8,128)(2,1)S(1)} %bitcast.70), channel_id=1, source_target_pairs={{0,2},{2,0},{4,6},{6,4},{1,3},{3,1},{5,7},{7,5},{8,10},{10,8},{12,... | collective-permute-start | bytes 2359304 | tf_op jit(solution)/shard_map/ppermute | solution.py:19
  31.4 55.2 %collective-permute-start.4 = (bf16[384,1024]{1,0:T(8,128)(2,1)S(1)}, bf16[384,1024]{1,0:T(8,128)(2,1)}, u32[]{:S(2)}, u32[]{:S(2)}) collective-permute-start(bf16[384,1024]{1,0:T(8,128)(2,1)S(1)} %bitcast.69), channel_id=1, source_target_pairs={{0,4},{2,6},{4,0},{6,2},{1,5},{3,7},{5,1},{7,3},{8,12},{10,14},{12... | collective-permute-start | bytes 2359304 | tf_op jit(solution)/shard_map/ppermute | solution.py:19
  33.9 52.6 %collective-permute-start.5 = (bf16[384,1024]{1,0:T(8,128)(2,1)S(1)}, bf16[384,1024]{1,0:T(8,128)(2,1)}, u32[]{:S(2)}, u32[]{:S(2)}) collective-permute-start(bf16[384,1024]{1,0:T(8,128)(2,1)S(1)} %bitcast.68), channel_id=1, source_target_pairs={{0,6},{2,4},{4,2},{6,0},{1,7},{3,5},{5,3},{7,1},{8,14},{10,12},{12... | collective-permute-start | bytes 2359304 | tf_op jit(solution)/shard_map/ppermute | solution.py:19
  34.6 54.1 %collective-permute-start.6 = (bf16[384,1024]{1,0:T(8,128)(2,1)S(1)}, bf16[384,1024]{1,0:T(8,128)(2,1)S(1)}, u32[]{:S(2)}, u32[]{:S(2)}) collective-permute-start(bf16[384,1024]{1,0:T(8,128)(2,1)S(1)} %bitcast.53), channel_id=1, source_target_pairs={{0,1},{1,0},{2,3},{3,2},{4,5},{5,4},{6,7},{7,6},{8,9},{9,8},{10,11... | collective-permute-start | bytes 2359304 | tf_op jit(solution)/shard_map/ppermute | solution.py:19
  65.2 23.5 %collective-permute-start.7 = (bf16[384,1024]{1,0:T(8,128)(2,1)}, bf16[384,1024]{1,0:T(8,128)(2,1)}, u32[]{:S(2)}, u32[]{:S(2)}) collective-permute-start(bf16[384,1024]{1,0:T(8,128)(2,1)} %collective-permute-done.3.refs_1_), channel_id=1, source_target_pairs={{0,1},{1,0},{2,3},{3,2},{4,5},{5,4},{6,7},{7,6},{8,9},{9,8},{10,11... | collective-permute-start | bytes 2359304 | tf_op jit(solution)/shard_map/ppermute | solution.py:19
  107.9 37.1 %collective-permute-start.14 = (bf16[896,512]{1,0:T(8,128)(2,1)}, bf16[896,512]{1,0:T(8,128)(2,1)}, u32[]{:S(2)}, u32[]{:S(2)}) collective-permute-start(bf16[896,512]{1,0:T(8,128)(2,1)} %get-tuple-element.36), channel_id=1, source_target_pairs={{0,8},{8,0},{16,24},{24,16},{1,9},{9,1},{17,25},{25,17},{2,10},{10... | collective-permute-start | bytes 2752520 | tf_op jit(solution)/shard_map/ppermute | solution.py:19
  109.3 40.8 %collective-permute-start.15 = (bf16[896,512]{1,0:T(8,128)(2,1)}, bf16[896,512]{1,0:T(8,128)(2,1)}, u32[]{:S(2)}, u32[]{:S(2)}) collective-permute-start(bf16[896,512]{1,0:T(8,128)(2,1)} %get-tuple-element.37), channel_id=1, source_target_pairs={{0,16},{8,24},{16,0},{24,8},{1,17},{9,25},{17,1},{25,9},{2,18},{10... | collective-permute-start | bytes 2752520 | tf_op jit(solution)/shard_map/ppermute | solution.py:19
  109.9 40.2 %collective-permute-start.16 = (bf16[896,512]{1,0:T(8,128)(2,1)}, bf16[896,512]{1,0:T(8,128)(2,1)}, u32[]{:S(2)}, u32[]{:S(2)}) collective-permute-start(bf16[896,512]{1,0:T(8,128)(2,1)} %get-tuple-element.38), channel_id=1, source_target_pairs={{0,24},{8,16},{16,8},{24,0},{1,25},{9,17},{17,9},{25,1},{2,26},{10... | collective-permute-start | bytes 2752520 | tf_op jit(solution)/shard_map/ppermute | solution.py:19
  135.3 5.8 %collective-permute-start.13 = (bf16[32,512]{1,0:T(8,128)(2,1)S(1)}, bf16[32,512]{1,0:T(8,128)(2,1)S(1)}, u32[]{:S(2)}, u32[]{:S(2)}) collective-permute-start(bf16[32,512]{1,0:T(8,128)(2,1)S(1)} %get-tuple-element.67), channel_id=1, source_target_pairs={{0,6},{2,4},{4,2},{6,0},{1,7},{3,5},{5,3},{7,1},{8,14},{10,12},{12... | collective-permute-start | bytes 98312 | tf_op jit(solution)/shard_map/ppermute | solution.py:19
  159.0 8.4 %collective-permute-start.18 = (bf16[768,1024]{1,0:T(8,128)(2,1)}, bf16[768,1024]{1,0:T(8,128)(2,1)}, u32[]{:S(2)}, u32[]{:S(2)}) collective-permute-start(bf16[768,1024]{1,0:T(8,128)(2,1)} %get-tuple-element.40), channel_id=1, source_target_pairs={{0,1},{1,0},{2,3},{3,2},{4,5},{5,4},{6,7},{7,6},{8,9},{9,8},{10,11... | collective-permute-start | bytes 4718600 | tf_op jit(solution)/shard_map/ppermute | solution.py:19
  159.9 25.4 %collective-permute-start.17 = (bf16[768,1024]{1,0:T(8,128)(2,1)}, bf16[768,1024]{1,0:T(8,128)(2,1)}, u32[]{:S(2)}, u32[]{:S(2)}) collective-permute-start(bf16[768,1024]{1,0:T(8,128)(2,1)} %get-tuple-element.39), channel_id=1, source_target_pairs={{0,1},{1,0},{2,3},{3,2},{4,5},{5,4},{6,7},{7,6},{8,9},{9,8},{10,11... | collective-permute-start | bytes 4718600 | tf_op jit(solution)/shard_map/ppermute | solution.py:19
  174.3 28.7 %all-to-all-start.2 = ((bf16[4,192,1024]{2,1,0:T(8,128)(2,1)}), bf16[4,192,1024]{2,1,0:T(8,128)(2,1)}, u32[]{:S(2)}, u32[]{:S(2)}) async-start(bf16[4,192,1024]{2,1,0:T(8,128)(2,1)} %down_own.2), calls=%async_computation.2 | async-start | bytes 3145728 | tf_op jit(solution)/shard_map/all_to_all | solution.py:543
  179.5 5.8 %collective-permute-start.24 = (bf16[32,128]{1,0:T(8,128)(2,1)S(1)}, bf16[32,128]{1,0:T(8,128)(2,1)S(1)}, u32[]{:S(2)}, u32[]{:S(2)}) collective-permute-start(bf16[32,128]{1,0:T(8,128)(2,1)S(1)} %get-tuple-element.70), channel_id=1, source_target_pairs={{0,6},{2,4},{4,2},{6,0},{1,7},{3,5},{5,3},{7,1},{8,14},{10,12},{12... | collective-permute-start | bytes 24584 | tf_op jit(solution)/shard_map/ppermute | solution.py:19
  195.8 4.9 %collective-permute-start.27 = (bf16[32,512]{1,0:T(8,128)(2,1)S(1)}, bf16[32,512]{1,0:T(8,128)(2,1)S(1)}, u32[]{:S(2)}, u32[]{:S(2)}) collective-permute-start(bf16[32,512]{1,0:T(8,128)(2,1)S(1)} %constant_dynamic-update-slice_fusion.refs_8_), channel_id=1, source_target_pairs={{0,24},{8,16},{16,8},{24,0},{1,25},{9,17},{17,9},{25,1},{2,26},{10... | collective-permute-start | bytes 98312 | tf_op jit(solution)/shard_map/ppermute | solution.py:19
  203.1 19.3 %all-to-all-start.1 = ((bf16[4,192,1024]{2,1,0:T(8,128)(2,1)}), bf16[4,192,1024]{2,1,0:T(8,128)(2,1)}, u32[]{:S(2)}, u32[]{:S(2)}) async-start(bf16[4,192,1024]{2,1,0:T(8,128)(2,1)} %down_own.3), calls=%async_computation.1 | async-start | bytes 3145728 | tf_op jit(solution)/shard_map/all_to_all | solution.py:543
  216.1 13.8 %collective-permute-start.29 = (bf16[96,1024]{1,0:T(8,128)(2,1)S(1)}, bf16[96,1024]{1,0:T(8,128)(2,1)S(1)}, u32[]{:S(2)}, u32[]{:S(2)}) collective-permute-start(bf16[96,1024]{1,0:T(8,128)(2,1)S(1)} %get-tuple-element.59), channel_id=1, source_target_pairs={{0,4},{2,6},{4,0},{6,2},{1,5},{3,7},{5,1},{7,3},{8,12},{10,14},{12... | collective-permute-start | bytes 589832 | tf_op jit(solution)/shard_map/ppermute | solution.py:19
  217.4 12.5 %collective-permute-start.30 = (bf16[96,1024]{1,0:T(8,128)(2,1)S(1)}, bf16[96,1024]{1,0:T(8,128)(2,1)S(1)}, u32[]{:S(2)}, u32[]{:S(2)}) collective-permute-start(bf16[96,1024]{1,0:T(8,128)(2,1)S(1)} %get-tuple-element.60), channel_id=1, source_target_pairs={{0,6},{2,4},{4,2},{6,0},{1,7},{3,5},{5,3},{7,1},{8,14},{10,12},{12... | collective-permute-start | bytes 589832 | tf_op jit(solution)/shard_map/ppermute | solution.py:19
  224.1 10.8 %collective-permute-start.28 = (bf16[96,1024]{1,0:T(8,128)(2,1)S(1)}, bf16[96,1024]{1,0:T(8,128)(2,1)S(1)}, u32[]{:S(2)}, u32[]{:S(2)}) collective-permute-start(bf16[96,1024]{1,0:T(8,128)(2,1)S(1)} %slice.180), channel_id=1, source_target_pairs={{0,2},{2,0},{4,6},{6,4},{1,3},{3,1},{5,7},{7,5},{8,10},{10,8},{12,... | collective-permute-start | bytes 589832 | tf_op jit(solution)/shard_map/ppermute | solution.py:19
  231.3 5.8 %collective-permute-start.34 = (bf16[16,2944]{1,0:T(8,128)(2,1)S(1)}, bf16[16,2944]{1,0:T(8,128)(2,1)S(1)}, u32[]{:S(2)}, u32[]{:S(2)}) collective-permute-start(bf16[16,2944]{1,0:T(8,128)(2,1)S(1)} %pad_maximum_fusion.3.refs_0_), channel_id=1, source_target_pairs={{0,24},{8,16},{16,8},{24,0},{1,25},{9,17},{17,9},{25,1},{2,26},{10... | collective-permute-start | bytes 282632 | tf_op jit(solution)/shard_map/ppermute | solution.py:19
  234.0 5.0 %collective-permute-start.33 = (bf16[16,2944]{1,0:T(8,128)(2,1)S(1)}, bf16[16,2944]{1,0:T(8,128)(2,1)S(1)}, u32[]{:S(2)}, u32[]{:S(2)}) collective-permute-start(bf16[16,2944]{1,0:T(8,128)(2,1)S(1)} %pad_maximum_fusion.3.refs_0_), channel_id=1, source_target_pairs={{0,16},{8,24},{16,0},{24,8},{1,17},{9,25},{17,1},{25,9},{2,18},{10... | collective-permute-start | bytes 282632 | tf_op jit(solution)/shard_map/ppermute | solution.py:19
  (25 other events, 426.8 us)

commit v5 on v4

--- a/solution.py
+++ b/solution.py
@@ -23,8 +23,9 @@
     return [value] + [send(value, axis, step) for step in range(1, lax.axis_size(axis))]
 
 
-def swap(values, axis):
-    return [values[0]] + [send(values[step], axis, step) for step in range(1, len(values))]
+def swap(values, axis, steps=None):
+    steps = range(len(values)) if steps is None else steps
+    return [send(value, axis, step) if step else value for value, step in zip(values, steps)]
 
 
 def after(value, *others):
@@ -226,94 +227,86 @@
     slot_grad[...] = dot(logit_grad, combine[...], 1, 1, precision=highest).astype(bf16)
 
 
-def fetch_down(groups, place, downs, weight, sems, side):
-    half, width = groups // 2, weight.shape[1] // (groups // 2)
-    for act in ("start", "wait"):
-        for k in range(groups):
-            source = place[0] ^ k
-            column = pl.multiple_of(lax.rem(source, half) * width, width)
-            copy = pltpu.make_async_copy(downs[k], weight.at[:, pl.ds(column, width)], sems.at[k])
-            pl.when(source // half == side)(getattr(copy, act))
-
-
 def column_chunks(count):
     size = min(count, 2 * lanes)
     return [slice(at, at + size) for at in range(0, count, size)]
 
 
-def other_kernel(groups, place, hidden, *refs):
-    downs, outs, (weight, sems) = refs[:groups], refs[groups:-2], refs[-2:]
+def down_kernel(first, near_count, capacity, place, hidden, *refs):
+    weight, sems = refs[-2:]
+    count = sems.shape[0]
+    downs, nears, outs = refs[:count], refs[count : count + near_count], refs[count + near_count : -2]
     step, steps = pl.program_id(0), pl.num_programs(0)
-    pl.when(step == 0)(lambda: fetch_down(groups, place, downs, weight, sems, 1 - place[1]))
-    for out, ref in enumerate(outs):
-
-        @pl.when(step // (steps // len(outs)) == out)
-        def _():
-            for columns in column_chunks(ref.shape[1]):
-                ref[:, columns] = dot(hidden[...], weight[:, columns], 1, 0).astype(bf16)
-
-
-def own_kernel(groups, capacity, place, hidden, *refs):
-    downs, (came, out, weight, sems) = refs[:groups], refs[groups:]
-    step = pl.program_id(0)
-    pl.when(step == 0)(lambda: fetch_down(groups, place, downs, weight, sems, place[1]))
+    width = downs[0].shape[1]
+
+    @pl.when(step == 0)
+    def _():
+        copies = []
+        for k, down in enumerate(downs):
+            column = pl.multiple_of(lax.rem(place[0] ^ (first + k), count) * width, width)
+            copies.append(pltpu.make_async_copy(down, weight.at[:, pl.ds(column, width)], sems.at[k]))
+        start(copies)
+        wait(copies)
+
     per_step = hidden.shape[0] // capacity
-    per_block = groups // per_step
-    row = pl.ds(pl.multiple_of(step // per_block * capacity, capacity), capacity)
-    for columns in column_chunks(out.shape[2]):
-        value = (dot(hidden[...], weight[:, columns], 1, 0) + came[:, columns].astype(f32)).astype(bf16)
-        for piece in range(per_step):
-            k = lax.rem(step, per_block) * per_step + piece
-            out[place[0] ^ k, row, columns] = value[piece * capacity : (piece + 1) * capacity]
-
-
-def chunk_block(first, count, step, place):
-    return jnp.clip(step - first, 0, count - 1), 0
-
-
-def down_other(place, hidden, groups, rows, downs, chunks):
+    per_block = 2 * count // per_step
+
+    def multiply(ref):
+        for columns in column_chunks(ref.shape[3]):
+            value = dot(hidden[...], weight[:, columns], 1, 0).astype(bf16)
+            for piece in range(per_step):
+                k = lax.rem(step, per_block) * per_step + piece
+                ref[place[0] ^ k, 0, :, columns] = value[piece * capacity : (piece + 1) * capacity]
+
+    def far(near, send, keep):
+        multiply(send)
+        keep[...] = near[...]
+
+    def both(near, send, keep):
+        pl.when(place[2] == 0)(lambda: far(near, send, keep))
+        pl.when(place[2] == 1)(lambda: far(near, keep, send))
+
+    chunks = near_count or len(outs)
+    for chunk in range(chunks):
+        if near_count:
+            work = functools.partial(both, nears[chunk], outs[chunk], outs[chunks + chunk])
+        else:
+            work = functools.partial(multiply, outs[chunk])
+        pl.when(step // (steps // chunks) == chunk)(work)
+
+
+def chunk_block(first, count, per_block, step, place):
+    return 0, jnp.clip(step - first, 0, count - 1) // per_block, 0, 0
+
+
+def down(place, hidden, rows, downs, first, nears, chunks, capacity, name):
     slots, (width, part) = hidden.shape[0], downs[0].shape
-    share = part * groups // 2
+    share = part * len(downs)
     half = slots // chunks // rows
+    results = 2 * chunks if nears else chunks
+    groups = 2 * len(downs)
+    per_block = groups * capacity // rows
+    specs = [
+        pl.BlockSpec((groups, 1, capacity, share), functools.partial(chunk_block, chunk * half, half, per_block))
+        for chunk in range(chunks)
+    ]
     return pl.pallas_call(
-        functools.partial(other_kernel, groups),
-        out_shape=[jax.ShapeDtypeStruct((slots // chunks, share), bf16)] * chunks,
+        functools.partial(down_kernel, first, len(nears), capacity),
+        out_shape=[jax.ShapeDtypeStruct((groups, half // per_block, capacity, share), bf16)] * results,
         grid_spec=pltpu.PrefetchScalarGridSpec(
             num_scalar_prefetch=1,
             grid=(slots // rows,),
             in_specs=[
                 pl.BlockSpec((rows, width), lambda i, place: ((chunks - 1 - i // half) * half + lax.rem(i, half), 0))
             ]
-            + [pl.BlockSpec(memory_space=pl.ANY)] * groups,
-            out_specs=[
-                pl.BlockSpec((rows, share), functools.partial(chunk_block, chunk * half, half)) for chunk in range(chunks)
-            ],
-            scratch_shapes=[pltpu.VMEM((width, share), bf16), pltpu.SemaphoreType.DMA((groups,))],
+            + [pl.BlockSpec(memory_space=pl.ANY)] * len(downs)
+            + (specs if nears else []),
+            out_specs=specs * (results // chunks),
+            scratch_shapes=[pltpu.VMEM((width, share), bf16), pltpu.SemaphoreType.DMA((len(downs),))],
         ),
         compiler_params=pltpu.CompilerParams(vmem_limit_bytes=62 * 1024 * 1024),
-        name="down_other",
-    )(place, hidden, *downs)
-
-
-def down_own(place, hidden, groups, first, rows, downs, came, capacity):
-    count, share = came.shape
-    width = hidden.shape[1]
-    shape = (groups, count // groups, share)
-    return pl.pallas_call(
-        functools.partial(own_kernel, groups, capacity),
-        out_shape=jax.ShapeDtypeStruct(shape, bf16),
-        grid_spec=pltpu.PrefetchScalarGridSpec(
-            num_scalar_prefetch=1,
-            grid=(count // rows,),
-            in_specs=[pl.BlockSpec((rows, width), lambda i, place: (first // rows + i, 0))]
-            + [pl.BlockSpec(memory_space=pl.ANY)] * groups
-            + [pl.BlockSpec((rows, share), lambda i, place: (i, 0))],
-            out_specs=pl.BlockSpec(shape, lambda i, place: (0, 0, 0)),
-            scratch_shapes=[pltpu.VMEM((width, share), bf16), pltpu.SemaphoreType.DMA((groups,))],
-        ),
-        compiler_params=pltpu.CompilerParams(vmem_limit_bytes=62 * 1024 * 1024),
-        name="down_own",
-    )(place, hidden, *downs, came)
+        name=name,
+    )(place, hidden, *downs, *nears)
 
 
 def pack_kernel(place, gate, up, down, tag_part, out):
@@ -473,7 +466,8 @@
     experts = lax.axis_size("expert")
     groups = lax.axis_size("dp")
     dp, expert, tensor = lax.axis_index("dp"), lax.axis_index("expert"), lax.axis_index("tensor")
-    place = jnp.stack([dp, tensor]).astype(jnp.int32)
+    upper = dp // (groups // 2)
+    place = jnp.stack([dp, tensor, upper ^ tensor]).astype(jnp.int32)
     tok_count, model_width = tokens.shape
     share_width = model_width // lax.axis_size("tensor")
     capacity = 3 * tok_count // experts
@@ -489,7 +483,8 @@
     weight = jnp.sum(jnp.where(member, gate_values[None], f32(0.0)), axis=2)
     upto = (jnp.arange(tok_count)[:, None] <= jnp.arange(tok_count)[None, :]).astype(f32)
     code = used * dot(used, upto, 1, 0)
-    order = jnp.arange(experts, dtype=jnp.int32) ^ expert
+    steps = sorted(range(experts), key=lambda step: (step % 2, step))
+    order = jnp.array(steps, jnp.int32) ^ expert
     places = jnp.arange(1, lanes + 1, dtype=jnp.int32).astype(f32)
     own_match = code[order][:, None, :] == places[None, :, None]
     combine = jnp.where(own_match, weight[order][:, None, :], f32(0.0)).reshape(experts * lanes, tok_count)
@@ -506,12 +501,12 @@
     plane_tokens = after(plane_tokens, parts, *downs)
     parts = lax.all_to_all(after(parts, *plane_parts), "dp", split_axis=0, concat_axis=0, tiled=True)
     x_own = []
-    for j in range(experts):
+    for j in steps:
         target_code = lax.dynamic_index_in_dim(plane_code, expert ^ j, 1, keepdims=False)
         match = (target_code[:, None, :] == places[None, :capacity, None]).astype(bf16)
         outgoing = jnp.einsum("gst,gtd->gsd", match, plane_tokens, preferred_element_type=f32).astype(bf16)
         x_own.append(outgoing.reshape(block_rows, share_width))
-    x_own = swap(x_own, "expert")
+    x_own = swap(x_own, "expert", steps)
     x_other = [send(value, "tensor", 1) for value in x_own]
     low_rank = low(place, x_own, x_other, adapter_in[0], rows)
     token_logits = dot(tag_weight, tokens, 0, 1)
@@ -526,24 +521,27 @@
     slot_logits = (slot_logits.astype(f32) + send(slot_logits, "tensor", 1).astype(f32)).astype(bf16)
     plane_lanes = groups * lanes
     pieces = [slot_logits[:, j * plane_lanes : (j + 1) * plane_lanes] for j in range(experts)]
-    pieces = swap(pieces, "expert")
-
-    hidden = after(hidden, *pieces)
+    pieces = swap(pieces, "expert", steps)
+
+    chunks = [(experts // 2, experts // 2), (0, experts // 2)]
+    half = groups // 2
+
+    def change(part):
+        return lax.all_to_all(part, "dp", split_axis=0, concat_axis=0, tiled=True)
+
+    near = down(place, hidden, rows, downs[:half], 0, [], len(chunks), capacity, "down_near")
+    hidden = after(hidden, near[0], *pieces)
     pieces = [
         jnp.concatenate([piece[:, k * lanes : (k + 1) * lanes] for piece in pieces], axis=1) for k in range(groups)
     ]
     pieces = swap(pieces, "dp")
-
-    chunks = [(experts // 2, experts // 2), (0, experts // 2)]
+    halves = down(place, hidden, rows, downs[half:], half, near, len(chunks), capacity, "down_far")
+    others, kept = [send(value, "tensor", 1) for value in halves[: len(chunks)]], halves[len(chunks) :]
 
     def own(chunk, came):
-        return down_own(place, hidden, groups, chunks[chunk][0] * block_rows, rows, downs, came, capacity)
-
-    def change(part):
-        return lax.all_to_all(part, "dp", split_axis=0, concat_axis=0, tiled=True)
-
-    others = down_other(place, hidden, groups, rows, downs, len(chunks))
-    others = [send(other, "tensor", 1) for other in others]
+        value = (kept[chunk].astype(f32) + came.astype(f32)).astype(bf16)
+        return value.reshape(groups, -1, share_width)
+
     first = own(0, after(others[0], *pieces))
 
     pieces[0] = after(pieces[0], first)
@@ -553,7 +551,7 @@
         compiler_params=pltpu.CompilerParams(vmem_limit_bytes=vmem_limit),
         name="tag_grad",
     )(*pieces, token_logits, combine, tag_labels[None, :])
-    slot_grad = swap([slot_grad[:, j * lanes : (j + 1) * lanes] for j in range(experts)], "expert")
+    slot_grad = swap([slot_grad[:, j * lanes : (j + 1) * lanes] for j in range(experts)], "expert", steps)
     second = own(1, after(others[1], *slot_grad))
     slot_grad[0] = after(slot_grad[0], second)
     slot_grad = gather(jnp.concatenate(slot_grad, axis=1), "dp")
@@ -570,7 +568,7 @@
         first, count = chunks[chunk]
         for j in range(first, first + count):
             kept = sums[chunk][(j - first) * capacity : (j - first + 1) * capacity]
-            returned[j] = send(kept, "expert", j) if j else kept
+            returned[j] = send(kept, "expert", steps[j]) if steps[j] else kept
 
     give_back(0)
     in_local = after(in_local, *returned[chunks[0][0] :])

time: 242 us -> 237 us (0.979)
  waiting for transfers between devices: 99.3 us -> 88.4 us
  other arithmetic: 4.7 us -> 11.8 us
  Pallas kernels: 66.8 us -> 63.8 us
    ppermute x35, waiting for transfers between devices: 83.8 us -> 70.1 us  [send(): lax.ppermute(value, axis, [(i, i ^ step) for i in range(lax.axis_size(axi...]
    convert_element_type x0 -> x2, other arithmetic: none -> 7.05 us  [own(): value = (kept[chunk].astype(f32) + came.astype(f32)).astype(bf16)]
    pallas_call x3 -> x2, Pallas kernels: 22.7 us -> 19.6 us  [down(): pl.pallas_call(functools.partial(down_kernel, first, len(nears), capacity...]
    all_to_all x1, waiting for transfers between devices: 12.6 us -> 15.4 us  [local(): lax.all_to_all(after(parts, *plane_parts), 'dp', split_axis=0, concat_axi...]
  transfers between devices with their start and end apart: 38 -> 38, of which waited for: 26 -> 21; matrix products, arithmetic and copies ran while one was open for 7% -> 10% of each run, Pallas kernels for 24% -> 22%
where the time goes in v5:
time: 237 us; the launch traced here: 236 us
  waiting for transfers between devices  88.4 us (37%)
  Pallas kernels  63.8 us (27%)
  starting transfers between devices  58 us (24%)
  other arithmetic  11.8 us (5%)
  local copies, waits for them, and re-layouts  8.73 us (4%)
  matrix products  4.52 us (2%)
    ppermute x35, waiting for transfers between devices, send(): lax.ppermute(value, axis, [(i, i ^ step) for i in range(lax.axis_size(axi...  70.1 us
    ppermute x35, starting transfers between devices, send(): lax.ppermute(value, axis, [(i, i ^ step) for i in range(lax.axis_size(axi...  43.5 us
    pallas_call x1, Pallas kernels, forward(): pl.pallas_call(functools.partial(forward_kernel, experts, block_rows // r...  21.7 us
    pallas_call x2, Pallas kernels, down(): pl.pallas_call(functools.partial(down_kernel, first, len(nears), capacity...  19.6 us
    all_to_all x1, waiting for transfers between devices, local(): lax.all_to_all(after(parts, *plane_parts), 'dp', split_axis=0, concat_axi...  15.4 us
    all_to_all x2, starting transfers between devices, change(): return lax.all_to_all(part, 'dp', split_axis=0, concat_axis=0, tiled=True)  9 us
    pallas_call x1, Pallas kernels, pack(): pl.pallas_call(pack_kernel, out_shape=jax.ShapeDtypeStruct((groups, part...  8.71 us
    convert_element_type x2, other arithmetic, own(): value = (kept[chunk].astype(f32) + came.astype(f32)).astype(bf16)  7.05 us
  transfers between devices with their start and end apart: 38, of which 21 were waited for; matrix products, arithmetic and copies ran while one was open for 10% of the time, Pallas kernels for 22%

profile of v5, /device:TPU:0, one launch (start us, length us, event | category | flops | bytes accessed | tf_op | source)
XLA Modules:
  0.0 236.4 jit_solution(1307379003657548934)
XLA Ops:
  1.8 4.0 %collective-permute-start.2 = (bf16[136,1024]{1,0:T(8,128)(2,1)S(1)}, bf16[136,1024]{1,0:T(8,128)(2,1)S(1)}, u32[]{:S(2)}, u32[]{:S(2)}) collective-permute-start(bf16[136,1024]{1,0:T(8,128)(2,1)S(1)} %get-tuple-element.70), channel_id=1, source_target_pairs={{0,24},{8,16},{16,8},{24,0},{1,25},{9,17},{17,9},{25,1},{2,26},{10... | collective-permute-start | bytes 835592 | tf_op jit(solution)/shard_map/ppermute | solution.py:19
  7.7 8.7 %pack.1 = bf16[4,7,528,256]{3,2,1,0:T(8,128)(2,1)} custom-call(s32[3]{0:T(128)S(1)} %pad_add_fusion.place, bf16[512,3584]{1,0:T(8,128)(2,1)} %bitcast.63, bf16[512,3584]{1,0:T(8,128)(2,1)} %bitcast.64, bf16[3584,512]{1,0:T(8,128)(2,1)} %bitcast.60, bf16[2048,32]{1,0:T(8,128)(2,1)S(1)} %copy.17.tag_part), custom_call_target="tpu_custom_call" | custom-call | tf_op jit(solution)/shard_map/pack/pallas_call | solution.py:333
  18.7 5.5 %all-to-all-start = ((bf16[4,7,528,256]{3,2,1,0:T(8,128)(2,1)}), bf16[4,7,528,256]{3,2,1,0:T(8,128)(2,1)}, u32[]{:S(2)}, u32[]{:S(2)}) async-start(bf16[4,7,528,256]{3,2,1,0:T(8,128)(2,1)} %pack.1), calls=%async_computation | async-start | bytes 15138816 | tf_op jit(solution)/shard_map/all_to_all | solution.py:502
  24.2 3.9 %dynamic-slice_bitcast_fusion = (bf16[896,512]{1,0:T(8,128)(2,1)}, bf16[896,512]{1,0:T(8,128)(2,1)}, bf16[896,512]{1,0:T(8,128)(2,1)}, bf16[896,512]{1,0:T(8,128)(2,1)}) fusion(bf16[1,3584,512]{2,1,0:T(8,128)(2,1)} %param.17, s32[]{:T(128)S(6)} %select_n.56, s32[]{:T(128)S(6)} %select_n.54, s32[]{:T(128)S(6)} %select_n.53, s32[]{:T(128)S(6)} %select_n.55), kind=kLoop, calls=%fused_computation.17 | loop fusion | bytes 7340048 | tf_op jit(solution)/shard_map/dynamic_slice | solution.py:500
  29.6 2.7 %collective-permute-start.3 = (bf16[384,1024]{1,0:T(8,128)(2,1)S(1)}, bf16[384,1024]{1,0:T(8,128)(2,1)}, u32[]{:S(2)}, u32[]{:S(2)}) collective-permute-start(bf16[384,1024]{1,0:T(8,128)(2,1)S(1)} %bitcast.73), channel_id=1, source_target_pairs={{0,4},{2,6},{4,0},{6,2},{1,5},{3,7},{5,1},{7,3},{8,12},{10,14},{12... | collective-permute-start | bytes 2359304 | tf_op jit(solution)/shard_map/ppermute | solution.py:19
  34.6 34.4 %collective-permute-done.3.refs_1_ = bf16[384,1024]{1,0:T(8,128)(2,1)} collective-permute-done((bf16[384,1024]{1,0:T(8,128)(2,1)S(1)}, bf16[384,1024]{1,0:T(8,128)(2,1)}, u32[]{:S(2)}, u32[]{:S(2)}) %collective-permute-start.3) | collective-permute-done | bytes 786464 | tf_op jit(solution)/shard_map/ppermute | solution.py:19
  69.5 15.4 %collective-permute-done.5.refs_3_ = bf16[384,1024]{1,0:T(8,128)(2,1)} collective-permute-done((bf16[384,1024]{1,0:T(8,128)(2,1)S(1)}, bf16[384,1024]{1,0:T(8,128)(2,1)}, u32[]{:S(2)}, u32[]{:S(2)}) %collective-permute-start.5) | collective-permute-done | bytes 786464 | tf_op jit(solution)/shard_map/ppermute | solution.py:19
  87.5 5.0 %low_rank.1.refs_8_.refs_14_ = bf16[1536,16]{1,0:T(8,128)(2,1)S(1)} custom-call(s32[3]{0:T(128)S(1)} %pad_add_fusion.place, bf16[384,1024]{1,0:T(8,128)(2,1)S(1)} %bitcast.55, bf16[384,1024]{1,0:T(8,128)(2,1)} %collective-permute-done.3.refs_1_, bf16[384,1024]{1,0:T(8,128)(2,1)} %collective-permute-done.4.refs_2_, ...), custom_call_target="tpu_custom_call" | custom-call | tf_op jit(solution)/shard_map/low_rank/pallas_call | solution.py:99
  92.6 15.4 %all-to-all-done.refs_10_ = bf16[4,7,528,256]{3,2,1,0:T(8,128)(2,1)} async-done(((bf16[4,7,528,256]{3,2,1,0:T(8,128)(2,1)}), bf16[4,7,528,256]{3,2,1,0:T(8,128)(2,1)}, u32[]{:S(2)}, u32[]{:S(2)}) %all-to-all-start) | async-done | bytes 7569440 | tf_op jit(solution)/shard_map/all_to_all | solution.py:502
  112.2 21.7 %gate_up.1 = (bf16[1536,896]{1,0:T(8,128)(2,1)}, bf16[1536,896]{1,0:T(8,128)(2,1)}, bf16[32,2048]{1,0:T(8,128)(2,1)S(1)}, bf16[32,896]{1,0:T(8,128)(2,1)S(1)}) custom-call(s32[3]{0:T(128)S(1)} %pad_add_fusion.place, bf16[384,1024]{1,0:T(8,128)(2,1)S(1)} %bitcast.56, bf16[384,1024]{1,0:T(8,128)(2,1)} %collective-permute-done.3.refs_1_, ...), custom_call_target="tpu_custom_call" | custom-call | tf_op jit(solution)/shard_map/gate_up/pallas_call | solution.py:185
  136.0 3.8 %collective-permute-start.14 = (bf16[32,512]{1,0:T(8,128)(2,1)}, bf16[32,512]{1,0:T(8,128)(2,1)}, u32[]{:S(2)}, u32[]{:S(2)}) collective-permute-start(bf16[32,512]{1,0:T(8,128)(2,1)} %get-tuple-element.75), channel_id=1, source_target_pairs={{0,6},{2,4},{4,2},{6,0},{1,7},{3,5},{5,3},{7,1},{8,14},{10,12},{12... | collective-permute-start | bytes 98312 | tf_op jit(solution)/shard_map/ppermute | solution.py:19
  140.4 9.2 %down_near.1 = (bf16[4,2,96,1024]{3,2,1,0:T(8,128)(2,1)}, bf16[4,2,96,1024]{3,2,1,0:T(8,128)(2,1)}) custom-call(s32[3]{0:T(128)} %copy-done.3, bf16[1536,896]{1,0:T(8,128)(2,1)} %get-tuple-element.41.hidden, bf16[896,512]{1,0:T(8,128)(2,1)} %get-tuple-element.37.refs_0_, bf16[896,512]{1,0:T(8,128)(2,1)} %collective-permute-done.10.refs_1_), custom_call_target="tpu_custom_call" | custom-call | tf_op jit(solution)/shard_map/down_near/pallas_call | solution.py:293
  150.1 10.4 %down_far.1 = (bf16[4,2,96,1024]{3,2,1,0:T(8,128)(2,1)}, bf16[4,2,96,1024]{3,2,1,0:T(8,128)(2,1)}, bf16[4,2,96,1024]{3,2,1,0:T(8,128)(2,1)}, bf16[4,2,96,1024]{3,2,1,0:T(8,128)(2,1)}) custom-call(s32[3]{0:T(128)} %copy-done.3, bf16[1536,896]{1,0:T(8,128)(2,1)} %get-tuple-element.41.hidden, bf16[896,512]{1,0:T(8,128)(2,1)} %collective-permute-done.15.refs_0_, ...), custom_call_target="tpu_custom_call" | custom-call | tf_op jit(solution)/shard_map/down_far/pallas_call | solution.py:293
  169.0 3.3 %add_convert_fusion.1 = bf16[4,2,96,1024]{3,2,1,0:T(8,128)(2,1)} fusion(bf16[4,2,96,1024]{3,2,1,0:T(8,128)(2,1)S(1)} %collective-permute-done.18, bf16[4,2,96,1024]{3,2,1,0:T(8,128)(2,1)} %get-tuple-element.47), kind=kLoop, calls=%fused_computation.3 | loop fusion | flops 3145728 | bytes 4718592 | tf_op jit(solution)/shard_map/convert_element_type | solution.py:542
  172.2 4.7 %all-to-all-start.2 = ((bf16[4,192,1024]{2,1,0:T(8,128)(2,1)}), bf16[4,192,1024]{2,1,0:T(8,128)(2,1)}, u32[]{:S(2)}, u32[]{:S(2)}) async-start(bf16[4,192,1024]{2,1,0:T(8,128)(2,1)} %bitcast.61), calls=%async_computation.2 | async-start | bytes 3145728 | tf_op jit(solution)/shard_map/all_to_all | solution.py:530
  177.5 4.1 %collective-permute-start.24 = (bf16[32,128]{1,0:T(8,128)(2,1)S(1)}, bf16[32,128]{1,0:T(8,128)(2,1)S(1)}, u32[]{:S(2)}, u32[]{:S(2)}) collective-permute-start(bf16[32,128]{1,0:T(8,128)(2,1)S(1)} %get-tuple-element.78), channel_id=1, source_target_pairs={{0,6},{2,4},{4,2},{6,0},{1,7},{3,5},{5,3},{7,1},{8,14},{10,12},{12... | collective-permute-start | bytes 24584 | tf_op jit(solution)/shard_map/ppermute | solution.py:19
  187.3 3.8 %add_convert_fusion = bf16[4,2,96,1024]{3,2,1,0:T(8,128)(2,1)} fusion(bf16[4,2,96,1024]{3,2,1,0:T(8,128)(2,1)} %collective-permute-done.17, bf16[4,2,96,1024]{3,2,1,0:T(8,128)(2,1)} %get-tuple-element.45), kind=kLoop, calls=%fused_computation.2 | loop fusion | flops 3145728 | bytes 4718592 | tf_op jit(solution)/shard_map/convert_element_type | solution.py:542
  191.2 2.8 %collective-permute-start.27 = (bf16[32,512]{1,0:T(8,128)(2,1)S(1)}, bf16[32,512]{1,0:T(8,128)(2,1)S(1)}, u32[]{:S(2)}, u32[]{:S(2)}) collective-permute-start(bf16[32,512]{1,0:T(8,128)(2,1)S(1)} %constant_dynamic-update-slice_fusion.refs_8_), channel_id=1, source_target_pairs={{0,24},{8,16},{16,8},{24,0},{1,25},{9,17},{17,9},{25,1},{2,26},{10... | collective-permute-start | bytes 98312 | tf_op jit(solution)/shard_map/ppermute | solution.py:19
  198.4 4.4 %all-to-all-start.1 = ((bf16[4,192,1024]{2,1,0:T(8,128)(2,1)}), bf16[4,192,1024]{2,1,0:T(8,128)(2,1)}, u32[]{:S(2)}, u32[]{:S(2)}) async-start(bf16[4,192,1024]{2,1,0:T(8,128)(2,1)} %bitcast.62), calls=%async_computation.1 | async-start | bytes 3145728 | tf_op jit(solution)/shard_map/all_to_all | solution.py:530
  204.5 6.9 %adapter_grad.1 = (f32[16,896]{1,0:T(8,128)S(1)}, f32[16,2048]{1,0:T(8,128)S(1)}) custom-call(s32[3]{0:T(128)S(1)} %copy-done.4, bf16[384,1024]{1,0:T(8,128)(2,1)S(1)} %bitcast.57, bf16[384,1024]{1,0:T(8,128)(2,1)} %collective-permute-done.3.refs_1_, bf16[384,1024]{1,0:T(8,128)(2,1)} %collective-permute-done.4.refs_2_, ...), custom_call_target="tpu_custom_call" | custom-call | tf_op jit(solution)/shard_map/adapter_grad/pallas_call | solution.py:391
  212.5 3.5 %collective-permute-start.30 = (bf16[96,1024]{1,0:T(8,128)(2,1)S(1)}, bf16[96,1024]{1,0:T(8,128)(2,1)S(1)}, u32[]{:S(2)}, u32[]{:S(2)}) collective-permute-start(bf16[96,1024]{1,0:T(8,128)(2,1)S(1)} %get-tuple-element.68), channel_id=1, source_target_pairs={{0,6},{2,4},{4,2},{6,0},{1,7},{3,5},{5,3},{7,1},{8,14},{10,12},{12... | collective-permute-start | bytes 589832 | tf_op jit(solution)/shard_map/ppermute | solution.py:19
  216.0 3.0 %all-to-all-done.1 = bf16[4,192,1024]{2,1,0:T(8,128)(2,1)} async-done(((bf16[4,192,1024]{2,1,0:T(8,128)(2,1)}), bf16[4,192,1024]{2,1,0:T(8,128)(2,1)}, u32[]{:S(2)}, u32[]{:S(2)}) %all-to-all-start.1) | async-done | bytes 1572896 | tf_op jit(solution)/shard_map/all_to_all | solution.py:530
  220.7 4.8 %collective-permute-start.28 = (bf16[96,1024]{1,0:T(8,128)(2,1)S(1)}, bf16[96,1024]{1,0:T(8,128)(2,1)S(1)}, u32[]{:S(2)}, u32[]{:S(2)}) collective-permute-start(bf16[96,1024]{1,0:T(8,128)(2,1)S(1)} %slice.180), channel_id=1, source_target_pairs={{0,4},{2,6},{4,0},{6,2},{1,5},{3,7},{5,1},{7,3},{8,12},{10,14},{12... | collective-permute-start | bytes 589832 | tf_op jit(solution)/shard_map/ppermute | solution.py:19
  230.9 2.9 %collective-permute-done.28 = bf16[96,1024]{1,0:T(8,128)(2,1)S(1)} collective-permute-done((bf16[96,1024]{1,0:T(8,128)(2,1)S(1)}, bf16[96,1024]{1,0:T(8,128)(2,1)S(1)}, u32[]{:S(2)}, u32[]{:S(2)}) %collective-permute-start.28) | collective-permute-done | bytes 196640 | tf_op jit(solution)/shard_map/ppermute | solution.py:19
  (135 shorter events, 51.3 us)
Async XLA Ops:
  1.8 14.6 %collective-permute-start.2 = (bf16[136,1024]{1,0:T(8,128)(2,1)S(1)}, bf16[136,1024]{1,0:T(8,128)(2,1)S(1)}, u32[]{:S(2)}, u32[]{:S(2)}) collective-permute-start(bf16[136,1024]{1,0:T(8,128)(2,1)S(1)} %get-tuple-element.70), channel_id=1, source_target_pairs={{0,24},{8,16},{16,8},{24,0},{1,25},{9,17},{17,9},{25,1},{2,26},{10... | collective-permute-start | bytes 835592 | tf_op jit(solution)/shard_map/ppermute | solution.py:19
  5.7 12.6 %collective-permute-start.1 = (bf16[136,1024]{1,0:T(8,128)(2,1)S(1)}, bf16[136,1024]{1,0:T(8,128)(2,1)S(1)}, u32[]{:S(2)}, u32[]{:S(2)}) collective-permute-start(bf16[136,1024]{1,0:T(8,128)(2,1)S(1)} %get-tuple-element.70), channel_id=1, source_target_pairs={{0,16},{8,24},{16,0},{24,8},{1,17},{9,25},{17,1},{25,9},{2,18},{10... | collective-permute-start | bytes 835592 | tf_op jit(solution)/shard_map/ppermute | solution.py:19
  6.2 12.4 %collective-permute-start = (bf16[136,1024]{1,0:T(8,128)(2,1)S(1)}, bf16[136,1024]{1,0:T(8,128)(2,1)S(1)}, u32[]{:S(2)}, u32[]{:S(2)}) collective-permute-start(bf16[136,1024]{1,0:T(8,128)(2,1)S(1)} %get-tuple-element.70), channel_id=1, source_target_pairs={{0,8},{8,0},{16,24},{24,16},{1,9},{9,1},{17,25},{25,17},{2,10},{10... | collective-permute-start | bytes 835592 | tf_op jit(solution)/shard_map/ppermute | solution.py:19
  18.7 89.3 %all-to-all-start = ((bf16[4,7,528,256]{3,2,1,0:T(8,128)(2,1)}), bf16[4,7,528,256]{3,2,1,0:T(8,128)(2,1)}, u32[]{:S(2)}, u32[]{:S(2)}) async-start(bf16[4,7,528,256]{3,2,1,0:T(8,128)(2,1)} %pack.1), calls=%async_computation | async-start | bytes 15138816 | tf_op jit(solution)/shard_map/all_to_all | solution.py:502
  29.6 39.4 %collective-permute-start.3 = (bf16[384,1024]{1,0:T(8,128)(2,1)S(1)}, bf16[384,1024]{1,0:T(8,128)(2,1)}, u32[]{:S(2)}, u32[]{:S(2)}) collective-permute-start(bf16[384,1024]{1,0:T(8,128)(2,1)S(1)} %bitcast.73), channel_id=1, source_target_pairs={{0,4},{2,6},{4,0},{6,2},{1,5},{3,7},{5,1},{7,3},{8,12},{10,14},{12... | collective-permute-start | bytes 2359304 | tf_op jit(solution)/shard_map/ppermute | solution.py:19
  32.2 36.7 %collective-permute-start.4 = (bf16[384,1024]{1,0:T(8,128)(2,1)S(1)}, bf16[384,1024]{1,0:T(8,128)(2,1)}, u32[]{:S(2)}, u32[]{:S(2)}) collective-permute-start(bf16[384,1024]{1,0:T(8,128)(2,1)S(1)} %bitcast.72), channel_id=1, source_target_pairs={{0,2},{2,0},{4,6},{6,4},{1,3},{3,1},{5,7},{7,5},{8,10},{10,8},{12,... | collective-permute-start | bytes 2359304 | tf_op jit(solution)/shard_map/ppermute | solution.py:19
  33.8 51.1 %collective-permute-start.5 = (bf16[384,1024]{1,0:T(8,128)(2,1)S(1)}, bf16[384,1024]{1,0:T(8,128)(2,1)}, u32[]{:S(2)}, u32[]{:S(2)}) collective-permute-start(bf16[384,1024]{1,0:T(8,128)(2,1)S(1)} %bitcast.71), channel_id=1, source_target_pairs={{0,6},{2,4},{4,2},{6,0},{1,7},{3,5},{5,3},{7,1},{8,14},{10,12},{12... | collective-permute-start | bytes 2359304 | tf_op jit(solution)/shard_map/ppermute | solution.py:19
  34.5 52.1 %collective-permute-start.6 = (bf16[384,1024]{1,0:T(8,128)(2,1)S(1)}, bf16[384,1024]{1,0:T(8,128)(2,1)S(1)}, u32[]{:S(2)}, u32[]{:S(2)}) collective-permute-start(bf16[384,1024]{1,0:T(8,128)(2,1)S(1)} %bitcast.54), channel_id=1, source_target_pairs={{0,1},{1,0},{2,3},{3,2},{4,5},{5,4},{6,7},{7,6},{8,9},{9,8},{10,11... | collective-permute-start | bytes 2359304 | tf_op jit(solution)/shard_map/ppermute | solution.py:19
  69.0 17.6 %collective-permute-start.7 = (bf16[384,1024]{1,0:T(8,128)(2,1)}, bf16[384,1024]{1,0:T(8,128)(2,1)}, u32[]{:S(2)}, u32[]{:S(2)}) collective-permute-start(bf16[384,1024]{1,0:T(8,128)(2,1)} %collective-permute-done.3.refs_1_), channel_id=1, source_target_pairs={{0,1},{1,0},{2,3},{3,2},{4,5},{5,4},{6,7},{7,6},{8,9},{9,8},{10,11... | collective-permute-start | bytes 2359304 | tf_op jit(solution)/shard_map/ppermute | solution.py:19
  69.0 17.6 %collective-permute-start.8 = (bf16[384,1024]{1,0:T(8,128)(2,1)}, bf16[384,1024]{1,0:T(8,128)(2,1)}, u32[]{:S(2)}, u32[]{:S(2)}) collective-permute-start(bf16[384,1024]{1,0:T(8,128)(2,1)} %collective-permute-done.4.refs_2_), channel_id=1, source_target_pairs={{0,1},{1,0},{2,3},{3,2},{4,5},{5,4},{6,7},{7,6},{8,9},{9,8},{10,11... | collective-permute-start | bytes 2359304 | tf_op jit(solution)/shard_map/ppermute | solution.py:19
  107.9 31.8 %collective-permute-start.10 = (bf16[896,512]{1,0:T(8,128)(2,1)}, bf16[896,512]{1,0:T(8,128)(2,1)}, u32[]{:S(2)}, u32[]{:S(2)}) collective-permute-start(bf16[896,512]{1,0:T(8,128)(2,1)} %get-tuple-element.38), channel_id=1, source_target_pairs={{0,8},{8,0},{16,24},{24,16},{1,9},{9,1},{17,25},{25,17},{2,10},{10... | collective-permute-start | bytes 2752520 | tf_op jit(solution)/shard_map/ppermute | solution.py:19
  109.3 40.8 %collective-permute-start.15 = (bf16[896,512]{1,0:T(8,128)(2,1)}, bf16[896,512]{1,0:T(8,128)(2,1)}, u32[]{:S(2)}, u32[]{:S(2)}) collective-permute-start(bf16[896,512]{1,0:T(8,128)(2,1)} %get-tuple-element.42), channel_id=1, source_target_pairs={{0,16},{8,24},{16,0},{24,8},{1,17},{9,25},{17,1},{25,9},{2,18},{10... | collective-permute-start | bytes 2752520 | tf_op jit(solution)/shard_map/ppermute | solution.py:19
  109.9 40.2 %collective-permute-start.16 = (bf16[896,512]{1,0:T(8,128)(2,1)}, bf16[896,512]{1,0:T(8,128)(2,1)}, u32[]{:S(2)}, u32[]{:S(2)}) collective-permute-start(bf16[896,512]{1,0:T(8,128)(2,1)} %get-tuple-element.43), channel_id=1, source_target_pairs={{0,24},{8,16},{16,8},{24,0},{1,25},{9,17},{17,9},{25,1},{2,26},{10... | collective-permute-start | bytes 2752520 | tf_op jit(solution)/shard_map/ppermute | solution.py:19
  136.0 13.6 %collective-permute-start.14 = (bf16[32,512]{1,0:T(8,128)(2,1)}, bf16[32,512]{1,0:T(8,128)(2,1)}, u32[]{:S(2)}, u32[]{:S(2)}) collective-permute-start(bf16[32,512]{1,0:T(8,128)(2,1)} %get-tuple-element.75), channel_id=1, source_target_pairs={{0,6},{2,4},{4,2},{6,0},{1,7},{3,5},{5,3},{7,1},{8,14},{10,12},{12... | collective-permute-start | bytes 98312 | tf_op jit(solution)/shard_map/ppermute | solution.py:19
  139.8 9.8 %collective-permute-start.13 = (bf16[32,512]{1,0:T(8,128)(2,1)}, bf16[32,512]{1,0:T(8,128)(2,1)S(1)}, u32[]{:S(2)}, u32[]{:S(2)}) collective-permute-start(bf16[32,512]{1,0:T(8,128)(2,1)} %get-tuple-element.76), channel_id=1, source_target_pairs={{0,2},{2,0},{4,6},{6,4},{1,3},{3,1},{5,7},{7,5},{8,10},{10,8},{12,... | collective-permute-start | bytes 98312 | tf_op jit(solution)/shard_map/ppermute | solution.py:19
  139.8 9.8 %collective-permute-start.12 = (bf16[32,512]{1,0:T(8,128)(2,1)}, bf16[32,512]{1,0:T(8,128)(2,1)S(1)}, u32[]{:S(2)}, u32[]{:S(2)}) collective-permute-start(bf16[32,512]{1,0:T(8,128)(2,1)} %get-tuple-element.77), channel_id=1, source_target_pairs={{0,4},{2,6},{4,0},{6,2},{1,5},{3,7},{5,1},{7,3},{8,12},{10,14},{12... | collective-permute-start | bytes 98312 | tf_op jit(solution)/shard_map/ppermute | solution.py:19
  160.6 8.4 %collective-permute-start.18 = (bf16[4,2,96,1024]{3,2,1,0:T(8,128)(2,1)}, bf16[4,2,96,1024]{3,2,1,0:T(8,128)(2,1)S(1)}, u32[]{:S(2)}, u32[]{:S(2)}) collective-permute-start(bf16[4,2,96,1024]{3,2,1,0:T(8,128)(2,1)} %get-tuple-element.48), channel_id=1, source_target_pairs={{0,1},{1,0},{2,3},{3,2},{4,5},{5,4},{6,7},{7,6},{8,9},{9,8},{10,11... | collective-permute-start | bytes 4718600 | tf_op jit(solution)/shard_map/ppermute | solution.py:19
  161.4 21.4 %collective-permute-start.17 = (bf16[4,2,96,1024]{3,2,1,0:T(8,128)(2,1)}, bf16[4,2,96,1024]{3,2,1,0:T(8,128)(2,1)}, u32[]{:S(2)}, u32[]{:S(2)}) collective-permute-start(bf16[4,2,96,1024]{3,2,1,0:T(8,128)(2,1)} %get-tuple-element.46), channel_id=1, source_target_pairs={{0,1},{1,0},{2,3},{3,2},{4,5},{5,4},{6,7},{7,6},{8,9},{9,8},{10,11... | collective-permute-start | bytes 4718600 | tf_op jit(solution)/shard_map/ppermute | solution.py:19
  172.2 26.2 %all-to-all-start.2 = ((bf16[4,192,1024]{2,1,0:T(8,128)(2,1)}), bf16[4,192,1024]{2,1,0:T(8,128)(2,1)}, u32[]{:S(2)}, u32[]{:S(2)}) async-start(bf16[4,192,1024]{2,1,0:T(8,128)(2,1)} %bitcast.61), calls=%async_computation.2 | async-start | bytes 3145728 | tf_op jit(solution)/shard_map/all_to_all | solution.py:530
  198.4 20.5 %all-to-all-start.1 = ((bf16[4,192,1024]{2,1,0:T(8,128)(2,1)}), bf16[4,192,1024]{2,1,0:T(8,128)(2,1)}, u32[]{:S(2)}, u32[]{:S(2)}) async-start(bf16[4,192,1024]{2,1,0:T(8,128)(2,1)} %bitcast.62), calls=%async_computation.1 | async-start | bytes 3145728 | tf_op jit(solution)/shard_map/all_to_all | solution.py:530
  211.4 14.5 %collective-permute-start.29 = (bf16[96,1024]{1,0:T(8,128)(2,1)S(1)}, bf16[96,1024]{1,0:T(8,128)(2,1)S(1)}, u32[]{:S(2)}, u32[]{:S(2)}) collective-permute-start(bf16[96,1024]{1,0:T(8,128)(2,1)S(1)} %get-tuple-element.67), channel_id=1, source_target_pairs={{0,2},{2,0},{4,6},{6,4},{1,3},{3,1},{5,7},{7,5},{8,10},{10,8},{12,... | collective-permute-start | bytes 589832 | tf_op jit(solution)/shard_map/ppermute | solution.py:19
  212.5 13.5 %collective-permute-start.30 = (bf16[96,1024]{1,0:T(8,128)(2,1)S(1)}, bf16[96,1024]{1,0:T(8,128)(2,1)S(1)}, u32[]{:S(2)}, u32[]{:S(2)}) collective-permute-start(bf16[96,1024]{1,0:T(8,128)(2,1)S(1)} %get-tuple-element.68), channel_id=1, source_target_pairs={{0,6},{2,4},{4,2},{6,0},{1,7},{3,5},{5,3},{7,1},{8,14},{10,12},{12... | collective-permute-start | bytes 589832 | tf_op jit(solution)/shard_map/ppermute | solution.py:19
  220.7 13.1 %collective-permute-start.28 = (bf16[96,1024]{1,0:T(8,128)(2,1)S(1)}, bf16[96,1024]{1,0:T(8,128)(2,1)S(1)}, u32[]{:S(2)}, u32[]{:S(2)}) collective-permute-start(bf16[96,1024]{1,0:T(8,128)(2,1)S(1)} %slice.180), channel_id=1, source_target_pairs={{0,4},{2,6},{4,0},{6,2},{1,5},{3,7},{5,1},{7,3},{8,12},{10,14},{12... | collective-permute-start | bytes 589832 | tf_op jit(solution)/shard_map/ppermute | solution.py:19
  227.4 7.6 %collective-permute-start.34 = (bf16[16,2944]{1,0:T(8,128)(2,1)S(1)}, bf16[16,2944]{1,0:T(8,128)(2,1)S(1)}, u32[]{:S(2)}, u32[]{:S(2)}) collective-permute-start(bf16[16,2944]{1,0:T(8,128)(2,1)S(1)} %pad_maximum_fusion.3.refs_0_), channel_id=1, source_target_pairs={{0,24},{8,16},{16,8},{24,0},{1,25},{9,17},{17,9},{25,1},{2,26},{10... | collective-permute-start | bytes 282632 | tf_op jit(solution)/shard_map/ppermute | solution.py:19
  (25 other events, 461.7 us)

commit v6 on v5

--- a/solution.py
+++ b/solution.py
@@ -228,7 +228,7 @@
 
 
 def column_chunks(count):
-    size = min(count, 2 * lanes)
+    size = min(count, 4 * lanes)
     return [slice(at, at + size) for at in range(0, count, size)]
 
 
@@ -542,7 +542,7 @@
         value = (kept[chunk].astype(f32) + came.astype(f32)).astype(bf16)
         return value.reshape(groups, -1, share_width)
 
-    first = own(0, after(others[0], *pieces))
+    first = own(0, others[0])
 
     pieces[0] = after(pieces[0], first)
     slot_grad = pl.pallas_call(
@@ -553,9 +553,8 @@
     )(*pieces, token_logits, combine, tag_labels[None, :])
     slot_grad = swap([slot_grad[:, j * lanes : (j + 1) * lanes] for j in range(experts)], "expert", steps)
     second = own(1, after(others[1], *slot_grad))
-    slot_grad[0] = after(slot_grad[0], second)
     slot_grad = gather(jnp.concatenate(slot_grad, axis=1), "dp")
-    came = [change(first), change(after(second, *slot_grad[1:]))]
+    came = [change(after(first, *pieces)), change(after(second, *slot_grad[1:]))]
 
     sums = [jnp.sum(came[0].astype(f32), axis=0).astype(bf16)]
     slot_grad[0] = after(slot_grad[0], sums[0])

time: 237 us -> 235 us (level)
  waiting for transfers between devices: 88.4 us -> 85.4 us
    ppermute x35, waiting for transfers between devices: 70.1 us -> 66.1 us  [send(): lax.ppermute(value, axis, [(i, i ^ step) for i in range(lax.axis_size(axi...]
  transfers between devices with their start and end apart: 38 -> 38, of which waited for: 21 -> 17; matrix products, arithmetic and copies ran while one was open for 10% -> 10% of each run, Pallas kernels for 22% -> 22%
where the time goes in v6:
time: 235 us; the launch traced here: 234 us
  waiting for transfers between devices  85.4 us (36%)
  Pallas kernels  63.4 us (27%)
  starting transfers between devices  58.6 us (25%)
  other arithmetic  11.8 us (5%)
  local copies, waits for them, and re-layouts  8.7 us (4%)
  matrix products  4.53 us (2%)
    ppermute x35, waiting for transfers between devices, send(): lax.ppermute(value, axis, [(i, i ^ step) for i in range(lax.axis_size(axi...  66.1 us
    ppermute x35, starting transfers between devices, send(): lax.ppermute(value, axis, [(i, i ^ step) for i in range(lax.axis_size(axi...  44.2 us
    pallas_call x1, Pallas kernels, forward(): pl.pallas_call(functools.partial(forward_kernel, experts, block_rows // r...  21.7 us
    pallas_call x2, Pallas kernels, down(): pl.pallas_call(functools.partial(down_kernel, first, len(nears), capacity...  19.3 us
    all_to_all x1, waiting for transfers between devices, local(): lax.all_to_all(after(parts, *plane_parts), 'dp', split_axis=0, concat_axi...  15.4 us
    all_to_all x2, starting transfers between devices, change(): return lax.all_to_all(part, 'dp', split_axis=0, concat_axis=0, tiled=True)  8.88 us
    pallas_call x1, Pallas kernels, pack(): pl.pallas_call(pack_kernel, out_shape=jax.ShapeDtypeStruct((groups, part...  8.71 us
    convert_element_type x2, other arithmetic, own(): value = (kept[chunk].astype(f32) + came.astype(f32)).astype(bf16)  7.05 us
  transfers between devices with their start and end apart: 38, of which 17 were waited for; matrix products, arithmetic and copies ran while one was open for 10% of the time, Pallas kernels for 22%

profile of v6, /device:TPU:0, one launch (start us, length us, event | category | flops | bytes accessed | tf_op | source)
XLA Modules:
  0.0 233.6 jit_solution(11982926960411925419)
XLA Ops:
  1.8 4.0 %collective-permute-start.2 = (bf16[136,1024]{1,0:T(8,128)(2,1)S(1)}, bf16[136,1024]{1,0:T(8,128)(2,1)S(1)}, u32[]{:S(2)}, u32[]{:S(2)}) collective-permute-start(bf16[136,1024]{1,0:T(8,128)(2,1)S(1)} %get-tuple-element.68), channel_id=1, source_target_pairs={{0,24},{8,16},{16,8},{24,0},{1,25},{9,17},{17,9},{25,1},{2,26},{10... | collective-permute-start | bytes 835592 | tf_op jit(solution)/shard_map/ppermute | solution.py:19
  7.7 8.7 %pack.1 = bf16[4,7,528,256]{3,2,1,0:T(8,128)(2,1)} custom-call(s32[3]{0:T(128)S(1)} %pad_add_fusion.place, bf16[512,3584]{1,0:T(8,128)(2,1)} %bitcast.63, bf16[512,3584]{1,0:T(8,128)(2,1)} %bitcast.64, bf16[3584,512]{1,0:T(8,128)(2,1)} %bitcast.60, bf16[2048,32]{1,0:T(8,128)(2,1)S(1)} %copy.17.tag_part), custom_call_target="tpu_custom_call" | custom-call | tf_op jit(solution)/shard_map/pack/pallas_call | solution.py:333
  18.7 5.5 %all-to-all-start = ((bf16[4,7,528,256]{3,2,1,0:T(8,128)(2,1)}), bf16[4,7,528,256]{3,2,1,0:T(8,128)(2,1)}, u32[]{:S(2)}, u32[]{:S(2)}) async-start(bf16[4,7,528,256]{3,2,1,0:T(8,128)(2,1)} %pack.1), calls=%async_computation | async-start | bytes 15138816 | tf_op jit(solution)/shard_map/all_to_all | solution.py:502
  24.2 3.9 %dynamic-slice_bitcast_fusion = (bf16[896,512]{1,0:T(8,128)(2,1)}, bf16[896,512]{1,0:T(8,128)(2,1)}, bf16[896,512]{1,0:T(8,128)(2,1)}, bf16[896,512]{1,0:T(8,128)(2,1)}) fusion(bf16[1,3584,512]{2,1,0:T(8,128)(2,1)} %param.17, s32[]{:T(128)S(6)} %select_n.56, s32[]{:T(128)S(6)} %select_n.54, s32[]{:T(128)S(6)} %select_n.53, s32[]{:T(128)S(6)} %select_n.55), kind=kLoop, calls=%fused_computation.17 | loop fusion | bytes 7340048 | tf_op jit(solution)/shard_map/dynamic_slice | solution.py:500
  34.6 34.4 %collective-permute-done.3.refs_1_ = bf16[384,1024]{1,0:T(8,128)(2,1)} collective-permute-done((bf16[384,1024]{1,0:T(8,128)(2,1)S(1)}, bf16[384,1024]{1,0:T(8,128)(2,1)}, u32[]{:S(2)}, u32[]{:S(2)}) %collective-permute-start.3) | collective-permute-done | bytes 786464 | tf_op jit(solution)/shard_map/ppermute | solution.py:19
  69.5 15.4 %collective-permute-done.5.refs_3_ = bf16[384,1024]{1,0:T(8,128)(2,1)} collective-permute-done((bf16[384,1024]{1,0:T(8,128)(2,1)S(1)}, bf16[384,1024]{1,0:T(8,128)(2,1)}, u32[]{:S(2)}, u32[]{:S(2)}) %collective-permute-start.5) | collective-permute-done | bytes 786464 | tf_op jit(solution)/shard_map/ppermute | solution.py:19
  87.5 5.0 %low_rank.1.refs_8_.refs_14_ = bf16[1536,16]{1,0:T(8,128)(2,1)S(1)} custom-call(s32[3]{0:T(128)S(1)} %pad_add_fusion.place, bf16[384,1024]{1,0:T(8,128)(2,1)S(1)} %bitcast.55, bf16[384,1024]{1,0:T(8,128)(2,1)} %collective-permute-done.3.refs_1_, bf16[384,1024]{1,0:T(8,128)(2,1)} %collective-permute-done.4.refs_2_, ...), custom_call_target="tpu_custom_call" | custom-call | tf_op jit(solution)/shard_map/low_rank/pallas_call | solution.py:99
  92.6 15.4 %all-to-all-done.refs_10_ = bf16[4,7,528,256]{3,2,1,0:T(8,128)(2,1)} async-done(((bf16[4,7,528,256]{3,2,1,0:T(8,128)(2,1)}), bf16[4,7,528,256]{3,2,1,0:T(8,128)(2,1)}, u32[]{:S(2)}, u32[]{:S(2)}) %all-to-all-start) | async-done | bytes 7569440 | tf_op jit(solution)/shard_map/all_to_all | solution.py:502
  112.2 21.7 %gate_up.1 = (bf16[1536,896]{1,0:T(8,128)(2,1)}, bf16[1536,896]{1,0:T(8,128)(2,1)}, bf16[32,2048]{1,0:T(8,128)(2,1)S(1)}, bf16[32,896]{1,0:T(8,128)(2,1)S(1)}) custom-call(s32[3]{0:T(128)S(1)} %pad_add_fusion.place, bf16[384,1024]{1,0:T(8,128)(2,1)S(1)} %bitcast.56, bf16[384,1024]{1,0:T(8,128)(2,1)} %collective-permute-done.3.refs_1_, ...), custom_call_target="tpu_custom_call" | custom-call | tf_op jit(solution)/shard_map/gate_up/pallas_call | solution.py:185
  136.0 3.8 %collective-permute-start.14 = (bf16[32,512]{1,0:T(8,128)(2,1)}, bf16[32,512]{1,0:T(8,128)(2,1)S(1)}, u32[]{:S(2)}, u32[]{:S(2)}) collective-permute-start(bf16[32,512]{1,0:T(8,128)(2,1)} %get-tuple-element.73), channel_id=1, source_target_pairs={{0,6},{2,4},{4,2},{6,0},{1,7},{3,5},{5,3},{7,1},{8,14},{10,12},{12... | collective-permute-start | bytes 98312 | tf_op jit(solution)/shard_map/ppermute | solution.py:19
  140.4 9.0 %down_near.1 = (bf16[4,2,96,1024]{3,2,1,0:T(8,128)(2,1)}, bf16[4,2,96,1024]{3,2,1,0:T(8,128)(2,1)}) custom-call(s32[3]{0:T(128)} %copy-done.3, bf16[1536,896]{1,0:T(8,128)(2,1)} %get-tuple-element.40.hidden, bf16[896,512]{1,0:T(8,128)(2,1)} %get-tuple-element.36.refs_0_, bf16[896,512]{1,0:T(8,128)(2,1)} %collective-permute-done.10.refs_1_), custom_call_target="tpu_custom_call" | custom-call | tf_op jit(solution)/shard_map/down_near/pallas_call | solution.py:293
  150.1 10.3 %down_far.1 = (bf16[4,2,96,1024]{3,2,1,0:T(8,128)(2,1)}, bf16[4,2,96,1024]{3,2,1,0:T(8,128)(2,1)}, bf16[4,2,96,1024]{3,2,1,0:T(8,128)(2,1)}, bf16[4,2,96,1024]{3,2,1,0:T(8,128)(2,1)}) custom-call(s32[3]{0:T(128)} %copy-done.3, bf16[1536,896]{1,0:T(8,128)(2,1)} %get-tuple-element.40.hidden, bf16[896,512]{1,0:T(8,128)(2,1)} %collective-permute-done.15.refs_0_, ...), custom_call_target="tpu_custom_call" | custom-call | tf_op jit(solution)/shard_map/down_far/pallas_call | solution.py:293
  165.3 3.3 %add_convert_fusion.1 = bf16[4,2,96,1024]{3,2,1,0:T(8,128)(2,1)} fusion(bf16[4,2,96,1024]{3,2,1,0:T(8,128)(2,1)S(1)} %collective-permute-done.18, bf16[4,2,96,1024]{3,2,1,0:T(8,128)(2,1)} %get-tuple-element.46), kind=kLoop, calls=%fused_computation.3 | loop fusion | flops 3145728 | bytes 4718592 | tf_op jit(solution)/shard_map/convert_element_type | solution.py:542
  168.7 4.5 %all-to-all-start.2 = ((bf16[4,192,1024]{2,1,0:T(8,128)(2,1)}), bf16[4,192,1024]{2,1,0:T(8,128)(2,1)}, u32[]{:S(2)}, u32[]{:S(2)}) async-start(bf16[4,192,1024]{2,1,0:T(8,128)(2,1)} %bitcast.61), calls=%async_computation.2 | async-start | bytes 3145728 | tf_op jit(solution)/shard_map/all_to_all | solution.py:530
  173.9 4.1 %collective-permute-start.24 = (bf16[32,128]{1,0:T(8,128)(2,1)S(1)}, bf16[32,128]{1,0:T(8,128)(2,1)S(1)}, u32[]{:S(2)}, u32[]{:S(2)}) collective-permute-start(bf16[32,128]{1,0:T(8,128)(2,1)S(1)} %get-tuple-element.76), channel_id=1, source_target_pairs={{0,6},{2,4},{4,2},{6,0},{1,7},{3,5},{5,3},{7,1},{8,14},{10,12},{12... | collective-permute-start | bytes 24584 | tf_op jit(solution)/shard_map/ppermute | solution.py:19
  187.2 3.8 %add_convert_fusion = bf16[4,2,96,1024]{3,2,1,0:T(8,128)(2,1)} fusion(bf16[4,2,96,1024]{3,2,1,0:T(8,128)(2,1)} %collective-permute-done.17, bf16[4,2,96,1024]{3,2,1,0:T(8,128)(2,1)} %get-tuple-element.44), kind=kLoop, calls=%fused_computation.2 | loop fusion | flops 3145728 | bytes 4718592 | tf_op jit(solution)/shard_map/convert_element_type | solution.py:542
  191.0 2.8 %collective-permute-done.27.refs_11_ = bf16[32,512]{1,0:T(8,128)(2,1)S(1)} collective-permute-done((bf16[32,512]{1,0:T(8,128)(2,1)S(1)}, bf16[32,512]{1,0:T(8,128)(2,1)S(1)}, u32[]{:S(2)}, u32[]{:S(2)}) %collective-permute-start.27) | collective-permute-done | bytes 32800 | tf_op jit(solution)/shard_map/ppermute | solution.py:19
  193.8 4.4 %all-to-all-start.1 = ((bf16[4,192,1024]{2,1,0:T(8,128)(2,1)}), bf16[4,192,1024]{2,1,0:T(8,128)(2,1)}, u32[]{:S(2)}, u32[]{:S(2)}) async-start(bf16[4,192,1024]{2,1,0:T(8,128)(2,1)} %bitcast.62), calls=%async_computation.1 | async-start | bytes 3145728 | tf_op jit(solution)/shard_map/all_to_all | solution.py:530
  199.9 6.9 %adapter_grad.1 = (f32[16,896]{1,0:T(8,128)S(1)}, f32[16,2048]{1,0:T(8,128)S(1)}) custom-call(s32[3]{0:T(128)S(1)} %copy-done.4, bf16[384,1024]{1,0:T(8,128)(2,1)S(1)} %bitcast.57, bf16[384,1024]{1,0:T(8,128)(2,1)} %collective-permute-done.3.refs_1_, bf16[384,1024]{1,0:T(8,128)(2,1)} %collective-permute-done.4.refs_2_, ...), custom_call_target="tpu_custom_call" | custom-call | tf_op jit(solution)/shard_map/adapter_grad/pallas_call | solution.py:391
  206.8 2.8 %collective-permute-start.29 = (bf16[96,1024]{1,0:T(8,128)(2,1)S(1)}, bf16[96,1024]{1,0:T(8,128)(2,1)S(1)}, u32[]{:S(2)}, u32[]{:S(2)}) collective-permute-start(bf16[96,1024]{1,0:T(8,128)(2,1)S(1)} %get-tuple-element.65), channel_id=1, source_target_pairs={{0,2},{2,0},{4,6},{6,4},{1,3},{3,1},{5,7},{7,5},{8,10},{10,8},{12,... | collective-permute-start | bytes 589832 | tf_op jit(solution)/shard_map/ppermute | solution.py:19
  209.6 3.5 %collective-permute-start.30 = (bf16[96,1024]{1,0:T(8,128)(2,1)S(1)}, bf16[96,1024]{1,0:T(8,128)(2,1)S(1)}, u32[]{:S(2)}, u32[]{:S(2)}) collective-permute-start(bf16[96,1024]{1,0:T(8,128)(2,1)S(1)} %get-tuple-element.66), channel_id=1, source_target_pairs={{0,6},{2,4},{4,2},{6,0},{1,7},{3,5},{5,3},{7,1},{8,14},{10,12},{12... | collective-permute-start | bytes 589832 | tf_op jit(solution)/shard_map/ppermute | solution.py:19
  213.1 3.9 %all-to-all-done.1 = bf16[4,192,1024]{2,1,0:T(8,128)(2,1)} async-done(((bf16[4,192,1024]{2,1,0:T(8,128)(2,1)}), bf16[4,192,1024]{2,1,0:T(8,128)(2,1)}, u32[]{:S(2)}, u32[]{:S(2)}) %all-to-all-start.1) | async-done | bytes 1572896 | tf_op jit(solution)/shard_map/all_to_all | solution.py:530
  218.8 3.9 %collective-permute-start.28 = (bf16[96,1024]{1,0:T(8,128)(2,1)S(1)}, bf16[96,1024]{1,0:T(8,128)(2,1)S(1)}, u32[]{:S(2)}, u32[]{:S(2)}) collective-permute-start(bf16[96,1024]{1,0:T(8,128)(2,1)S(1)} %slice.180), channel_id=1, source_target_pairs={{0,4},{2,6},{4,0},{6,2},{1,5},{3,7},{5,1},{7,3},{8,12},{10,14},{12... | collective-permute-start | bytes 589832 | tf_op jit(solution)/shard_map/ppermute | solution.py:19
  228.1 2.9 %collective-permute-done.28 = bf16[96,1024]{1,0:T(8,128)(2,1)S(1)} collective-permute-done((bf16[96,1024]{1,0:T(8,128)(2,1)S(1)}, bf16[96,1024]{1,0:T(8,128)(2,1)S(1)}, u32[]{:S(2)}, u32[]{:S(2)}) %collective-permute-start.28) | collective-permute-done | bytes 196640 | tf_op jit(solution)/shard_map/ppermute | solution.py:19
  (132 shorter events, 48.7 us)
Async XLA Ops:
  1.8 14.6 %collective-permute-start.2 = (bf16[136,1024]{1,0:T(8,128)(2,1)S(1)}, bf16[136,1024]{1,0:T(8,128)(2,1)S(1)}, u32[]{:S(2)}, u32[]{:S(2)}) collective-permute-start(bf16[136,1024]{1,0:T(8,128)(2,1)S(1)} %get-tuple-element.68), channel_id=1, source_target_pairs={{0,24},{8,16},{16,8},{24,0},{1,25},{9,17},{17,9},{25,1},{2,26},{10... | collective-permute-start | bytes 835592 | tf_op jit(solution)/shard_map/ppermute | solution.py:19
  5.7 12.6 %collective-permute-start.1 = (bf16[136,1024]{1,0:T(8,128)(2,1)S(1)}, bf16[136,1024]{1,0:T(8,128)(2,1)S(1)}, u32[]{:S(2)}, u32[]{:S(2)}) collective-permute-start(bf16[136,1024]{1,0:T(8,128)(2,1)S(1)} %get-tuple-element.68), channel_id=1, source_target_pairs={{0,16},{8,24},{16,0},{24,8},{1,17},{9,25},{17,1},{25,9},{2,18},{10... | collective-permute-start | bytes 835592 | tf_op jit(solution)/shard_map/ppermute | solution.py:19
  6.2 12.4 %collective-permute-start = (bf16[136,1024]{1,0:T(8,128)(2,1)S(1)}, bf16[136,1024]{1,0:T(8,128)(2,1)S(1)}, u32[]{:S(2)}, u32[]{:S(2)}) collective-permute-start(bf16[136,1024]{1,0:T(8,128)(2,1)S(1)} %get-tuple-element.68), channel_id=1, source_target_pairs={{0,8},{8,0},{16,24},{24,16},{1,9},{9,1},{17,25},{25,17},{2,10},{10... | collective-permute-start | bytes 835592 | tf_op jit(solution)/shard_map/ppermute | solution.py:19
  18.7 89.3 %all-to-all-start = ((bf16[4,7,528,256]{3,2,1,0:T(8,128)(2,1)}), bf16[4,7,528,256]{3,2,1,0:T(8,128)(2,1)}, u32[]{:S(2)}, u32[]{:S(2)}) async-start(bf16[4,7,528,256]{3,2,1,0:T(8,128)(2,1)} %pack.1), calls=%async_computation | async-start | bytes 15138816 | tf_op jit(solution)/shard_map/all_to_all | solution.py:502
  29.6 39.4 %collective-permute-start.3 = (bf16[384,1024]{1,0:T(8,128)(2,1)S(1)}, bf16[384,1024]{1,0:T(8,128)(2,1)}, u32[]{:S(2)}, u32[]{:S(2)}) collective-permute-start(bf16[384,1024]{1,0:T(8,128)(2,1)S(1)} %bitcast.73), channel_id=1, source_target_pairs={{0,4},{2,6},{4,0},{6,2},{1,5},{3,7},{5,1},{7,3},{8,12},{10,14},{12... | collective-permute-start | bytes 2359304 | tf_op jit(solution)/shard_map/ppermute | solution.py:19
  32.2 36.7 %collective-permute-start.4 = (bf16[384,1024]{1,0:T(8,128)(2,1)S(1)}, bf16[384,1024]{1,0:T(8,128)(2,1)}, u32[]{:S(2)}, u32[]{:S(2)}) collective-permute-start(bf16[384,1024]{1,0:T(8,128)(2,1)S(1)} %bitcast.72), channel_id=1, source_target_pairs={{0,2},{2,0},{4,6},{6,4},{1,3},{3,1},{5,7},{7,5},{8,10},{10,8},{12,... | collective-permute-start | bytes 2359304 | tf_op jit(solution)/shard_map/ppermute | solution.py:19
  33.8 51.1 %collective-permute-start.5 = (bf16[384,1024]{1,0:T(8,128)(2,1)S(1)}, bf16[384,1024]{1,0:T(8,128)(2,1)}, u32[]{:S(2)}, u32[]{:S(2)}) collective-permute-start(bf16[384,1024]{1,0:T(8,128)(2,1)S(1)} %bitcast.71), channel_id=1, source_target_pairs={{0,6},{2,4},{4,2},{6,0},{1,7},{3,5},{5,3},{7,1},{8,14},{10,12},{12... | collective-permute-start | bytes 2359304 | tf_op jit(solution)/shard_map/ppermute | solution.py:19
  34.5 52.1 %collective-permute-start.6 = (bf16[384,1024]{1,0:T(8,128)(2,1)S(1)}, bf16[384,1024]{1,0:T(8,128)(2,1)S(1)}, u32[]{:S(2)}, u32[]{:S(2)}) collective-permute-start(bf16[384,1024]{1,0:T(8,128)(2,1)S(1)} %bitcast.54), channel_id=1, source_target_pairs={{0,1},{1,0},{2,3},{3,2},{4,5},{5,4},{6,7},{7,6},{8,9},{9,8},{10,11... | collective-permute-start | bytes 2359304 | tf_op jit(solution)/shard_map/ppermute | solution.py:19
  69.0 17.6 %collective-permute-start.7 = (bf16[384,1024]{1,0:T(8,128)(2,1)}, bf16[384,1024]{1,0:T(8,128)(2,1)}, u32[]{:S(2)}, u32[]{:S(2)}) collective-permute-start(bf16[384,1024]{1,0:T(8,128)(2,1)} %collective-permute-done.3.refs_1_), channel_id=1, source_target_pairs={{0,1},{1,0},{2,3},{3,2},{4,5},{5,4},{6,7},{7,6},{8,9},{9,8},{10,11... | collective-permute-start | bytes 2359304 | tf_op jit(solution)/shard_map/ppermute | solution.py:19
  69.0 17.6 %collective-permute-start.8 = (bf16[384,1024]{1,0:T(8,128)(2,1)}, bf16[384,1024]{1,0:T(8,128)(2,1)}, u32[]{:S(2)}, u32[]{:S(2)}) collective-permute-start(bf16[384,1024]{1,0:T(8,128)(2,1)} %collective-permute-done.4.refs_2_), channel_id=1, source_target_pairs={{0,1},{1,0},{2,3},{3,2},{4,5},{5,4},{6,7},{7,6},{8,9},{9,8},{10,11... | collective-permute-start | bytes 2359304 | tf_op jit(solution)/shard_map/ppermute | solution.py:19
  107.9 31.8 %collective-permute-start.10 = (bf16[896,512]{1,0:T(8,128)(2,1)}, bf16[896,512]{1,0:T(8,128)(2,1)}, u32[]{:S(2)}, u32[]{:S(2)}) collective-permute-start(bf16[896,512]{1,0:T(8,128)(2,1)} %get-tuple-element.37), channel_id=1, source_target_pairs={{0,8},{8,0},{16,24},{24,16},{1,9},{9,1},{17,25},{25,17},{2,10},{10... | collective-permute-start | bytes 2752520 | tf_op jit(solution)/shard_map/ppermute | solution.py:19
  109.3 40.8 %collective-permute-start.15 = (bf16[896,512]{1,0:T(8,128)(2,1)}, bf16[896,512]{1,0:T(8,128)(2,1)}, u32[]{:S(2)}, u32[]{:S(2)}) collective-permute-start(bf16[896,512]{1,0:T(8,128)(2,1)} %get-tuple-element.41), channel_id=1, source_target_pairs={{0,16},{8,24},{16,0},{24,8},{1,17},{9,25},{17,1},{25,9},{2,18},{10... | collective-permute-start | bytes 2752520 | tf_op jit(solution)/shard_map/ppermute | solution.py:19
  109.9 40.2 %collective-permute-start.16 = (bf16[896,512]{1,0:T(8,128)(2,1)}, bf16[896,512]{1,0:T(8,128)(2,1)}, u32[]{:S(2)}, u32[]{:S(2)}) collective-permute-start(bf16[896,512]{1,0:T(8,128)(2,1)} %get-tuple-element.42), channel_id=1, source_target_pairs={{0,24},{8,16},{16,8},{24,0},{1,25},{9,17},{17,9},{25,1},{2,26},{10... | collective-permute-start | bytes 2752520 | tf_op jit(solution)/shard_map/ppermute | solution.py:19
  136.0 13.4 %collective-permute-start.14 = (bf16[32,512]{1,0:T(8,128)(2,1)}, bf16[32,512]{1,0:T(8,128)(2,1)S(1)}, u32[]{:S(2)}, u32[]{:S(2)}) collective-permute-start(bf16[32,512]{1,0:T(8,128)(2,1)} %get-tuple-element.73), channel_id=1, source_target_pairs={{0,6},{2,4},{4,2},{6,0},{1,7},{3,5},{5,3},{7,1},{8,14},{10,12},{12... | collective-permute-start | bytes 98312 | tf_op jit(solution)/shard_map/ppermute | solution.py:19
  139.8 9.6 %collective-permute-start.13 = (bf16[32,512]{1,0:T(8,128)(2,1)}, bf16[32,512]{1,0:T(8,128)(2,1)S(1)}, u32[]{:S(2)}, u32[]{:S(2)}) collective-permute-start(bf16[32,512]{1,0:T(8,128)(2,1)} %get-tuple-element.74), channel_id=1, source_target_pairs={{0,2},{2,0},{4,6},{6,4},{1,3},{3,1},{5,7},{7,5},{8,10},{10,8},{12,... | collective-permute-start | bytes 98312 | tf_op jit(solution)/shard_map/ppermute | solution.py:19
  139.8 9.6 %collective-permute-start.12 = (bf16[32,512]{1,0:T(8,128)(2,1)}, bf16[32,512]{1,0:T(8,128)(2,1)}, u32[]{:S(2)}, u32[]{:S(2)}) collective-permute-start(bf16[32,512]{1,0:T(8,128)(2,1)} %get-tuple-element.75), channel_id=1, source_target_pairs={{0,4},{2,6},{4,0},{6,2},{1,5},{3,7},{5,1},{7,3},{8,12},{10,14},{12... | collective-permute-start | bytes 98312 | tf_op jit(solution)/shard_map/ppermute | solution.py:19
  161.3 25.9 %collective-permute-start.17 = (bf16[4,2,96,1024]{3,2,1,0:T(8,128)(2,1)}, bf16[4,2,96,1024]{3,2,1,0:T(8,128)(2,1)}, u32[]{:S(2)}, u32[]{:S(2)}) collective-permute-start(bf16[4,2,96,1024]{3,2,1,0:T(8,128)(2,1)} %get-tuple-element.45), channel_id=1, source_target_pairs={{0,1},{1,0},{2,3},{3,2},{4,5},{5,4},{6,7},{7,6},{8,9},{9,8},{10,11... | collective-permute-start | bytes 4718600 | tf_op jit(solution)/shard_map/ppermute | solution.py:19
  168.7 25.1 %all-to-all-start.2 = ((bf16[4,192,1024]{2,1,0:T(8,128)(2,1)}), bf16[4,192,1024]{2,1,0:T(8,128)(2,1)}, u32[]{:S(2)}, u32[]{:S(2)}) async-start(bf16[4,192,1024]{2,1,0:T(8,128)(2,1)} %bitcast.61), calls=%async_computation.2 | async-start | bytes 3145728 | tf_op jit(solution)/shard_map/all_to_all | solution.py:530
  183.7 10.1 %collective-permute-start.27 = (bf16[32,512]{1,0:T(8,128)(2,1)S(1)}, bf16[32,512]{1,0:T(8,128)(2,1)S(1)}, u32[]{:S(2)}, u32[]{:S(2)}) collective-permute-start(bf16[32,512]{1,0:T(8,128)(2,1)S(1)} %pad_maximum_fusion.8.refs_8_), channel_id=1, source_target_pairs={{0,24},{8,16},{16,8},{24,0},{1,25},{9,17},{17,9},{25,1},{2,26},{10... | collective-permute-start | bytes 98312 | tf_op jit(solution)/shard_map/ppermute | solution.py:19
  193.8 23.3 %all-to-all-start.1 = ((bf16[4,192,1024]{2,1,0:T(8,128)(2,1)}), bf16[4,192,1024]{2,1,0:T(8,128)(2,1)}, u32[]{:S(2)}, u32[]{:S(2)}) async-start(bf16[4,192,1024]{2,1,0:T(8,128)(2,1)} %bitcast.62), calls=%async_computation.1 | async-start | bytes 3145728 | tf_op jit(solution)/shard_map/all_to_all | solution.py:530
  206.8 16.3 %collective-permute-start.29 = (bf16[96,1024]{1,0:T(8,128)(2,1)S(1)}, bf16[96,1024]{1,0:T(8,128)(2,1)S(1)}, u32[]{:S(2)}, u32[]{:S(2)}) collective-permute-start(bf16[96,1024]{1,0:T(8,128)(2,1)S(1)} %get-tuple-element.65), channel_id=1, source_target_pairs={{0,2},{2,0},{4,6},{6,4},{1,3},{3,1},{5,7},{7,5},{8,10},{10,8},{12,... | collective-permute-start | bytes 589832 | tf_op jit(solution)/shard_map/ppermute | solution.py:19
  209.6 13.5 %collective-permute-start.30 = (bf16[96,1024]{1,0:T(8,128)(2,1)S(1)}, bf16[96,1024]{1,0:T(8,128)(2,1)S(1)}, u32[]{:S(2)}, u32[]{:S(2)}) collective-permute-start(bf16[96,1024]{1,0:T(8,128)(2,1)S(1)} %get-tuple-element.66), channel_id=1, source_target_pairs={{0,6},{2,4},{4,2},{6,0},{1,7},{3,5},{5,3},{7,1},{8,14},{10,12},{12... | collective-permute-start | bytes 589832 | tf_op jit(solution)/shard_map/ppermute | solution.py:19
  218.8 12.2 %collective-permute-start.28 = (bf16[96,1024]{1,0:T(8,128)(2,1)S(1)}, bf16[96,1024]{1,0:T(8,128)(2,1)S(1)}, u32[]{:S(2)}, u32[]{:S(2)}) collective-permute-start(bf16[96,1024]{1,0:T(8,128)(2,1)S(1)} %slice.180), channel_id=1, source_target_pairs={{0,4},{2,6},{4,0},{6,2},{1,5},{3,7},{5,1},{7,3},{8,12},{10,14},{12... | collective-permute-start | bytes 589832 | tf_op jit(solution)/shard_map/ppermute | solution.py:19
  224.5 7.6 %collective-permute-start.34 = (bf16[16,2944]{1,0:T(8,128)(2,1)S(1)}, bf16[16,2944]{1,0:T(8,128)(2,1)S(1)}, u32[]{:S(2)}, u32[]{:S(2)}) collective-permute-start(bf16[16,2944]{1,0:T(8,128)(2,1)S(1)} %pad_maximum_fusion.3.refs_0_), channel_id=1, source_target_pairs={{0,24},{8,16},{16,8},{24,0},{1,25},{9,17},{17,9},{25,1},{2,26},{10... | collective-permute-start | bytes 282632 | tf_op jit(solution)/shard_map/ppermute | solution.py:19
  (25 other events, 472.3 us)

commit v7 on v6

--- a/solution.py
+++ b/solution.py
@@ -11,7 +11,7 @@
 f32 = jnp.float32
 bf16 = jnp.bfloat16
 highest = lax.Precision.HIGHEST
-vmem_limit = 52 * 1024 * 1024
+vmem_limit = 46 * 1024 * 1024
 lanes = 128
 
 
@@ -573,9 +573,11 @@
     in_local = after(in_local, *returned[chunks[0][0] :])
     in_local = in_local + send(in_local.astype(bf16), "tensor", 1).astype(f32)
     both = gather(jnp.concatenate([in_local, out_local], axis=1).astype(bf16), "dp")
-    sums.append(jnp.sum(came[1].astype(f32), axis=0).astype(bf16))
-    give_back(1)
-    both[0] = after(both[0], sums[-1])
+    for j in range(chunks[1][1] - 1, -1, -1):
+        value = came[1][:, j * capacity : (j + 1) * capacity]
+        value = jnp.sum(value.astype(f32), axis=0).astype(bf16)
+        returned[j] = send(value, "expert", steps[j]) if steps[j] else after(value, both[0])
+        both[0] = after(both[0], value) if steps[j] else both[0]
     in_total, out_total = finish(place, both, model_width)
     layer_out = token_half.astype(f32)
     for j in range(experts):

time: 235 us -> 234 us (level)
  local copies, waits for them, and re-layouts: 8.7 us -> 13.4 us
  waiting for transfers between devices: 85.4 us -> 81.6 us
    unnamed x23 -> x29, local copies, waits for them, and re-layouts: 1.44 us -> 5.52 us
  transfers between devices with their start and end apart: 38 -> 38, of which waited for: 17 -> 15; matrix products, arithmetic and copies ran while one was open for 10% -> 11% of each run, Pallas kernels for 22% -> 22%
where the time goes in v7:
time: 234 us; the launch traced here: 233 us
  waiting for transfers between devices  81.6 us (35%)
  Pallas kernels  61.8 us (26%)
  starting transfers between devices  58.9 us (25%)
  local copies, waits for them, and re-layouts  13.4 us (6%)
  other arithmetic  11.9 us (5%)
  matrix products  4.53 us (2%)
    ppermute x35, waiting for transfers between devices, send(): lax.ppermute(value, axis, [(i, i ^ step) for i in range(lax.axis_size(axi...  65.1 us
    ppermute x35, starting transfers between devices, send(): lax.ppermute(value, axis, [(i, i ^ step) for i in range(lax.axis_size(axi...  44.5 us
    pallas_call x1, Pallas kernels, forward(): pl.pallas_call(functools.partial(forward_kernel, experts, block_rows // r...  21.7 us
    pallas_call x2, Pallas kernels, down(): pl.pallas_call(functools.partial(down_kernel, first, len(nears), capacity...  19.2 us
    all_to_all x1, waiting for transfers between devices, local(): lax.all_to_all(after(parts, *plane_parts), 'dp', split_axis=0, concat_axi...  13.2 us
    all_to_all x2, starting transfers between devices, change(): return lax.all_to_all(part, 'dp', split_axis=0, concat_axis=0, tiled=True)  8.89 us
    pallas_call x1, Pallas kernels, pack(): pl.pallas_call(pack_kernel, out_shape=jax.ShapeDtypeStruct((groups, part...  7.12 us
    convert_element_type x2, other arithmetic, own(): value = (kept[chunk].astype(f32) + came.astype(f32)).astype(bf16)  7.06 us
  transfers between devices with their start and end apart: 38, of which 15 were waited for; matrix products, arithmetic and copies ran while one was open for 11% of the time, Pallas kernels for 22%

profile of v7, /device:TPU:0, one launch (start us, length us, event | category | flops | bytes accessed | tf_op | source)
XLA Modules:
  0.0 233.3 jit_solution(10305693162599812635)
XLA Ops:
  1.8 4.0 %collective-permute-start.2 = (bf16[136,1024]{1,0:T(8,128)(2,1)S(1)}, bf16[136,1024]{1,0:T(8,128)(2,1)S(1)}, u32[]{:S(2)}, u32[]{:S(2)}) collective-permute-start(bf16[136,1024]{1,0:T(8,128)(2,1)S(1)} %get-tuple-element.72), channel_id=1, source_target_pairs={{0,24},{8,16},{16,8},{24,0},{1,25},{9,17},{17,9},{25,1},{2,26},{10... | collective-permute-start | bytes 835592 | tf_op jit(solution)/shard_map/ppermute | solution.py:19
  11.8 7.1 %pack.1 = bf16[4,7,528,256]{3,2,1,0:T(8,128)(2,1)} custom-call(s32[3]{0:T(128)S(1)} %pad_add_fusion.place, bf16[512,3584]{1,0:T(8,128)(2,1)S(1)} %bitcast.59, bf16[512,3584]{1,0:T(8,128)(2,1)S(1)} %bitcast.60, bf16[3584,512]{1,0:T(8,128)(2,1)} %bitcast.63, bf16[2048,32]{1,0:T(8,128)(2,1)S(1)} %copy.17.tag_part), custom_call_target="tpu_custom_call" | custom-call | tf_op jit(solution)/shard_map/pack/pallas_call | solution.py:333
  18.9 5.5 %all-to-all-start = ((bf16[4,7,528,256]{3,2,1,0:T(8,128)(2,1)}), bf16[4,7,528,256]{3,2,1,0:T(8,128)(2,1)}, u32[]{:S(2)}, u32[]{:S(2)}) async-start(bf16[4,7,528,256]{3,2,1,0:T(8,128)(2,1)} %pack.1), calls=%async_computation | async-start | bytes 15138816 | tf_op jit(solution)/shard_map/all_to_all | solution.py:502
  24.5 3.9 %dynamic-slice_bitcast_fusion = (bf16[896,512]{1,0:T(8,128)(2,1)}, bf16[896,512]{1,0:T(8,128)(2,1)}, bf16[896,512]{1,0:T(8,128)(2,1)}, bf16[896,512]{1,0:T(8,128)(2,1)}) fusion(bf16[1,3584,512]{2,1,0:T(8,128)(2,1)} %param.17, s32[]{:T(128)S(6)} %select_n.56, s32[]{:T(128)S(6)} %select_n.54, s32[]{:T(128)S(6)} %select_n.53, s32[]{:T(128)S(6)} %select_n.55), kind=kLoop, calls=%fused_computation.17 | loop fusion | bytes 7340048 | tf_op jit(solution)/shard_map/dynamic_slice | solution.py:500
  29.8 3.1 %collective-permute-start.3 = (bf16[384,1024]{1,0:T(8,128)(2,1)S(1)}, bf16[384,1024]{1,0:T(8,128)(2,1)S(1)}, u32[]{:S(2)}, u32[]{:S(2)}) collective-permute-start(bf16[384,1024]{1,0:T(8,128)(2,1)S(1)} %bitcast.74), channel_id=1, source_target_pairs={{0,4},{2,6},{4,0},{6,2},{1,5},{3,7},{5,1},{7,3},{8,12},{10,14},{12... | collective-permute-start | bytes 2359304 | tf_op jit(solution)/shard_map/ppermute | solution.py:19
  35.0 49.8 %collective-permute-done.3.refs_1_ = bf16[384,1024]{1,0:T(8,128)(2,1)S(1)} collective-permute-done((bf16[384,1024]{1,0:T(8,128)(2,1)S(1)}, bf16[384,1024]{1,0:T(8,128)(2,1)S(1)}, u32[]{:S(2)}, u32[]{:S(2)}) %collective-permute-start.3) | collective-permute-done | bytes 786464 | tf_op jit(solution)/shard_map/ppermute | solution.py:19
  89.7 5.0 %low_rank.1.refs_8_.refs_14_ = bf16[1536,16]{1,0:T(8,128)(2,1)S(1)} custom-call(s32[3]{0:T(128)S(1)} %pad_add_fusion.place, bf16[384,1024]{1,0:T(8,128)(2,1)S(1)} %bitcast.56, bf16[384,1024]{1,0:T(8,128)(2,1)S(1)} %collective-permute-done.3.refs_1_, bf16[384,1024]{1,0:T(8,128)(2,1)} %collective-permute-done.4.refs_2_, ...), custom_call_target="tpu_custom_call" | custom-call | tf_op jit(solution)/shard_map/low_rank/pallas_call | solution.py:99
  94.7 13.2 %all-to-all-done.refs_10_ = bf16[4,7,528,256]{3,2,1,0:T(8,128)(2,1)} async-done(((bf16[4,7,528,256]{3,2,1,0:T(8,128)(2,1)}), bf16[4,7,528,256]{3,2,1,0:T(8,128)(2,1)}, u32[]{:S(2)}, u32[]{:S(2)}) %all-to-all-start) | async-done | bytes 7569440 | tf_op jit(solution)/shard_map/all_to_all | solution.py:502
  112.2 21.7 %gate_up.1 = (bf16[1536,896]{1,0:T(8,128)(2,1)}, bf16[1536,896]{1,0:T(8,128)(2,1)}, bf16[32,2048]{1,0:T(8,128)(2,1)S(1)}, bf16[32,896]{1,0:T(8,128)(2,1)S(1)}) custom-call(s32[3]{0:T(128)S(1)} %pad_add_fusion.place, bf16[384,1024]{1,0:T(8,128)(2,1)S(1)} %bitcast.57, bf16[384,1024]{1,0:T(8,128)(2,1)S(1)} %collective-permute-done.3.refs_1_, ...), custom_call_target="tpu_custom_call" | custom-call | tf_op jit(solution)/shard_map/gate_up/pallas_call | solution.py:185
  135.9 3.8 %collective-permute-start.14 = (bf16[32,512]{1,0:T(8,128)(2,1)}, bf16[32,512]{1,0:T(8,128)(2,1)S(1)}, u32[]{:S(2)}, u32[]{:S(2)}) collective-permute-start(bf16[32,512]{1,0:T(8,128)(2,1)} %get-tuple-element.77), channel_id=1, source_target_pairs={{0,6},{2,4},{4,2},{6,0},{1,7},{3,5},{5,3},{7,1},{8,14},{10,12},{12... | collective-permute-start | bytes 98312 | tf_op jit(solution)/shard_map/ppermute | solution.py:19
  140.3 8.9 %down_near.1 = (bf16[4,2,96,1024]{3,2,1,0:T(8,128)(2,1)}, bf16[4,2,96,1024]{3,2,1,0:T(8,128)(2,1)}) custom-call(s32[3]{0:T(128)} %copy-done.7, bf16[1536,896]{1,0:T(8,128)(2,1)} %get-tuple-element.41.hidden, bf16[896,512]{1,0:T(8,128)(2,1)} %get-tuple-element.37.refs_0_, bf16[896,512]{1,0:T(8,128)(2,1)} %collective-permute-done.10.refs_1_), custom_call_target="tpu_custom_call" | custom-call | tf_op jit(solution)/shard_map/down_near/pallas_call | solution.py:293
  149.8 10.3 %down_far.1 = (bf16[4,2,96,1024]{3,2,1,0:T(8,128)(2,1)}, bf16[4,2,96,1024]{3,2,1,0:T(8,128)(2,1)}, bf16[4,2,96,1024]{3,2,1,0:T(8,128)(2,1)}, bf16[4,2,96,1024]{3,2,1,0:T(8,128)(2,1)}) custom-call(s32[3]{0:T(128)} %copy-done.7, bf16[1536,896]{1,0:T(8,128)(2,1)} %get-tuple-element.41.hidden, bf16[896,512]{1,0:T(8,128)(2,1)} %collective-permute-done.15.refs_0_, ...), custom_call_target="tpu_custom_call" | custom-call | tf_op jit(solution)/shard_map/down_far/pallas_call | solution.py:293
  165.0 3.3 %add_convert_fusion.1 = bf16[4,2,96,1024]{3,2,1,0:T(8,128)(2,1)} fusion(bf16[4,2,96,1024]{3,2,1,0:T(8,128)(2,1)S(1)} %collective-permute-done.18, bf16[4,2,96,1024]{3,2,1,0:T(8,128)(2,1)} %get-tuple-element.47), kind=kLoop, calls=%fused_computation.3 | loop fusion | flops 3145728 | bytes 4718592 | tf_op jit(solution)/shard_map/convert_element_type | solution.py:542
  168.4 4.5 %all-to-all-start.2 = ((bf16[4,192,1024]{2,1,0:T(8,128)(2,1)}), bf16[4,192,1024]{2,1,0:T(8,128)(2,1)}, u32[]{:S(2)}, u32[]{:S(2)}) async-start(bf16[4,192,1024]{2,1,0:T(8,128)(2,1)} %bitcast.64), calls=%async_computation.2 | async-start | bytes 3145728 | tf_op jit(solution)/shard_map/all_to_all | solution.py:530
  173.6 3.7 %collective-permute-start.24 = (bf16[32,128]{1,0:T(8,128)(2,1)S(1)}, bf16[32,128]{1,0:T(8,128)(2,1)S(1)}, u32[]{:S(2)}, u32[]{:S(2)}) collective-permute-start(bf16[32,128]{1,0:T(8,128)(2,1)S(1)} %get-tuple-element.80), channel_id=1, source_target_pairs={{0,6},{2,4},{4,2},{6,0},{1,7},{3,5},{5,3},{7,1},{8,14},{10,12},{12... | collective-permute-start | bytes 24584 | tf_op jit(solution)/shard_map/ppermute | solution.py:19
  187.0 3.8 %add_convert_fusion = bf16[4,2,96,1024]{3,2,1,0:T(8,128)(2,1)} fusion(bf16[4,2,96,1024]{3,2,1,0:T(8,128)(2,1)} %collective-permute-done.17, bf16[4,2,96,1024]{3,2,1,0:T(8,128)(2,1)} %get-tuple-element.45), kind=kLoop, calls=%fused_computation.2 | loop fusion | flops 3145728 | bytes 4718592 | tf_op jit(solution)/shard_map/convert_element_type | solution.py:542
  190.8 2.7 %collective-permute-done.27.refs_11_ = bf16[32,512]{1,0:T(8,128)(2,1)S(1)} collective-permute-done((bf16[32,512]{1,0:T(8,128)(2,1)S(1)}, bf16[32,512]{1,0:T(8,128)(2,1)S(1)}, u32[]{:S(2)}, u32[]{:S(2)}) %collective-permute-start.27) | collective-permute-done | bytes 32800 | tf_op jit(solution)/shard_map/ppermute | solution.py:19
  193.5 4.4 %all-to-all-start.1 = ((bf16[4,192,1024]{2,1,0:T(8,128)(2,1)}), bf16[4,192,1024]{2,1,0:T(8,128)(2,1)}, u32[]{:S(2)}, u32[]{:S(2)}) async-start(bf16[4,192,1024]{2,1,0:T(8,128)(2,1)} %bitcast.65), calls=%async_computation.1 | async-start | bytes 3145728 | tf_op jit(solution)/shard_map/all_to_all | solution.py:530
  200.4 2.8 %collective-permute-start.28 = (bf16[96,1024]{1,0:T(8,128)(2,1)}, bf16[96,1024]{1,0:T(8,128)(2,1)S(1)}, u32[]{:S(2)}, u32[]{:S(2)}) collective-permute-start(bf16[96,1024]{1,0:T(8,128)(2,1)} %get-tuple-element.69), channel_id=1, source_target_pairs={{0,2},{2,0},{4,6},{6,4},{1,3},{3,1},{5,7},{7,5},{8,10},{10,8},{12,... | collective-permute-start | bytes 589832 | tf_op jit(solution)/shard_map/ppermute | solution.py:19
  203.2 3.5 %collective-permute-start.29 = (bf16[96,1024]{1,0:T(8,128)(2,1)S(1)}, bf16[96,1024]{1,0:T(8,128)(2,1)S(1)}, u32[]{:S(2)}, u32[]{:S(2)}) collective-permute-start(bf16[96,1024]{1,0:T(8,128)(2,1)S(1)} %get-tuple-element.70), channel_id=1, source_target_pairs={{0,6},{2,4},{4,2},{6,0},{1,7},{3,5},{5,3},{7,1},{8,14},{10,12},{12... | collective-permute-start | bytes 589832 | tf_op jit(solution)/shard_map/ppermute | solution.py:19
  206.7 6.8 %adapter_grad.1 = (f32[16,896]{1,0:T(8,128)S(1)}, f32[16,2048]{1,0:T(8,128)S(1)}) custom-call(s32[3]{0:T(128)S(1)} %copy-done.8, bf16[384,1024]{1,0:T(8,128)(2,1)S(1)} %bitcast.58, bf16[384,1024]{1,0:T(8,128)(2,1)S(1)} %copy-done.3, bf16[384,1024]{1,0:T(8,128)(2,1)} %collective-permute-done.4.refs_2_, bf16[384,1024]{1,0:T(8,128)(2,1)} %collective-permute-done.5.refs_3_, ...), custom_call_target="tpu_custom_call" | custom-call | tf_op jit(solution)/shard_map/adapter_grad/pallas_call | solution.py:391
  213.5 3.2 %all-to-all-done.1 = bf16[4,192,1024]{2,1,0:T(8,128)(2,1)} async-done(((bf16[4,192,1024]{2,1,0:T(8,128)(2,1)}), bf16[4,192,1024]{2,1,0:T(8,128)(2,1)}, u32[]{:S(2)}, u32[]{:S(2)}) %all-to-all-start.1) | async-done | bytes 1572896 | tf_op jit(solution)/shard_map/all_to_all | solution.py:530
  218.6 3.9 %collective-permute-start.31 = (bf16[96,1024]{1,0:T(8,128)(2,1)S(1)}, bf16[96,1024]{1,0:T(8,128)(2,1)S(1)}, u32[]{:S(2)}, u32[]{:S(2)}) collective-permute-start(bf16[96,1024]{1,0:T(8,128)(2,1)S(1)} %get-tuple-element.63), channel_id=1, source_target_pairs={{0,4},{2,6},{4,0},{6,2},{1,5},{3,7},{5,1},{7,3},{8,12},{10,14},{12... | collective-permute-start | bytes 589832 | tf_op jit(solution)/shard_map/ppermute | solution.py:19
  227.9 2.9 %collective-permute-done.31 = bf16[96,1024]{1,0:T(8,128)(2,1)S(1)} collective-permute-done((bf16[96,1024]{1,0:T(8,128)(2,1)S(1)}, bf16[96,1024]{1,0:T(8,128)(2,1)S(1)}, u32[]{:S(2)}, u32[]{:S(2)}) %collective-permute-start.31) | collective-permute-done | bytes 196640 | tf_op jit(solution)/shard_map/ppermute | solution.py:19
  (137 shorter events, 50.3 us)
Async XLA Ops:
  1.8 17.1 %collective-permute-start.2 = (bf16[136,1024]{1,0:T(8,128)(2,1)S(1)}, bf16[136,1024]{1,0:T(8,128)(2,1)S(1)}, u32[]{:S(2)}, u32[]{:S(2)}) collective-permute-start(bf16[136,1024]{1,0:T(8,128)(2,1)S(1)} %get-tuple-element.72), channel_id=1, source_target_pairs={{0,24},{8,16},{16,8},{24,0},{1,25},{9,17},{17,9},{25,1},{2,26},{10... | collective-permute-start | bytes 835592 | tf_op jit(solution)/shard_map/ppermute | solution.py:19
  5.7 13.2 %collective-permute-start.1 = (bf16[136,1024]{1,0:T(8,128)(2,1)S(1)}, bf16[136,1024]{1,0:T(8,128)(2,1)S(1)}, u32[]{:S(2)}, u32[]{:S(2)}) collective-permute-start(bf16[136,1024]{1,0:T(8,128)(2,1)S(1)} %get-tuple-element.72), channel_id=1, source_target_pairs={{0,16},{8,24},{16,0},{24,8},{1,17},{9,25},{17,1},{25,9},{2,18},{10... | collective-permute-start | bytes 835592 | tf_op jit(solution)/shard_map/ppermute | solution.py:19
  6.2 12.7 %collective-permute-start = (bf16[136,1024]{1,0:T(8,128)(2,1)S(1)}, bf16[136,1024]{1,0:T(8,128)(2,1)S(1)}, u32[]{:S(2)}, u32[]{:S(2)}) collective-permute-start(bf16[136,1024]{1,0:T(8,128)(2,1)S(1)} %get-tuple-element.72), channel_id=1, source_target_pairs={{0,8},{8,0},{16,24},{24,16},{1,9},{9,1},{17,25},{25,17},{2,10},{10... | collective-permute-start | bytes 835592 | tf_op jit(solution)/shard_map/ppermute | solution.py:19
  18.9 89.0 %all-to-all-start = ((bf16[4,7,528,256]{3,2,1,0:T(8,128)(2,1)}), bf16[4,7,528,256]{3,2,1,0:T(8,128)(2,1)}, u32[]{:S(2)}, u32[]{:S(2)}) async-start(bf16[4,7,528,256]{3,2,1,0:T(8,128)(2,1)} %pack.1), calls=%async_computation | async-start | bytes 15138816 | tf_op jit(solution)/shard_map/all_to_all | solution.py:502
  29.8 55.0 %collective-permute-start.3 = (bf16[384,1024]{1,0:T(8,128)(2,1)S(1)}, bf16[384,1024]{1,0:T(8,128)(2,1)S(1)}, u32[]{:S(2)}, u32[]{:S(2)}) collective-permute-start(bf16[384,1024]{1,0:T(8,128)(2,1)S(1)} %bitcast.74), channel_id=1, source_target_pairs={{0,4},{2,6},{4,0},{6,2},{1,5},{3,7},{5,1},{7,3},{8,12},{10,14},{12... | collective-permute-start | bytes 2359304 | tf_op jit(solution)/shard_map/ppermute | solution.py:19
  32.9 51.9 %collective-permute-start.4 = (bf16[384,1024]{1,0:T(8,128)(2,1)S(1)}, bf16[384,1024]{1,0:T(8,128)(2,1)}, u32[]{:S(2)}, u32[]{:S(2)}) collective-permute-start(bf16[384,1024]{1,0:T(8,128)(2,1)S(1)} %bitcast.73), channel_id=1, source_target_pairs={{0,2},{2,0},{4,6},{6,4},{1,3},{3,1},{5,7},{7,5},{8,10},{10,8},{12,... | collective-permute-start | bytes 2359304 | tf_op jit(solution)/shard_map/ppermute | solution.py:19
  34.5 50.9 %collective-permute-start.5 = (bf16[384,1024]{1,0:T(8,128)(2,1)S(1)}, bf16[384,1024]{1,0:T(8,128)(2,1)}, u32[]{:S(2)}, u32[]{:S(2)}) collective-permute-start(bf16[384,1024]{1,0:T(8,128)(2,1)S(1)} %bitcast.72), channel_id=1, source_target_pairs={{0,6},{2,4},{4,2},{6,0},{1,7},{3,5},{5,3},{7,1},{8,14},{10,12},{12... | collective-permute-start | bytes 2359304 | tf_op jit(solution)/shard_map/ppermute | solution.py:19
  34.9 52.1 %collective-permute-start.6 = (bf16[384,1024]{1,0:T(8,128)(2,1)S(1)}, bf16[384,1024]{1,0:T(8,128)(2,1)}, u32[]{:S(2)}, u32[]{:S(2)}) collective-permute-start(bf16[384,1024]{1,0:T(8,128)(2,1)S(1)} %bitcast.55), channel_id=1, source_target_pairs={{0,1},{1,0},{2,3},{3,2},{4,5},{5,4},{6,7},{7,6},{8,9},{9,8},{10,11... | collective-permute-start | bytes 2359304 | tf_op jit(solution)/shard_map/ppermute | solution.py:19
  107.9 31.8 %collective-permute-start.10 = (bf16[896,512]{1,0:T(8,128)(2,1)}, bf16[896,512]{1,0:T(8,128)(2,1)}, u32[]{:S(2)}, u32[]{:S(2)}) collective-permute-start(bf16[896,512]{1,0:T(8,128)(2,1)} %get-tuple-element.38), channel_id=1, source_target_pairs={{0,8},{8,0},{16,24},{24,16},{1,9},{9,1},{17,25},{25,17},{2,10},{10... | collective-permute-start | bytes 2752520 | tf_op jit(solution)/shard_map/ppermute | solution.py:19
  109.3 40.5 %collective-permute-start.15 = (bf16[896,512]{1,0:T(8,128)(2,1)}, bf16[896,512]{1,0:T(8,128)(2,1)}, u32[]{:S(2)}, u32[]{:S(2)}) collective-permute-start(bf16[896,512]{1,0:T(8,128)(2,1)} %get-tuple-element.42), channel_id=1, source_target_pairs={{0,16},{8,24},{16,0},{24,8},{1,17},{9,25},{17,1},{25,9},{2,18},{10... | collective-permute-start | bytes 2752520 | tf_op jit(solution)/shard_map/ppermute | solution.py:19
  109.9 39.9 %collective-permute-start.16 = (bf16[896,512]{1,0:T(8,128)(2,1)}, bf16[896,512]{1,0:T(8,128)(2,1)}, u32[]{:S(2)}, u32[]{:S(2)}) collective-permute-start(bf16[896,512]{1,0:T(8,128)(2,1)} %get-tuple-element.43), channel_id=1, source_target_pairs={{0,24},{8,16},{16,8},{24,0},{1,25},{9,17},{17,9},{25,1},{2,26},{10... | collective-permute-start | bytes 2752520 | tf_op jit(solution)/shard_map/ppermute | solution.py:19
  135.9 13.3 %collective-permute-start.14 = (bf16[32,512]{1,0:T(8,128)(2,1)}, bf16[32,512]{1,0:T(8,128)(2,1)S(1)}, u32[]{:S(2)}, u32[]{:S(2)}) collective-permute-start(bf16[32,512]{1,0:T(8,128)(2,1)} %get-tuple-element.77), channel_id=1, source_target_pairs={{0,6},{2,4},{4,2},{6,0},{1,7},{3,5},{5,3},{7,1},{8,14},{10,12},{12... | collective-permute-start | bytes 98312 | tf_op jit(solution)/shard_map/ppermute | solution.py:19
  139.7 9.6 %collective-permute-start.13 = (bf16[32,512]{1,0:T(8,128)(2,1)}, bf16[32,512]{1,0:T(8,128)(2,1)S(1)}, u32[]{:S(2)}, u32[]{:S(2)}) collective-permute-start(bf16[32,512]{1,0:T(8,128)(2,1)} %get-tuple-element.78), channel_id=1, source_target_pairs={{0,2},{2,0},{4,6},{6,4},{1,3},{3,1},{5,7},{7,5},{8,10},{10,8},{12,... | collective-permute-start | bytes 98312 | tf_op jit(solution)/shard_map/ppermute | solution.py:19
  139.7 9.6 %collective-permute-start.12 = (bf16[32,512]{1,0:T(8,128)(2,1)}, bf16[32,512]{1,0:T(8,128)(2,1)}, u32[]{:S(2)}, u32[]{:S(2)}) collective-permute-start(bf16[32,512]{1,0:T(8,128)(2,1)} %get-tuple-element.79), channel_id=1, source_target_pairs={{0,4},{2,6},{4,0},{6,2},{1,5},{3,7},{5,1},{7,3},{8,12},{10,14},{12... | collective-permute-start | bytes 98312 | tf_op jit(solution)/shard_map/ppermute | solution.py:19
  161.0 26.0 %collective-permute-start.17 = (bf16[4,2,96,1024]{3,2,1,0:T(8,128)(2,1)}, bf16[4,2,96,1024]{3,2,1,0:T(8,128)(2,1)}, u32[]{:S(2)}, u32[]{:S(2)}) collective-permute-start(bf16[4,2,96,1024]{3,2,1,0:T(8,128)(2,1)} %get-tuple-element.46), channel_id=1, source_target_pairs={{0,1},{1,0},{2,3},{3,2},{4,5},{5,4},{6,7},{7,6},{8,9},{9,8},{10,11... | collective-permute-start | bytes 4718600 | tf_op jit(solution)/shard_map/ppermute | solution.py:19
  161.5 6.8 %collective-permute-start.19 = (bf16[32,512]{1,0:T(8,128)(2,1)S(1)}, bf16[32,512]{1,0:T(8,128)(2,1)S(1)}, u32[]{:S(2)}, u32[]{:S(2)}) collective-permute-start(bf16[32,512]{1,0:T(8,128)(2,1)S(1)} %pad_maximum_fusion.5), channel_id=1, source_target_pairs={{0,8},{8,0},{16,24},{24,16},{1,9},{9,1},{17,25},{25,17},{2,10},{10... | collective-permute-start | bytes 98312 | tf_op jit(solution)/shard_map/ppermute | solution.py:19
  168.4 25.1 %all-to-all-start.2 = ((bf16[4,192,1024]{2,1,0:T(8,128)(2,1)}), bf16[4,192,1024]{2,1,0:T(8,128)(2,1)}, u32[]{:S(2)}, u32[]{:S(2)}) async-start(bf16[4,192,1024]{2,1,0:T(8,128)(2,1)} %bitcast.64), calls=%async_computation.2 | async-start | bytes 3145728 | tf_op jit(solution)/shard_map/all_to_all | solution.py:530
  183.5 10.0 %collective-permute-start.27 = (bf16[32,512]{1,0:T(8,128)(2,1)S(1)}, bf16[32,512]{1,0:T(8,128)(2,1)S(1)}, u32[]{:S(2)}, u32[]{:S(2)}) collective-permute-start(bf16[32,512]{1,0:T(8,128)(2,1)S(1)} %pad_maximum_fusion.8.refs_8_), channel_id=1, source_target_pairs={{0,24},{8,16},{16,8},{24,0},{1,25},{9,17},{17,9},{25,1},{2,26},{10... | collective-permute-start | bytes 98312 | tf_op jit(solution)/shard_map/ppermute | solution.py:19
  186.2 7.3 %collective-permute-start.26 = (bf16[32,512]{1,0:T(8,128)(2,1)S(1)}, bf16[32,512]{1,0:T(8,128)(2,1)S(1)}, u32[]{:S(2)}, u32[]{:S(2)}) collective-permute-start(bf16[32,512]{1,0:T(8,128)(2,1)S(1)} %pad_maximum_fusion.8.refs_8_), channel_id=1, source_target_pairs={{0,16},{8,24},{16,0},{24,8},{1,17},{9,25},{17,1},{25,9},{2,18},{10... | collective-permute-start | bytes 98312 | tf_op jit(solution)/shard_map/ppermute | solution.py:19
  193.5 23.3 %all-to-all-start.1 = ((bf16[4,192,1024]{2,1,0:T(8,128)(2,1)}), bf16[4,192,1024]{2,1,0:T(8,128)(2,1)}, u32[]{:S(2)}, u32[]{:S(2)}) async-start(bf16[4,192,1024]{2,1,0:T(8,128)(2,1)} %bitcast.65), calls=%async_computation.1 | async-start | bytes 3145728 | tf_op jit(solution)/shard_map/all_to_all | solution.py:530
  200.4 22.1 %collective-permute-start.28 = (bf16[96,1024]{1,0:T(8,128)(2,1)}, bf16[96,1024]{1,0:T(8,128)(2,1)S(1)}, u32[]{:S(2)}, u32[]{:S(2)}) collective-permute-start(bf16[96,1024]{1,0:T(8,128)(2,1)} %get-tuple-element.69), channel_id=1, source_target_pairs={{0,2},{2,0},{4,6},{6,4},{1,3},{3,1},{5,7},{7,5},{8,10},{10,8},{12,... | collective-permute-start | bytes 589832 | tf_op jit(solution)/shard_map/ppermute | solution.py:19
  203.2 19.3 %collective-permute-start.29 = (bf16[96,1024]{1,0:T(8,128)(2,1)S(1)}, bf16[96,1024]{1,0:T(8,128)(2,1)S(1)}, u32[]{:S(2)}, u32[]{:S(2)}) collective-permute-start(bf16[96,1024]{1,0:T(8,128)(2,1)S(1)} %get-tuple-element.70), channel_id=1, source_target_pairs={{0,6},{2,4},{4,2},{6,0},{1,7},{3,5},{5,3},{7,1},{8,14},{10,12},{12... | collective-permute-start | bytes 589832 | tf_op jit(solution)/shard_map/ppermute | solution.py:19
  218.6 12.2 %collective-permute-start.31 = (bf16[96,1024]{1,0:T(8,128)(2,1)S(1)}, bf16[96,1024]{1,0:T(8,128)(2,1)S(1)}, u32[]{:S(2)}, u32[]{:S(2)}) collective-permute-start(bf16[96,1024]{1,0:T(8,128)(2,1)S(1)} %get-tuple-element.63), channel_id=1, source_target_pairs={{0,4},{2,6},{4,0},{6,2},{1,5},{3,7},{5,1},{7,3},{8,12},{10,14},{12... | collective-permute-start | bytes 589832 | tf_op jit(solution)/shard_map/ppermute | solution.py:19
  223.9 8.1 %collective-permute-start.34 = (bf16[16,2944]{1,0:T(8,128)(2,1)S(1)}, bf16[16,2944]{1,0:T(8,128)(2,1)S(1)}, u32[]{:S(2)}, u32[]{:S(2)}) collective-permute-start(bf16[16,2944]{1,0:T(8,128)(2,1)S(1)} %pad_maximum_fusion.3.refs_0_), channel_id=1, source_target_pairs={{0,24},{8,16},{16,8},{24,0},{1,25},{9,17},{17,9},{25,1},{2,26},{10... | collective-permute-start | bytes 282632 | tf_op jit(solution)/shard_map/ppermute | solution.py:19
  (28 other events, 511.7 us)
